TPU v7x, 32 devices: a whole 2x2x4 slice. The times are simulated.
32 devices in a mesh: seq: 16 (over z, y, x), span: 2 (over core).
Axes of the slice: x: 2, y: 2, z: 4, core: 2. Of those that a mesh axis runs over, the one named last changes fastest.
Arguments:
- tokens: bfloat16 [32, 1024, 768], P('seq', 'span'), may hold values from -6 to 6
- conditions: bfloat16 [32, 128], P('seq'), may hold values from -6 to 6
- assignment: int32 [32], P('seq'), may hold values from 0 to 31, each once
- lengths: int32 [32], P('seq'), may hold values from 128 to 1024, as said below
- norm1_gain: bfloat16 [768], replicated, may hold values from 0.099609375 to 1.8984375
- ada_weight: bfloat16 [128, 4608], replicated, may hold values from -0.5 to 0.5
- ada_bias: bfloat16 [4608], replicated, may hold values from -4 to 4
- qkv_weight: bfloat16 [768, 2304], replicated, may hold values from -0.21875 to 0.21875
- out_weight: bfloat16 [768, 768], replicated, may hold values from -3.5 to 3.5
- norm2_gain: bfloat16 [768], replicated, may hold values from 0.099609375 to 1.8984375
- up_weight: bfloat16 [768, 3072], replicated, may hold values from -0.21875 to 0.21875
- up_bias: bfloat16 [3072], replicated, may hold values from -6 to 6
- down_weight: bfloat16 [3072, 768], replicated, may hold values from -0.21875 to 0.21875
- down_bias: bfloat16 [768], replicated, may hold values from -4 to 4
- cotangent: bfloat16 [32, 1024, 768], P('seq', 'span'), may hold values from -6 to 6
Outputs:
- out: bfloat16 [32, 1024, 768], P('seq', 'span')
- grad_input: float32 [32, 1024, 768], P('seq', 'span')
- grad_conditions: float32 [32, 128], P('seq')
- grad_norm1_gain: float32 [768], replicated
- grad_ada_weight: float32 [128, 4608], P('seq', 'span')
- grad_ada_bias: float32 [4608], replicated
- grad_qkv_weight: float32 [768, 2304], P('seq', 'span')
- grad_out_weight: float32 [768, 768], P('seq', 'span')
- grad_norm2_gain: float32 [768], replicated
- grad_up_weight: float32 [768, 3072], P('seq', 'span')
- grad_up_bias: float32 [3072], replicated
- grad_down_weight: float32 [3072, 768], P('seq', 'span')
- grad_down_bias: float32 [768], replicated
Inputs may be any that keep to these rules, and one draw needn't show every extreme that they name: `assignment`: each sequence is held by exactly one slot. `lengths`: among the 2 slots of each index of seq, one has length 1024 and another has length 128.
All inputs are finite; a program needn't handle non-finite values.
Results may differ from a plain program's by a relative error of at most 0.01.
The roundings to bfloat16 on the way count: a program that leaves them out, or rounds other values in their place, can miss the bound.
Values may be sent and summed in bfloat16 or wider, within the bound.
A program may use at most 320 MiB of HBM per device.

v0:
```python
from functools import partial

import jax
import jax.numpy as jnp
from jax import lax
from jax.sharding import PartitionSpec as P

H = 12
HD = 64


EPSILON = 1e-05
MASKED = -1e30
HIGHEST = lax.Precision.HIGHEST


def matmul(left_in, right_in):
    return jnp.dot(left_in, right_in, preferred_element_type=jnp.float32)


def matmul_tn(left_in, right_in):
    return lax.dot_general(
        left_in, right_in, (((0,), (0,)), ((), ())), preferred_element_type=jnp.float32
    )


def matmul_nt(left_in, right_in):
    return lax.dot_general(
        left_in, right_in, (((1,), (1,)), ((), ())), preferred_element_type=jnp.float32
    )


def layer_norm(inputs, gain_vec):
    center = inputs - jnp.mean(inputs, axis=-1, keepdims=True)
    spread = jnp.mean(center * center, axis=-1, keepdims=True)
    return center * lax.rsqrt(spread + EPSILON) * gain_vec


def modulate(inputs, gain_vec, shift_vec, scale_vec):
    return layer_norm(inputs, gain_vec) * (1.0 + scale_vec) + shift_vec


def rotary_tables(positions, half_size):
    frequency = jnp.power(10000.0, -jnp.arange(half_size, dtype=jnp.float32) / half_size)
    angles = positions.astype(jnp.float32)[:, None] * frequency[None, :]
    return (jnp.cos(angles), jnp.sin(angles))


def rotate(inputs, cos_table, sine_table):
    half_size = inputs.shape[-1] // 2
    former = inputs[..., :half_size]
    latter = inputs[..., half_size:]
    cos_part = cos_table[:, None, :]
    sine_part = sine_table[:, None, :]
    return jnp.concatenate(
        [former * cos_part - latter * sine_part, latter * cos_part + former * sine_part], axis=-1
    )


def rotate_pair(first_in, second_in, cos_table, sine_table):
    return (rotate(first_in, cos_table, sine_table), rotate(second_in, cos_table, sine_table))


def gelu_tanh(upper_in):
    return jax.nn.gelu(upper_in, approximate=True)


def slot_scores(queries, keys_all, length):
    head_count, head_size = (queries.shape[1], queries.shape[2])
    keys_heads = keys_all.reshape(keys_all.shape[0], head_count, head_size)
    scores = jnp.einsum(
        "qhd,khd->hqk", queries, keys_heads, preferred_element_type=jnp.float32
    ) * head_size ** (-0.5)
    visible = jnp.arange(keys_all.shape[0], dtype=jnp.int32) < length
    return (jnp.where(visible[None, None, :], scores, MASKED), keys_heads)


def attend_slot(pieces):
    queries, keys_all, values_all, length = pieces
    scores, keys_heads = slot_scores(queries, keys_all, length)
    values_heads = values_all.reshape(keys_heads.shape)
    maximum = jnp.max(scores, axis=-1, keepdims=True)
    exponent = jnp.exp(scores - maximum)
    totals = jnp.sum(exponent, axis=-1, keepdims=True)
    soft_weights = (exponent / totals).astype(jnp.bfloat16)
    attended = jnp.einsum(
        "hqk,khd->qhd", soft_weights, values_heads, preferred_element_type=jnp.float32
    )
    return (attended, maximum, totals)


def attend_back(pieces):
    queries, keys_all, values_all, length, maximum, totals, d_attended = pieces
    scores, keys_heads = slot_scores(queries, keys_all, length)
    values_heads = values_all.reshape(keys_heads.shape)
    soft_full = jnp.exp(scores - maximum) / totals
    d_soft = jnp.einsum(
        "qhd,khd->hqk", d_attended, values_heads, preferred_element_type=jnp.float32
    )
    inner_sum = jnp.sum(soft_full * d_soft, axis=-1, keepdims=True)
    scaling = queries.shape[2] ** (-0.5)
    d_scores = (soft_full * (d_soft - inner_sum) * scaling).astype(jnp.bfloat16)
    d_queries = jnp.einsum("hqk,khd->qhd", d_scores, keys_heads, preferred_element_type=jnp.float32)
    d_keys = jnp.einsum("hqk,qhd->khd", d_scores, queries, preferred_element_type=jnp.float32)
    d_values = jnp.einsum(
        "hqk,qhd->khd",
        soft_full.astype(jnp.bfloat16),
        d_attended,
        preferred_element_type=jnp.float32,
    )
    return (d_queries, d_keys.reshape(keys_all.shape), d_values.reshape(keys_all.shape))


def weight_tiles(gradient, seq_count, span_count):
    rows_all, cols_all = gradient.shape
    shaped = gradient.reshape(seq_count, rows_all // seq_count, span_count, cols_all // span_count)
    return shaped.transpose(0, 2, 1, 3).reshape(
        seq_count * span_count, rows_all // seq_count, cols_all // span_count
    )


def shards(
    tokens,
    conditions,
    assignment,
    lengths,
    norm1_gain,
    ada_weight,
    ada_bias,
    qkv_weight,
    out_weight,
    norm2_gain,
    up_weight,
    up_bias,
    down_weight,
    down_bias,
    cotangent,
):
    slot_count, span_rows, model_width = tokens.shape
    head_count = H
    head_size = HD
    flat_rows = slot_count * span_rows
    seq_count = lax.axis_size("seq")
    span_count = lax.axis_size("span")
    cond_table = lax.all_gather(conditions, "seq", axis=0, tiled=True)
    picker = assignment[:, None] == jnp.arange(cond_table.shape[0], dtype=jnp.int32)[None, :]
    cond_rows = matmul(picker.astype(jnp.bfloat16), cond_table)
    silu_val, silu_pull = jax.vjp(jax.nn.silu, cond_rows)
    silu_low = silu_val.astype(jnp.bfloat16)
    modulation = matmul(silu_low, ada_weight) + ada_bias.astype(jnp.float32)
    shift_one, scale_one, gate_one, shift_two, scale_two, gate_two = jnp.split(
        modulation[:, None, :], 6, axis=2
    )
    tokens_f = tokens.astype(jnp.float32)
    hidden_one, pull_one = jax.vjp(
        modulate, tokens_f, norm1_gain.astype(jnp.float32), shift_one, scale_one
    )
    hidden_one = hidden_one.astype(jnp.bfloat16).reshape(flat_rows, model_width)
    qkv_all = matmul(hidden_one, qkv_weight).reshape(
        slot_count, span_rows, 3, head_count, head_size
    )
    positions = lax.axis_index("span") * span_rows + jnp.arange(span_rows, dtype=jnp.int32)
    cos_table, sine_table = rotary_tables(positions, head_size // 2)
    turned, pull_turn = jax.vjp(
        partial(rotate_pair, cos_table=cos_table, sine_table=sine_table),
        qkv_all[:, :, 0],
        qkv_all[:, :, 1],
    )
    queries = turned[0].astype(jnp.bfloat16)
    keys_low = turned[1].astype(jnp.bfloat16).reshape(slot_count, span_rows, model_width)
    values_low = qkv_all[:, :, 2].astype(jnp.bfloat16).reshape(slot_count, span_rows, model_width)
    keys_all, values_all = (
        lax.all_gather(keys_low, "span", axis=1, tiled=True),
        lax.all_gather(values_low, "span", axis=1, tiled=True),
    )
    attended, maximum, totals = lax.map(attend_slot, (queries, keys_all, values_all, lengths))
    attended_low = attended.astype(jnp.bfloat16).reshape(flat_rows, model_width)
    attention = matmul(attended_low, out_weight).reshape(slot_count, span_rows, model_width)
    middle = tokens_f + gate_one * attention
    hidden_two, pull_two = jax.vjp(
        modulate, middle, norm2_gain.astype(jnp.float32), shift_two, scale_two
    )
    hidden_two = hidden_two.astype(jnp.bfloat16).reshape(flat_rows, model_width)
    upper_in = matmul(hidden_two, up_weight) + up_bias.astype(jnp.float32)
    activation, pull_gelu = jax.vjp(gelu_tanh, upper_in)
    activation = activation.astype(jnp.bfloat16)
    lowered = (matmul(activation, down_weight) + down_bias.astype(jnp.float32)).reshape(
        slot_count, span_rows, model_width
    )
    result = (middle + gate_two * lowered).astype(jnp.bfloat16)
    d_out = cotangent.astype(jnp.float32)
    d_gate_two = jnp.sum(d_out * lowered, axis=1, keepdims=True)
    d_lowered = (gate_two * d_out).astype(jnp.bfloat16).reshape(flat_rows, model_width)
    grad_down_bias = jnp.sum(d_lowered.astype(jnp.float32), axis=0)
    grad_down = matmul_tn(activation, d_lowered)
    d_upper = pull_gelu(matmul_nt(d_lowered, down_weight))[0].astype(jnp.bfloat16)
    grad_up_bias = jnp.sum(d_upper.astype(jnp.float32), axis=0)
    grad_up = matmul_tn(hidden_two, d_upper)
    d_middle_norm, grad_gain_two, d_shift_two, d_scale_two = pull_two(
        matmul_nt(d_upper, up_weight).reshape(slot_count, span_rows, model_width)
    )
    d_middle = d_out + d_middle_norm
    d_gate_one = jnp.sum(d_middle * attention, axis=1, keepdims=True)
    d_attention = (gate_one * d_middle).astype(jnp.bfloat16).reshape(flat_rows, model_width)
    grad_out = matmul_tn(attended_low, d_attention)
    d_attended = (
        matmul_nt(d_attention, out_weight)
        .astype(jnp.bfloat16)
        .reshape(slot_count, span_rows, head_count, head_size)
    )
    keys_back, values_back = (keys_all, values_all)
    d_queries, d_keys_all, d_values_all = lax.map(
        attend_back, (queries, keys_back, values_back, lengths, maximum, totals, d_attended)
    )
    d_keys, d_values = (
        lax.psum_scatter(d_keys_all, "span", scatter_dimension=1, tiled=True),
        lax.psum_scatter(d_values_all, "span", scatter_dimension=1, tiled=True),
    )
    d_query_raw, d_key_raw = pull_turn(
        (d_queries, d_keys.reshape(slot_count, span_rows, head_count, head_size))
    )
    d_qkv = jnp.stack(
        [d_query_raw, d_key_raw, d_values.reshape(slot_count, span_rows, head_count, head_size)],
        axis=2,
    )
    d_qkv = d_qkv.astype(jnp.bfloat16).reshape(flat_rows, 3 * model_width)
    grad_qkv = matmul_tn(hidden_one, d_qkv)
    d_tokens_norm, grad_gain_one, d_shift_one, d_scale_one = pull_one(
        matmul_nt(d_qkv, qkv_weight).reshape(slot_count, span_rows, model_width)
    )
    grad_input = d_middle + d_tokens_norm
    d_modulation = jnp.concatenate(
        [d_shift_one, d_scale_one, d_gate_one, d_shift_two, d_scale_two, d_gate_two], axis=2
    )[:, 0, :]
    grad_ada_part = lax.dot_general(
        silu_low.astype(jnp.float32),
        d_modulation,
        (((0,), (0,)), ((), ())),
        precision=HIGHEST,
        preferred_element_type=jnp.float32,
    )
    grad_ada_bias = jnp.sum(d_modulation, axis=0)
    d_silu = lax.dot_general(
        d_modulation,
        ada_weight.astype(jnp.float32),
        (((1,), (1,)), ((), ())),
        precision=HIGHEST,
        preferred_element_type=jnp.float32,
    )
    d_cond = silu_pull(d_silu)[0]
    cond_part = lax.dot_general(
        picker.astype(jnp.float32),
        d_cond,
        (((0,), (0,)), ((), ())),
        precision=HIGHEST,
        preferred_element_type=jnp.float32,
    )
    block_qkv, block_out, block_ada, feed_up, feed_down = (
        lax.psum_scatter(
            weight_tiles(grad_qkv, seq_count, span_count),
            ("seq", "span"),
            scatter_dimension=0,
            tiled=True,
        ),
        lax.psum_scatter(
            weight_tiles(grad_out, seq_count, span_count),
            ("seq", "span"),
            scatter_dimension=0,
            tiled=True,
        ),
        lax.psum_scatter(
            weight_tiles(grad_ada_part, seq_count, span_count),
            ("seq", "span"),
            scatter_dimension=0,
            tiled=True,
        ),
        lax.psum_scatter(
            weight_tiles(grad_up, seq_count, span_count),
            ("seq", "span"),
            scatter_dimension=0,
            tiled=True,
        ),
        lax.psum_scatter(
            weight_tiles(grad_down, seq_count, span_count),
            ("seq", "span"),
            scatter_dimension=0,
            tiled=True,
        ),
    )
    gain_one_sum, gain_two_sum, up_bias_sum, down_bias_sum, ada_bias_sum, cond_sum = lax.psum(
        (grad_gain_one, grad_gain_two, grad_up_bias, grad_down_bias, grad_ada_bias, cond_part),
        ("seq", "span"),
    )
    grad_cond = lax.dynamic_slice_in_dim(
        cond_sum, lax.axis_index("seq") * slot_count, slot_count, 0
    )
    return (
        result,
        grad_input,
        grad_cond,
        gain_one_sum,
        block_ada[0],
        ada_bias_sum,
        block_qkv[0],
        block_out[0],
        gain_two_sum,
        feed_up[0],
        up_bias_sum,
        feed_down[0],
        down_bias_sum,
    )


def solution(mesh):
    in_specs = (
        P("seq", "span", None),
        P("seq", None),
        P("seq"),
        P("seq"),
        P(),
        P(),
        P(),
        P(),
        P(),
        P(),
        P(),
        P(),
        P(),
        P(),
        P("seq", "span", None),
    )
    out_specs = (
        P("seq", "span", None),
        P("seq", "span", None),
        P("seq", None),
        P(),
        P("seq", "span"),
        P(),
        P("seq", "span"),
        P("seq", "span"),
        P(),
        P("seq", "span"),
        P(),
        P("seq", "span"),
        P(),
    )
    return jax.shard_map(shards, mesh=mesh, in_specs=in_specs, out_specs=out_specs, check_vma=False)
```

profile of v0, /device:TPU:0, one launch (start us, length us, event | category | flops | bytes accessed | tf_op | source)
XLA Modules:
  0.0 1129.7 jit_solution(5912439835737681933)
XLA Ops:
  7.3 42.5 %all-gather = bf16[16,2,128]{2,1,0:T(2,128)(2,1)S(1)} all-gather(bf16[1,2,128]{2,1,0:T(2,128)(2,1)} %bitcast.382), channel_id=1, replica_groups=mesh['seq'=16,'span'=2] {'seq'}, dimensions={0}, use_global_device_ids=true | all-gather | bytes 8704 | tf_op jit(solution)/shard_map/all_gather | solution.py:145
  92.9 15.4 %all-gather.4.cloned.1.call-done = bf16[2,1024,768]{1,2,0:T(8,128)(2,1)} async-done(((bf16[2,512,768]{1,2,0:T(8,128)(2,1)}), bf16[2,1024,768]{1,2,0:T(8,128)(2,1)}) %all-gather.4.cloned.1.call-update) | async-done | bytes 3145744 | tf_op jit(solution)/shard_map/all_gather | solution.py:174
  108.3 73.4 %while.30 = (s32[]{:T(128)}, bf16[2,512,12,64]{1,3,2,0:T(8,128)(2,1)}, f32[2,12,512,1]{2,1,3,0:T(8,128)S(1)}, f32[2,12,512,1]{2,1,3,0:T(8,128)S(1)}, bf16[2,1024...) while((s32[]{:T(128)}, ...), condition=%wide.region_5.6_spmd.clone, body=%wide.region_2.5_spmd.sunk.clone | while | flops 1686098944 | bytes 106427048 | solution.py:176
  111.4 10.2 fusion.185
  121.6 11.4 %fusion.186 = f32[12,512]{1,0:T(8,128)S(1)} fusion(f32[12,512,1024]{2,1,0:T(8,128)} %get-tuple-element.409, f32[12,512]{1,0:T(8,128)S(1)} %get-tuple-element.410, pred[1024]{0:T(1024)(128)(4,1)S(1)} %iota_compare_fusion.9), kind=kLoop, calls=%fused_computation.4.clone.1.clone | loop fusion | flops 25159680 | bytes 25216000 | tf_op jit(solution)/shard_map/while/body/eval_jaxpr/reduce_sum | solution.py:84
  133.2 12.0 %bitcast_dynamic-update-slice_fusion.10 = bf16[2,512,12,64]{1,3,2,0:T(8,128)(2,1)} fusion(bf16[2,512,12,64]{1,3,2,0:T(8,128)(2,1)} %get-tuple-element.459, s32[]{:T(128)} %get-tuple-element.458, bf16[1024,12,64]{0,2,1:T(8,128)(2,1)S(1)} %bitcast.348, f32[12,512,1024]{2,1,0:T(8,128)} %get-tuple-element.409, f32[12,512]{1,0:T(8,128)S(1)} %fusion.186, ...), kind=kOutput, calls=%fused_computation.6.clone.1.clone | convolution fusion | flops 836763648 | bytes 28362240 | tf_op jit(solution)/shard_map/while/body/eval_jaxpr/hqk,khd->qhd/dot_general | solution.py:86
  158.1 11.4 %fusion.186 = f32[12,512]{1,0:T(8,128)S(1)} fusion(f32[12,512,1024]{2,1,0:T(8,128)} %get-tuple-element.409, f32[12,512]{1,0:T(8,128)S(1)} %get-tuple-element.410, pred[1024]{0:T(1024)(128)(4,1)S(1)} %iota_compare_fusion.9), kind=kLoop, calls=%fused_computation.4.clone.1.clone | loop fusion | flops 25159680 | bytes 25216000 | tf_op jit(solution)/shard_map/while/body/eval_jaxpr/reduce_sum | solution.py:84
  169.7 12.0 %bitcast_dynamic-update-slice_fusion.10 = bf16[2,512,12,64]{1,3,2,0:T(8,128)(2,1)} fusion(bf16[2,512,12,64]{1,3,2,0:T(8,128)(2,1)} %get-tuple-element.459, s32[]{:T(128)} %get-tuple-element.458, bf16[1024,12,64]{0,2,1:T(8,128)(2,1)S(1)} %bitcast.348, f32[12,512,1024]{2,1,0:T(8,128)} %get-tuple-element.409, f32[12,512]{1,0:T(8,128)S(1)} %fusion.186, ...), kind=kOutput, calls=%fused_computation.6.clone.1.clone | convolution fusion | flops 836763648 | bytes 28362240 | tf_op jit(solution)/shard_map/while/body/eval_jaxpr/hqk,khd->qhd/dot_general | solution.py:86
  197.6 18.7 %convert_reduce_fusion = (f32[3072]{0:T(1024)}, bf16[1024,3072]{1,0:T(8,128)(2,1)}, f32[1024,3072]{1,0:T(8,128)}) fusion(f32[1024,3072]{1,0:T(8,128)} %fusion.114, f32[3072]{0:T(1024)S(1)} %copy-done.48, bf16[1024,768]{1,0:T(8,128)(2,1)S(1)} %bitcast.362, bf16[3072,768]{1,0:T(8,128)(2,1)} %param.31), kind=kOutput, calls=%fused_computation.77 | convolution fusion | flops 4904186880 | bytes 37773312 | tf_op jit(solution)/shard_map/dot_general | solution.py:28
  254.1 216.8 %while.31 = (s32[]{:T(128)}, f32[2,512,12,64]{1,3,2,0:T(8,128)}, f32[2,1024,768]{1,2,0:T(8,128)}, f32[2,1024,768]{1,2,0:T(8,128)}, bf16[2,1024,768]{1,2,0:T(8,12...) while((s32[]{:T(128)}, f32[2,512,12,64]{1,3,2,0:T(8,128)}, ...), condition=%wide.region_12.13_spmd.clone, body=%wide.region_10.12_spmd.sunk.clone | while | flops 4120919040 | bytes 324178112 | solution.py:212
  258.0 10.7 exponential_divide_fusion.3
  278.8 34.0 %fusion.198 = f32[12,64,1024]{2,1,0:T(8,128)} fusion(f32[12,512,1024]{2,1,0:T(8,128)} %exponential_divide_fusion.3, f32[12,512,1024]{2,1,0:T(8,128)} %fusion.197, bf16[2,512,12,64]{1,3,2,0:T(8,128)(2,1)} %get-tuple-element.502, s32[]{:T(128)} %get-tuple-element.485), kind=kOutput, calls=%fused_computation.25.clone.1.clone | convolution fusion | flops 836770816 | bytes 104595968 | tf_op jit(solution)/shard_map/while/body/eval_jaxpr/hqk,qhd->khd/dot_general | solution.py:104
  316.7 33.3 %bitcast_dynamic-update-slice_fusion.12 = f32[2,512,12,64]{1,3,2,0:T(8,128)} fusion(f32[2,512,12,64]{1,3,2,0:T(8,128)} %get-tuple-element.486, s32[]{:T(128)} %get-tuple-element.485, bf16[1024,12,64]{0,2,1:T(8,128)(2,1)} %bitcast.347, f32[12,512,1024]{2,1,0:T(8,128)} %exponential_divide_fusion.3, f32[12,512,1024]{2,1,0:T(8,128)} %fusion.197), kind=kOutput, calls=%fused_computation.27.clone.1.clone | convolution fusion | flops 836770816 | bytes 103809536 | tf_op jit(solution)/shard_map/while/body/eval_jaxpr/hqk,khd->qhd/dot_general | solution.py:103
  350.0 10.4 fusion.199
  366.2 10.7 exponential_divide_fusion.3
  387.0 33.9 %fusion.198 = f32[12,64,1024]{2,1,0:T(8,128)} fusion(f32[12,512,1024]{2,1,0:T(8,128)} %exponential_divide_fusion.3, f32[12,512,1024]{2,1,0:T(8,128)} %fusion.197, bf16[2,512,12,64]{1,3,2,0:T(8,128)(2,1)} %get-tuple-element.502, s32[]{:T(128)} %get-tuple-element.485), kind=kOutput, calls=%fused_computation.25.clone.1.clone | convolution fusion | flops 836770816 | bytes 104595968 | tf_op jit(solution)/shard_map/while/body/eval_jaxpr/hqk,qhd->khd/dot_general | solution.py:104
  425.0 33.3 %bitcast_dynamic-update-slice_fusion.12 = f32[2,512,12,64]{1,3,2,0:T(8,128)} fusion(f32[2,512,12,64]{1,3,2,0:T(8,128)} %get-tuple-element.486, s32[]{:T(128)} %get-tuple-element.485, bf16[1024,12,64]{0,2,1:T(8,128)(2,1)} %bitcast.347, f32[12,512,1024]{2,1,0:T(8,128)} %exponential_divide_fusion.3, f32[12,512,1024]{2,1,0:T(8,128)} %fusion.197), kind=kOutput, calls=%fused_computation.27.clone.1.clone | convolution fusion | flops 836770816 | bytes 103809536 | tf_op jit(solution)/shard_map/while/body/eval_jaxpr/hqk,khd->qhd/dot_general | solution.py:103
  458.4 10.4 fusion.199
  482.2 19.5 %fusion.54 = (bf16[3072,1024]{0,1:T(8,128)(2,1)}, bf16[3072,1024]{0,1:T(8,128)(2,1)}) fusion(f32[1024,3072]{1,0:T(8,128)} %fusion.114, f32[3072]{0:T(1024)S(1)} %copy-done.49, f32[1024,3072]{1,0:T(8,128)} %get-tuple-element.262), kind=kLoop, calls=%fused_computation.72 | loop fusion | flops 72351744 | bytes 37761024 | tf_op jit(solution)/shard_map/convert_element_type | solution.py:186
  594.4 42.1 %all-reduce.4 = (f32[32,128]{1,0:T(8,128)S(1)}, f32[768]{0:T(1024)}, f32[4608]{0:T(1024)}, f32[768]{0:T(1024)}, f32[3072]{0:T(1024)}, /*index=5*/f32[768]{0:T(1024)}) all-reduce(f32[32,128]{1,0:T(8,128)S(1)} %fusion.95, f32[768]{0:T(1024)S(1)} %get-tuple-element.168, ...), channel_id=1, replica_groups=mesh['seq'=16,'span'=2] {'seq','span'}, use_global_device_ids=true, to_apply=%region_23.24 | all-reduce | flops 14080 | bytes 112640 | tf_op jit(solution)/shard_map/psum | solution.py:290
  637.1 115.6 %reduce-scatter.18.cloned.1.call-done = f32[1,48,1536]{2,1,0:T(8,128)} async-done(((f32[32,48,1536]{2,1,0:T(8,128)}), f32[1,48,1536]{2,1,0:T(8,128)}) %reduce-scatter.18.cloned.1.call-update) | async-done | bytes 294928 | tf_op jit(solution)/shard_map/reduce_scatter | solution.py:277
  752.7 141.0 %reduce-scatter.20.cloned.1.call-done = f32[1,192,384]{2,1,0:T(8,128)} async-done(((f32[32,192,384]{2,1,0:T(8,128)}), f32[1,192,384]{2,1,0:T(8,128)}) %reduce-scatter.20.cloned.1.call-update) | async-done | bytes 294928 | tf_op jit(solution)/shard_map/reduce_scatter | solution.py:283
  893.6 104.9 %reduce-scatter.12.cloned.1.call-done = f32[1,8,2304]{2,1,0:T(8,128)} async-done(((f32[32,8,2304]{2,1,0:T(8,128)}), f32[1,8,2304]{2,1,0:T(8,128)}) %reduce-scatter.12.cloned.1.call-update) | async-done | bytes 73744 | tf_op jit(solution)/shard_map/reduce_scatter | solution.py:271
  998.6 124.5 %reduce-scatter.14.cloned.1.call-done = f32[1,48,1152]{2,1,0:T(8,128)} async-done(((f32[32,48,1152]{2,1,0:T(8,128)}), f32[1,48,1152]{2,1,0:T(8,128)}) %reduce-scatter.14.cloned.1.call-update) | async-done | bytes 221200 | tf_op jit(solution)/shard_map/reduce_scatter | solution.py:259
  (280 shorter events, 256.5 us)
Async XLA Ops:
  7.2 174.6 %copy-start = (bf16[768,768]{1,0:T(8,128)(2,1)S(1)}, bf16[768,768]{1,0:T(8,128)(2,1)}, u32[]{:S(2)}) copy-start(bf16[768,768]{1,0:T(8,128)(2,1)} %param.27) | copy-start | bytes 3538948
  7.2 48.5 %copy-start.3 = (bf16[2,512,768]{2,1,0:T(8,128)(2,1)S(1)}, bf16[2,512,768]{2,1,0:T(8,128)(2,1)}, u32[]{:S(2)}) copy-start(bf16[2,512,768]{2,1,0:T(8,128)(2,1)} %param.19) | copy-start | bytes 4718596
  7.2 49.7 %copy-start.62 = (bf16[768]{0:T(1024)(128)(2,1)S(1)}, bf16[768]{0:T(1024)(128)(2,1)}, u32[]{:S(2)}) copy-start(bf16[768]{0:T(1024)(128)(2,1)} %param.23) | copy-start | bytes 4612
  7.2 85.7 %all-gather.6.cloned.1.call-start = ((), (), s32[]{:S(2)}) async-start(), calls=%async_computation.8 | async-start | bytes 4718592 | tf_op jit(solution)/shard_map/all_gather | solution.py:173
  84.7 23.6 %all-gather.4.cloned.1.call-start = ((), (), s32[]{:S(2)}) async-start(), calls=%async_computation.7 | async-start | bytes 4718592 | tf_op jit(solution)/shard_map/all_gather | solution.py:174
  88.1 20.2 %copy-start.69 = (s32[2]{0:T(128)S(1)}, s32[2]{0:T(128)}, u32[]{:S(2)}) copy-start(s32[2]{0:T(128)} %param.22) | copy-start | bytes 28
  88.1 456.2 %reduce-scatter.8.cloned.1.call-start = ((), (), s32[]{:S(2)}) async-start(), calls=%async_computation.9 | async-start | bytes 9437184 | tf_op jit(solution)/shard_map/reduce_scatter | solution.py:216
  108.3 73.4 %copy-start.4 = (bf16[2,512,768]{2,1,0:T(8,128)(2,1)S(1)}, bf16[2,512,768]{2,1,0:T(8,128)(2,1)}, u32[]{:S(2)}) copy-start(bf16[2,512,768]{2,1,0:T(8,128)(2,1)} %param.19) | copy-start | bytes 4718596
  108.3 73.4 %copy-start.40 = (f32[2,768]{1,0:T(2,128)S(1)}, f32[2,768]{1,0:T(2,128)}, u32[]{:S(2)}) copy-start(f32[2,768]{1,0:T(2,128)} %get-tuple-element.258) | copy-start | bytes 18436
  121.6 11.4 %copy-start.2 = (bf16[2,1024,768]{1,2,0:T(8,128)(2,1)S(1)}, bf16[2,1024,768]{1,2,0:T(8,128)(2,1)}, u32[]{:S(2)}) copy-start(bf16[2,1024,768]{1,2,0:T(8,128)(2,1)} %get-tuple-element.470) | copy-start | bytes 9437188 | tf_op jit(solution)/shard_map/while
  158.1 11.4 %copy-start.2 = (bf16[2,1024,768]{1,2,0:T(8,128)(2,1)S(1)}, bf16[2,1024,768]{1,2,0:T(8,128)(2,1)}, u32[]{:S(2)}) copy-start(bf16[2,1024,768]{1,2,0:T(8,128)(2,1)} %get-tuple-element.470) | copy-start | bytes 9437188 | tf_op jit(solution)/shard_map/while
  187.8 9.9 copy-start.22
  216.4 10.0 copy-start.15
  226.4 10.2 copy-start.47
  256.6 12.1 %copy-start.8 = (bf16[1,1024,768]{1,2,0:T(8,128)(2,1)}, bf16[1,1024,768]{1,2,0:T(8,128)(2,1)S(1)}, u32[]{:S(2)}) copy-start(bf16[1,1024,768]{1,2,0:T(8,128)(2,1)S(1)} %get-tuple-element.434) | copy-start | bytes 4718596 | tf_op jit(solution)/shard_map/while
  364.9 12.1 %copy-start.8 = (bf16[1,1024,768]{1,2,0:T(8,128)(2,1)}, bf16[1,1024,768]{1,2,0:T(8,128)(2,1)S(1)}, u32[]{:S(2)}) copy-start(bf16[1,1024,768]{1,2,0:T(8,128)(2,1)S(1)} %get-tuple-element.434) | copy-start | bytes 4718596 | tf_op jit(solution)/shard_map/while
  470.9 79.0 %reduce-scatter.10.cloned.1.call-start = ((), (), s32[]{:S(2)}) async-start(), calls=%async_computation.10 | async-start | bytes 9437184 | tf_op jit(solution)/shard_map/reduce_scatter | solution.py:217
  471.5 165.6 %reduce-scatter.16.cloned.1.call-start = ((), (), s32[]{:S(2)}) async-start(), calls=%async_computation.13 | async-start | bytes 2433024 | tf_op jit(solution)/shard_map/reduce_scatter | solution.py:265
  482.0 270.7 %reduce-scatter.18.cloned.1.call-start = ((), (), s32[]{:S(2)}) async-start(), calls=%async_computation.14 | async-start | bytes 9732096 | tf_op jit(solution)/shard_map/reduce_scatter | solution.py:277
  522.2 371.4 %reduce-scatter.20.cloned.1.call-start = ((), (), s32[]{:S(2)}) async-start(), calls=%async_computation.15 | async-start | bytes 9732096 | tf_op jit(solution)/shard_map/reduce_scatter | solution.py:283
  525.2 8.9 copy-start.29
  543.6 454.9 %reduce-scatter.12.cloned.1.call-start = ((), (), s32[]{:S(2)}) async-start(), calls=%async_computation.11 | async-start | bytes 2433024 | tf_op jit(solution)/shard_map/reduce_scatter | solution.py:271
  570.0 553.0 %reduce-scatter.14.cloned.1.call-start = ((), (), s32[]{:S(2)}) async-start(), calls=%async_computation.12 | async-start | bytes 7299072 | tf_op jit(solution)/shard_map/reduce_scatter | solution.py:259
  591.7 531.3 %copy-start.1 = (bf16[768,768]{1,0:T(8,128)(2,1)S(1)}, bf16[768,768]{1,0:T(8,128)(2,1)}, u32[]{:S(2)}) copy-start(bf16[768,768]{1,0:T(8,128)(2,1)} %param.27) | copy-start | bytes 3538948
  (60 other events, 213.1 us)
Sparse Core Ops, SparseCore 0:
  84.8 7.9 all-gather.5
  95.0 13.2 all-gather.3
  471.0 15.6 reduce-scatter.7
  489.0 15.6 reduce-scatter.9
  510.4 100.2 reduce-scatter.15
  618.0 134.5 reduce-scatter.17
  759.1 134.4 reduce-scatter.19
  900.3 98.1 reduce-scatter.11
  1004.8 118.1 reduce-scatter.13
where the time goes:
time: 1140 us; the launch traced here: 1130 us
  waiting for transfers between devices  502 us (44%)
  matrix products  337 us (30%)
  local copies, waits for them, and re-layouts  101 us (9%)
  other arithmetic  88.1 us (8%)
  blocking collectives  84.5 us (7%)
  between operations  14.8 us (1%)
    reduce_scatter x1, waiting for transfers between devices, shards(): lax.psum_scatter(weight_tiles(grad_down, seq_count, span_count), ('seq',...  141 us
    reduce_scatter x1, waiting for transfers between devices, shards(): lax.psum_scatter(weight_tiles(grad_qkv, seq_count, span_count), ('seq', '...  124 us
    reduce_scatter x1, waiting for transfers between devices, shards(): lax.psum_scatter(weight_tiles(grad_up, seq_count, span_count), ('seq', 's...  116 us
    reduce_scatter x1, waiting for transfers between devices, shards(): lax.psum_scatter(weight_tiles(grad_ada_part, seq_count, span_count), ('se...  105 us
    dot_general x2, matrix products, attend_back(): jnp.einsum('hqk,qhd->khd', d_scores, queries, preferred_element_type=jnp....  67.9 us
    dot_general x2, matrix products, attend_back(): jnp.einsum('hqk,khd->qhd', d_scores, keys_heads, preferred_element_type=j...  66.7 us
    all_gather x1, blocking collectives, shards(): cond_table = lax.all_gather(conditions, 'seq', axis=0, tiled=True)  42.5 us
    psum x1, blocking collectives, shards(): lax.psum((grad_gain_one, grad_gain_two, grad_up_bias, grad_down_bias, gra...  42.1 us
  transfers between devices with their start and end apart: 9, of which 5 were waited for; matrix products, arithmetic and copies ran while one was open for 11% of the time, Pallas kernels for 0%

commit v1 on v0

v1 whole, which is shorter than its diff:
```python
from functools import partial

import jax
import jax.numpy as jnp
import numpy as np
from jax import lax
from jax.experimental import pallas as pl
from jax.experimental.pallas import tpu as pltpu
from jax.sharding import PartitionSpec as P

HEADS = 12
HEAD = 64
D = 768
FF = 3072
PAIR = 128
PAIRS = HEADS // 2
LEN = 1024
SHORT = 128
SLOTS = 2
CHUNK = 768
EPSILON = 1e-5
LOG2E = 1.4426950408889634
GELU_C = 0.7978845608028654
BIG = 62 << 20
MESH = pl.DeviceIdType.MESH
F32 = jnp.float32
BF16 = jnp.bfloat16
HIGHEST = lax.Precision.HIGHEST


def nn(a, b):
    return lax.dot_general(a, b, (((1,), (0,)), ((), ())), preferred_element_type=F32)


def nt(a, b):
    return lax.dot_general(a, b, (((1,), (1,)), ((), ())), preferred_element_type=F32)


def tn(a, b):
    return lax.dot_general(a, b, (((0,), (0,)), ((), ())), preferred_element_type=F32)


def whole(shape, buffers=1):
    return pl.BlockSpec(shape, lambda *_: (0,) * len(shape), pipeline_mode=pl.Buffered(buffers))


def cost(flops, bytes_accessed, transcendentals=0):
    return pl.CostEstimate(
        flops=int(flops), bytes_accessed=int(bytes_accessed), transcendentals=int(transcendentals)
    )


def col_sum(x):
    return jnp.sum(x, axis=0, keepdims=True)


def row_mean(x):
    return jnp.mean(x, axis=-1, keepdims=True)


def rotary(length):
    half = HEAD // 2
    freq = np.power(np.float32(10000.0), -np.arange(half, dtype=np.float32) / np.float32(half))
    angles = np.arange(length, dtype=np.float32)[:, None] * freq.astype(np.float32)[None, :]
    cos, sin = np.cos(angles), np.sin(angles)
    return (
        np.concatenate([cos] * 4, axis=1).astype(np.float32),
        np.concatenate([-sin, sin, -sin, sin], axis=1).astype(np.float32),
    )


def swap_halves(x):
    lane = lax.broadcasted_iota(jnp.int32, x.shape, 1)
    first = (lane & 32) == 0
    return jnp.where(first, pltpu.roll(x, x.shape[1] - 32, 1), pltpu.roll(x, 32, 1))


def turn(x, cos, sin):
    return x * cos + swap_halves(x) * sin


def turn_back(x, cos, sin):
    return x * cos - swap_halves(x) * sin


def heads_of(x):
    lane = lax.broadcasted_iota(jnp.int32, x.shape, 1)
    zero = jnp.zeros_like(x)
    return jnp.where(lane < HEAD, x, zero), jnp.where(lane < HEAD, zero, x)


def modulation_kernel(n, own_ref, weight_ref, bias_ref, mod_ref, table_ref, send, recv, local):
    me = lax.axis_index("seq")
    barrier = pltpu.get_barrier_semaphore()
    for step in range(1, n):
        pl.semaphore_signal(
            barrier, inc=1, device_id={"seq": lax.rem(me + step, n)}, device_id_type=MESH
        )
    mine = pltpu.make_async_copy(own_ref, table_ref.at[me], local)
    mine.start()
    pl.semaphore_wait(barrier, n - 1)
    copies = []
    for step in range(1, n):
        copy = pltpu.make_async_remote_copy(
            src_ref=own_ref,
            dst_ref=table_ref.at[me],
            send_sem=send.at[step],
            recv_sem=recv.at[step],
            device_id={"seq": lax.rem(me + step, n)},
            device_id_type=MESH,
        )
        copy.start()
        copies.append(copy)
    mine.wait()
    for copy in copies:
        copy.wait()
    source = lax.broadcasted_iota(jnp.int32, (n, 128), 0).astype(F32) * SLOTS
    rows = []
    for slot in range(SLOTS):
        wanted = own_ref[SLOTS + slot : SLOTS + slot + 1, :]
        row = jnp.zeros((1, 128), F32)
        for k in range(SLOTS):
            row += col_sum(jnp.where(wanted == source + k, table_ref[:, k, :], 0.0))
        rows.append(row)
    cond = jnp.concatenate(rows + [jnp.zeros((8 - SLOTS, 128), F32)], axis=0)
    silu = (cond / (1.0 + jnp.exp(-cond))).astype(BF16)
    mod_ref[...] = nn(silu, weight_ref[...]) + bias_ref[...].astype(F32)


def modulation_call(own, ada_weight, ada_bias, n):
    vmem = pl.BlockSpec(memory_space=pltpu.VMEM)
    return pl.pallas_call(
        partial(modulation_kernel, n),
        name="modulation",
        out_shape=(
            jax.ShapeDtypeStruct((8, 6 * D), F32),
            jax.ShapeDtypeStruct((n, 8, 128), F32),
        ),
        in_specs=[vmem] * 3,
        out_specs=(vmem, vmem),
        scratch_shapes=[
            pltpu.SemaphoreType.DMA((n,)),
            pltpu.SemaphoreType.DMA((n,)),
            pltpu.SemaphoreType.DMA,
        ],
        compiler_params=pltpu.CompilerParams(
            collective_id=0, has_side_effects=True, vmem_limit_bytes=16 << 20
        ),
        cost_estimate=cost(1e7, 2e6),
    )(own, ada_weight, ada_bias)


def project_kernel(
    order, tok_ref, mod_ref, gain_ref, weight_ref, cos_ref, sin_ref,
    q_ref, h_ref, kvl_ref, kvs_ref,
):
    j = pl.program_id(0)
    row = mod_ref[pl.ds(order[j], 1), :]
    shift, scale = row[:, :D], row[:, D : 2 * D]
    x = tok_ref[...].astype(F32)
    center = x - row_mean(x)
    xhat = center * lax.rsqrt(row_mean(center * center) + EPSILON)
    hidden = (xhat * gain_ref[...].astype(F32) * (1.0 + scale) + shift).astype(BF16)
    h_ref[...] = hidden
    cos = jnp.concatenate([cos_ref[...]] * PAIRS, axis=1)
    sin = jnp.concatenate([sin_ref[...]] * PAIRS, axis=1)
    q_ref[...] = turn(nn(hidden, weight_ref[:, :D]), cos, sin).astype(BF16)
    k = turn(nn(hidden, weight_ref[:, D : 2 * D]), cos, sin).astype(BF16)
    v = nn(hidden, weight_ref[:, 2 * D :]).astype(BF16)

    @pl.when(j == 0)
    def _():
        kvl_ref[:, :D] = k
        kvl_ref[:, D:] = v

    @pl.when(j == 1)
    def _():
        kvs_ref[:, :D] = k
        kvs_ref[:, D:] = v


def project_call(place, tokens, mod, gain, weight, cos, sin, rows):
    tile = min(256, rows)
    tiles = rows // tile
    return pl.pallas_call(
        project_kernel,
        name="project",
        out_shape=(
            jax.ShapeDtypeStruct((SLOTS * rows, D), BF16),
            jax.ShapeDtypeStruct((SLOTS * rows, D), BF16),
            jax.ShapeDtypeStruct((rows, 2 * D), BF16),
            jax.ShapeDtypeStruct((rows, 2 * D), BF16),
        ),
        grid_spec=pltpu.PrefetchScalarGridSpec(
            num_scalar_prefetch=1,
            grid=(SLOTS, tiles),
            in_specs=[
                pl.BlockSpec((tile, D), lambda j, t, o: (o[j] * tiles + t, 0)),
                whole((8, 6 * D)),
                whole((1, D)),
                whole((D, 3 * D)),
                pl.BlockSpec((tile, PAIR), lambda j, t, o: (o[2] * tiles + t, 0)),
                pl.BlockSpec((tile, PAIR), lambda j, t, o: (o[2] * tiles + t, 0)),
            ],
            out_specs=[
                pl.BlockSpec((tile, D), lambda j, t, o: (j * tiles + t, 0)),
                pl.BlockSpec((tile, D), lambda j, t, o: (j * tiles + t, 0)),
                pl.BlockSpec((tile, 2 * D), lambda j, t, o: (t + j * (tiles - 1 - t), 0)),
                pl.BlockSpec((tile, 2 * D), lambda j, t, o: (j * t, 0)),
            ],
        ),
        compiler_params=pltpu.CompilerParams(vmem_limit_bytes=BIG),
        cost_estimate=cost(2 * SLOTS * rows * D * 3 * D, 14e6),
    )(place, tokens, mod, gain, weight, cos, sin)


def attend_slot(q, keys, values):
    outs, stats = [], []
    for head, qh in enumerate(heads_of(q)):
        scores = [nt(k, qh) for k in keys]
        top = jnp.max(scores[0], axis=0, keepdims=True)
        for s in scores[1:]:
            top = jnp.maximum(top, jnp.max(s, axis=0, keepdims=True))
        total, out = None, None
        for s, v in zip(scores, values):
            p = jnp.exp2((s - top) * (0.125 * LOG2E))
            part = col_sum(p)
            o = tn(v, p.astype(BF16))
            total = part if total is None else total + part
            out = o if out is None else out + o
        out = out[head * HEAD : (head + 1) * HEAD] / total
        outs.append(out)
        stats.append(top * (0.125 * LOG2E) + jnp.log2(total))
    return jnp.concatenate(outs, axis=0).T.astype(BF16), stats


def attend_kernel(ql, qs, ko, vo, kx, vx, ks, vs, out_ref, lse_ref):
    rows = ql.shape[0]
    out, stats = attend_slot(ql[...], [ko[...], kx[...]], [vo[...], vx[...]])
    out_ref[:rows, :] = out
    lse_ref[0, 0:1, :] = stats[0]
    lse_ref[0, 1:2, :] = stats[1]
    out, stats = attend_slot(qs[...], [ks[...]], [vs[...]])
    out_ref[rows:, :] = out
    lse_ref[0, 2:3, :] = stats[0]
    lse_ref[0, 3:4, :] = stats[1]


def pair_specs(rows):
    def at(n, block, base):
        return pl.BlockSpec((n, PAIR), lambda h: (block, base + h))

    return [
        at(rows, 0, 0),
        at(rows, 1, 0),
        at(rows, 0, 0),
        at(rows, 0, PAIRS),
        at(LEN - rows, 0, 0),
        at(LEN - rows, 0, PAIRS),
        at(SHORT, 0, 0),
        at(SHORT, 0, PAIRS),
    ]


def attend_call(q, kv_own, kv_other, kv_short, rows):
    return pl.pallas_call(
        attend_kernel,
        name="attend",
        grid=(PAIRS,),
        out_shape=(
            jax.ShapeDtypeStruct((SLOTS * rows, D), BF16),
            jax.ShapeDtypeStruct((PAIRS, 4, rows), F32),
        ),
        in_specs=pair_specs(rows),
        out_specs=(
            pl.BlockSpec((SLOTS * rows, PAIR), lambda h: (0, h)),
            pl.BlockSpec((1, 4, rows), lambda h: (h, 0, 0)),
        ),
        compiler_params=pltpu.CompilerParams(vmem_limit_bytes=BIG),
        cost_estimate=cost(16 * D * rows * (LEN + SHORT), 9e6, HEADS * rows * (LEN + SHORT)),
    )(q, q, kv_own, kv_own, kv_other, kv_other, kv_short, kv_short)


def attend_back_slot(q, keys, values, d_out, lse):
    d_keys, d_values = [None] * len(keys), [None] * len(keys)
    d_query = []
    q_heads, d_heads = heads_of(q), heads_of(d_out)
    for head in range(2):
        qh, dh = q_heads[head], d_heads[head]
        probs = [jnp.exp2(nt(k, qh) * (0.125 * LOG2E) - lse[head]) for k in keys]
        d_probs = [nt(v, dh) for v in values]
        inner = None
        for p, dp in zip(probs, d_probs):
            part = col_sum(p * dp)
            inner = part if inner is None else inner + part
        dq = None
        for i in range(len(keys)):
            d_scores = (probs[i] * (d_probs[i] - inner) * 0.125).astype(BF16)
            dv = nn(probs[i].astype(BF16), dh)
            dk = nn(d_scores, qh)
            part = tn(keys[i], d_scores)
            dq = part if dq is None else dq + part
            d_values[i] = dv if head == 0 else d_values[i] + dv
            d_keys[i] = dk if head == 0 else d_keys[i] + dk
        d_query.append(dq[head * HEAD : (head + 1) * HEAD])
    return jnp.concatenate(d_query, axis=0).T, d_keys, d_values


def attend_back_kernel(
    place, ql, qs, ko, vo, kx, vx, ks, vs, dol, dos, lse, cos, sin,
    dq_ref, dko, dvo, dkx, dvx, dks, dvs,
):
    rows = ql.shape[0]
    stats = lse[0]
    dq, dk, dv = attend_back_slot(
        ql[...], [ko[...], kx[...]], [vo[...], vx[...]], dol[...], [stats[0:1], stats[1:2]]
    )
    dq_ref[:rows, :] = turn_back(dq, cos[...], sin[...]).astype(BF16)
    dko[...] = dk[0]
    dvo[...] = dv[0]
    dkx[...] = dk[1].astype(BF16)
    dvx[...] = dv[1].astype(BF16)
    dq, dk, dv = attend_back_slot(
        qs[...], [ks[...]], [vs[...]], dos[...], [stats[2:3], stats[3:4]]
    )
    dq_ref[rows:, :] = turn_back(dq, cos[...], sin[...]).astype(BF16)
    dks[...] = dk[0]
    dvs[...] = dv[0]


def attend_back_call(place, q, kv_own, kv_other, kv_short, d_att, lse, cos, sin, rows):
    specs = [
        pl.BlockSpec(s.block_shape, partial(lambda m, h, o: m(h), s.index_map))
        for s in pair_specs(rows)
    ]
    other = LEN - rows
    return pl.pallas_call(
        attend_back_kernel,
        name="attend_back",
        out_shape=(
            jax.ShapeDtypeStruct((SLOTS * rows, D), BF16),
            jax.ShapeDtypeStruct((rows, D), F32),
            jax.ShapeDtypeStruct((rows, D), F32),
            jax.ShapeDtypeStruct((other, D), BF16),
            jax.ShapeDtypeStruct((other, D), BF16),
            jax.ShapeDtypeStruct((SHORT, D), F32),
            jax.ShapeDtypeStruct((SHORT, D), F32),
        ),
        grid_spec=pltpu.PrefetchScalarGridSpec(
            num_scalar_prefetch=1,
            grid=(PAIRS,),
            in_specs=specs
            + [
                pl.BlockSpec((rows, PAIR), lambda h, o: (0, h)),
                pl.BlockSpec((rows, PAIR), lambda h, o: (1, h)),
                pl.BlockSpec((1, 4, rows), lambda h, o: (h, 0, 0)),
                pl.BlockSpec((rows, PAIR), lambda h, o: (o[2], 0)),
                pl.BlockSpec((rows, PAIR), lambda h, o: (o[2], 0)),
            ],
            out_specs=[
                pl.BlockSpec((SLOTS * rows, PAIR), lambda h, o: (0, h)),
                pl.BlockSpec((rows, PAIR), lambda h, o: (0, h)),
                pl.BlockSpec((rows, PAIR), lambda h, o: (0, h)),
                pl.BlockSpec((other, PAIR), lambda h, o: (0, h)),
                pl.BlockSpec((other, PAIR), lambda h, o: (0, h)),
                pl.BlockSpec((SHORT, PAIR), lambda h, o: (0, h)),
                pl.BlockSpec((SHORT, PAIR), lambda h, o: (0, h)),
            ],
        ),
        compiler_params=pltpu.CompilerParams(vmem_limit_bytes=BIG),
        cost_estimate=cost(40 * D * rows * (LEN + SHORT), 16e6, HEADS * rows * (LEN + SHORT)),
    )(
        place, q, q, kv_own, kv_own, kv_other, kv_other, kv_short, kv_short,
        d_att, d_att, lse, cos, sin,
    )


def add_to(ref, value, first):
    @pl.when(first)
    def _():
        ref[...] = value

    @pl.when(jnp.logical_not(first))
    def _():
        ref[...] += value


def feed_kernel(
    order, tok_ref, att_ref, cot_ref, mod_ref, gain_ref, wo_ref, wu_ref, bu_ref, wd_ref, bd_ref,
    out_ref, dmid_ref, datt_ref, act_ref, dlow_ref, h_ref, dup_ref, dattn_ref,
    dmod_ref, dgain_ref, dbd_ref, dbu_ref,
):
    j, t = pl.program_id(0), pl.program_id(1)
    row = mod_ref[pl.ds(order[j], 1), :]
    gate1, shift2 = row[:, 2 * D : 3 * D], row[:, 3 * D : 4 * D]
    scale2, gate2 = row[:, 4 * D : 5 * D], row[:, 5 * D :]
    gain = gain_ref[...].astype(F32)
    attention = nn(att_ref[...], wo_ref[...])
    middle = tok_ref[...].astype(F32) + gate1 * attention
    center = middle - row_mean(middle)
    r = lax.rsqrt(row_mean(center * center) + EPSILON)
    xhat = center * r
    hidden = (xhat * gain * (1.0 + scale2) + shift2).astype(BF16)
    h_ref[...] = hidden
    dy = cot_ref[...].astype(F32)
    d_low = (gate2 * dy).astype(BF16)
    dlow_ref[...] = d_low
    lowered, d_hidden = None, None
    sums = []
    for f in range(0, FF, CHUNK):
        cols = slice(f, f + CHUNK)
        up = nn(hidden, wu_ref[:, cols]) + bu_ref[:, cols].astype(F32)
        d_act = nt(d_low, wd_ref[cols, :])
        square = up * up
        bend = jnp.tanh(up * (GELU_C + (GELU_C * 0.044715) * square))
        half = 0.5 * (1.0 + bend)
        act = (up * half).astype(BF16)
        slope = half + (0.5 * up) * (1.0 - bend * bend) * (
            GELU_C + (3 * GELU_C * 0.044715) * square
        )
        d_up = (d_act * slope).astype(BF16)
        act_ref[:, cols] = act
        dup_ref[:, cols] = d_up
        sums.append(col_sum(d_up.astype(F32)))
        low = nn(act, wd_ref[cols, :])
        dh = nt(d_up, wu_ref[:, cols])
        lowered = low if lowered is None else lowered + low
        d_hidden = dh if d_hidden is None else d_hidden + dh
    lowered = lowered + bd_ref[...].astype(F32)
    out_ref[...] = (middle + gate2 * lowered).astype(BF16)
    d_gate2 = col_sum(dy * lowered)
    d_shift2 = col_sum(d_hidden)
    hx = col_sum(d_hidden * xhat)
    e = d_hidden * (1.0 + scale2)
    fx = e * gain
    d_mid = dy + r * (fx - row_mean(fx) - xhat * row_mean(fx * xhat))
    dmid_ref[...] = d_mid
    d_gate1 = col_sum(d_mid * attention)
    d_attention = (gate1 * d_mid).astype(BF16)
    dattn_ref[...] = d_attention
    datt_ref[...] = nt(d_attention, wo_ref[...]).astype(BF16)
    first = jnp.logical_and(j == 0, t == 0)
    add_to(
        dmod_ref,
        jnp.concatenate(
            [d_gate1, d_shift2, hx * gain, d_gate2, jnp.zeros((4, D), F32)], axis=0
        )[None],
        t == 0,
    )
    add_to(dgain_ref, hx * (1.0 + scale2), first)
    add_to(dbd_ref, col_sum(d_low.astype(F32)), first)
    add_to(dbu_ref, jnp.concatenate(sums, axis=1), first)


def feed_call(place, tokens, att, cot, mod, gain, wo, wu, bu, wd, bd, rows):
    tile = min(256, rows)
    tiles = rows // tile

    def own(j, t, o):
        return (o[j] * tiles + t, 0)

    def sorted_(j, t, o):
        return (j * tiles + t, 0)

    n = SLOTS * rows
    return pl.pallas_call(
        feed_kernel,
        name="feed",
        out_shape=(
            jax.ShapeDtypeStruct((n, D), BF16),
            jax.ShapeDtypeStruct((n, D), F32),
            jax.ShapeDtypeStruct((n, D), BF16),
            jax.ShapeDtypeStruct((n, FF), BF16),
            jax.ShapeDtypeStruct((n, D), BF16),
            jax.ShapeDtypeStruct((n, D), BF16),
            jax.ShapeDtypeStruct((n, FF), BF16),
            jax.ShapeDtypeStruct((n, D), BF16),
            jax.ShapeDtypeStruct((SLOTS, 8, D), F32),
            jax.ShapeDtypeStruct((1, D), F32),
            jax.ShapeDtypeStruct((1, D), F32),
            jax.ShapeDtypeStruct((1, FF), F32),
        ),
        grid_spec=pltpu.PrefetchScalarGridSpec(
            num_scalar_prefetch=1,
            grid=(SLOTS, tiles),
            in_specs=[
                pl.BlockSpec((tile, D), own),
                pl.BlockSpec((tile, D), sorted_),
                pl.BlockSpec((tile, D), own),
                whole((8, 6 * D)),
                whole((1, D)),
                whole((D, D)),
                whole((D, FF)),
                whole((1, FF)),
                whole((FF, D)),
                whole((1, D)),
            ],
            out_specs=[
                pl.BlockSpec((tile, D), own),
                pl.BlockSpec((tile, D), sorted_),
                pl.BlockSpec((tile, D), sorted_),
                pl.BlockSpec((tile, FF), sorted_),
                pl.BlockSpec((tile, D), sorted_),
                pl.BlockSpec((tile, D), sorted_),
                pl.BlockSpec((tile, FF), sorted_),
                pl.BlockSpec((tile, D), sorted_),
                pl.BlockSpec((1, 8, D), lambda j, t, o: (o[j], 0, 0)),
                pl.BlockSpec((1, D), lambda j, t, o: (0, 0)),
                pl.BlockSpec((1, D), lambda j, t, o: (0, 0)),
                pl.BlockSpec((1, FF), lambda j, t, o: (0, 0)),
            ],
        ),
        compiler_params=pltpu.CompilerParams(vmem_limit_bytes=BIG),
        cost_estimate=cost(2 * n * D * (4 * FF + 2 * D), 40e6, n * FF),
    )(place, tokens, att, cot, mod, gain, wo, wu, bu, wd, bd)


def weight_kernel(place, left_ref, right_ref, other_ref, mine_ref):
    value = tn(left_ref[...], right_ref[...]).astype(BF16)

    @pl.when(pl.program_id(0) == 0)
    def _():
        other_ref[...] = value

    @pl.when(pl.program_id(0) == 1)
    def _():
        mine_ref[...] = value


def weight_call(place, left, right, tile, name):
    n, rows = left.shape
    half = right.shape[1] // 2
    tiles = rows // tile
    return pl.pallas_call(
        weight_kernel,
        name=name,
        out_shape=(jax.ShapeDtypeStruct((rows, half), BF16),) * 2,
        grid_spec=pltpu.PrefetchScalarGridSpec(
            num_scalar_prefetch=1,
            grid=(2, tiles),
            in_specs=[
                pl.BlockSpec((n, tile), lambda c, m, o: (0, m)),
                pl.BlockSpec((n, half), lambda c, m, o: (0, c * o[2] + (1 - c) * (1 - o[2]))),
            ],
            out_specs=[
                pl.BlockSpec((tile, half), lambda c, m, o: (m + c * (tiles - 1 - m), 0)),
                pl.BlockSpec((tile, half), lambda c, m, o: (c * m, 0)),
            ],
        ),
        compiler_params=pltpu.CompilerParams(vmem_limit_bytes=BIG),
        cost_estimate=cost(2 * n * rows * 2 * half, 2 * (n * rows + 2 * (n + rows) * half)),
    )(place, left, right)


def flip(index, bit):
    return index + bit - 2 * bit * ((index // bit) % 2)


def reduce_tiles(other, mine):
    s = lax.axis_index("seq")
    x, y, z = s % 2, (s // 2) % 2, s // 4
    rows, cols = mine.shape
    part = rows // 16
    came = lax.ppermute(other, "span", [(0, 1), (1, 0)])
    pair = (mine.astype(F32) + came.astype(F32)).reshape(2, 2, 2, 2, part, cols)
    along_x = [(i, flip(i, 1)) for i in range(16)]
    along_y = [(i, flip(i, 2)) for i in range(16)]

    def pick(array, axis, index):
        return lax.dynamic_index_in_dim(array, index, axis, keepdims=False)

    first, second = pair[0], pair[1]
    sent_a = lax.ppermute(pick(first, 2, 1 - x).astype(BF16), "seq", along_x)
    sent_b = lax.ppermute(pick(second, 1, 1 - y).astype(BF16), "seq", along_y)
    first = pick(first, 2, x) + sent_a.astype(F32)
    second = pick(second, 1, y) + sent_b.astype(F32)
    sent_a = lax.ppermute(pick(first, 1, 1 - y).astype(BF16), "seq", along_y)
    sent_b = lax.ppermute(pick(second, 1, 1 - x).astype(BF16), "seq", along_x)
    first = pick(first, 1, y) + sent_a.astype(F32)
    second = pick(second, 1, x) + sent_b.astype(F32)
    quarter = jnp.concatenate([first, second], axis=0)
    total = pick(quarter, 0, z)
    for step in range(1, 4):
        came = lax.ppermute(
            pick(quarter, 0, (z + step) % 4).astype(BF16),
            "seq",
            [(i, (i + 4 * step) % 16) for i in range(16)],
        )
        total = total + came.astype(F32)
    return total


def weight_gradient(place, left, right, tile, name):
    seq, span = lax.axis_size("seq"), lax.axis_size("span")
    if seq == 16 and span == 2:
        return reduce_tiles(*weight_call(place, left, right, tile, name))
    grad = tn(left, right)
    rows, cols = grad.shape
    shaped = grad.reshape(seq, rows // seq, span, cols // span).transpose(0, 2, 1, 3)
    return lax.psum_scatter(
        shaped.reshape(seq * span, rows // seq, cols // span),
        ("seq", "span"),
        scatter_dimension=0,
        tiled=True,
    )[0]


def join_kernel(place, dq_ref, dk_ref, dv_ref, ek_ref, ev_ref, sk_ref, sv_ref, cos, sin, out_ref):
    j, t = pl.program_id(0), pl.program_id(1)
    out_ref[:, :D] = dq_ref[...]
    wide_cos = jnp.concatenate([cos[...]] * PAIRS, axis=1)
    wide_sin = jnp.concatenate([sin[...]] * PAIRS, axis=1)

    @pl.when(j == 0)
    def _():
        dk = dk_ref[...] + ek_ref[...].astype(F32)
        out_ref[:, D : 2 * D] = turn_back(dk, wide_cos, wide_sin).astype(BF16)
        out_ref[:, 2 * D :] = (dv_ref[...] + ev_ref[...].astype(F32)).astype(BF16)

    @pl.when(j == 1)
    def _():
        out_ref[:, D:] = jnp.zeros((out_ref.shape[0], 2 * D), BF16)

    @pl.when(jnp.logical_and(j == 1, jnp.logical_and(t == 0, place[2] == 0)))
    def _():
        dk = turn_back(sk_ref[...], wide_cos[:SHORT], wide_sin[:SHORT])
        out_ref[:SHORT, D : 2 * D] = dk.astype(BF16)
        out_ref[:SHORT, 2 * D :] = sv_ref[...].astype(BF16)


def join_call(place, dq, dk, dv, ek, ev, sk, sv, cos, sin, rows):
    tile = min(256, rows)
    tiles = rows // tile

    def long(j, t, o):
        return (t + j * (tiles - 1 - t), 0)

    return pl.pallas_call(
        join_kernel,
        name="join",
        out_shape=jax.ShapeDtypeStruct((SLOTS * rows, 3 * D), BF16),
        grid_spec=pltpu.PrefetchScalarGridSpec(
            num_scalar_prefetch=1,
            grid=(SLOTS, tiles),
            in_specs=[pl.BlockSpec((tile, D), lambda j, t, o: (j * tiles + t, 0))]
            + [pl.BlockSpec((tile, D), long)] * 4
            + [whole((SHORT, D))] * 2
            + [pl.BlockSpec((tile, PAIR), lambda j, t, o: (o[2] * tiles + t, 0))] * 2,
            out_specs=pl.BlockSpec((tile, 3 * D), lambda j, t, o: (j * tiles + t, 0)),
        ),
        compiler_params=pltpu.CompilerParams(vmem_limit_bytes=BIG),
        cost_estimate=cost(1e7, 12e6),
    )(place, dq, dk, dv, ek, ev, sk, sv, cos, sin)


def last_kernel(
    order, tok_ref, dqkv_ref, dmid_ref, mod_ref, gain_ref, weight_ref,
    out_ref, dmod_ref, dgain_ref,
):
    j, t = pl.program_id(0), pl.program_id(1)
    scale = mod_ref[pl.ds(order[j], 1), :][:, D : 2 * D]
    gain = gain_ref[...].astype(F32)
    d_hidden = nt(dqkv_ref[...], weight_ref[...])
    x = tok_ref[...].astype(F32)
    center = x - row_mean(x)
    r = lax.rsqrt(row_mean(center * center) + EPSILON)
    xhat = center * r
    hx = col_sum(d_hidden * xhat)
    fx = d_hidden * (1.0 + scale) * gain
    out_ref[...] = dmid_ref[...] + r * (fx - row_mean(fx) - xhat * row_mean(fx * xhat))
    first = jnp.logical_and(j == 0, t == 0)
    add_to(
        dmod_ref,
        jnp.concatenate([col_sum(d_hidden), hx * gain, jnp.zeros((6, D), F32)], axis=0)[None],
        t == 0,
    )
    add_to(dgain_ref, hx * (1.0 + scale), first)


def last_call(place, tokens, dqkv, dmid, mod, gain, weight, rows):
    tile = min(256, rows)
    tiles = rows // tile

    def own(j, t, o):
        return (o[j] * tiles + t, 0)

    def sorted_(j, t, o):
        return (j * tiles + t, 0)

    n = SLOTS * rows
    return pl.pallas_call(
        last_kernel,
        name="last",
        out_shape=(
            jax.ShapeDtypeStruct((n, D), F32),
            jax.ShapeDtypeStruct((SLOTS, 8, D), F32),
            jax.ShapeDtypeStruct((1, D), F32),
        ),
        grid_spec=pltpu.PrefetchScalarGridSpec(
            num_scalar_prefetch=1,
            grid=(SLOTS, tiles),
            in_specs=[
                pl.BlockSpec((tile, D), own),
                pl.BlockSpec((tile, 3 * D), sorted_),
                pl.BlockSpec((tile, D), sorted_),
                whole((8, 6 * D)),
                whole((1, D)),
                whole((D, 3 * D)),
            ],
            out_specs=[
                pl.BlockSpec((tile, D), own),
                pl.BlockSpec((1, 8, D), lambda j, t, o: (o[j], 0, 0)),
                pl.BlockSpec((1, D), lambda j, t, o: (0, 0)),
            ],
        ),
        compiler_params=pltpu.CompilerParams(vmem_limit_bytes=BIG),
        cost_estimate=cost(2 * n * D * 3 * D, 18e6),
    )(place, tokens, dqkv, dmid, mod, gain, weight)


def from_peers(array, span):
    return [
        lax.ppermute(array, "span", [((i + step) % span, i) for i in range(span)])
        for step in range(1, span)
    ]


def gather_all(flat):
    seq, span = lax.axis_size("seq"), lax.axis_size("span")
    return lax.all_gather(flat, ("seq", "span"), axis=0).reshape(seq, span, flat.shape[0])


def shards(
    tokens, conditions, assignment, lengths, norm1_gain, ada_weight, ada_bias, qkv_weight,
    out_weight, norm2_gain, up_weight, up_bias, down_weight, down_bias, cotangent,
):
    slots, rows, _ = tokens.shape
    seq, span = lax.axis_size("seq"), lax.axis_size("span")
    seq_at, span_at = lax.axis_index("seq"), lax.axis_index("span")
    flat = slots * rows
    longest = (lengths[1] > lengths[0]).astype(jnp.int32)
    place = jnp.stack([longest, 1 - longest, span_at.astype(jnp.int32)])
    cos, sin = (jnp.asarray(table) for table in rotary(LEN))
    cond = conditions.astype(F32)
    asked = jnp.broadcast_to(assignment.astype(F32)[:, None], (slots, 128))
    own = jnp.concatenate([cond, asked, jnp.zeros((8 - 2 * slots, 128), F32)], axis=0)
    mod, table = modulation_call(own, ada_weight, ada_bias[None], seq)

    tokens2 = tokens.reshape(flat, D)
    gain1, gain2 = norm1_gain[None], norm2_gain[None]
    q, hidden1, kv_long, kv_tail = project_call(
        place, tokens2, mod, gain1, qkv_weight, cos, sin, rows
    )
    pieces = from_peers(kv_long, span)
    kv_other = pieces[0] if span == 2 else jnp.concatenate(pieces, axis=0)
    kv_short = kv_tail[:SHORT]
    sent = [lax.ppermute(kv_short, "span", [(0, i)]) for i in range(1, span)]
    kv_short = jnp.where(span_at == 0, kv_short, sum(sent[1:], sent[0]))
    att, lse = attend_call(q, kv_long, kv_other, kv_short, rows)
    (
        out, d_mid, d_att, act, d_low, hidden2, d_up, d_attention, d_mod2, d_gain2, d_bd, d_bu,
    ) = feed_call(
        place, tokens2, att, cotangent.reshape(flat, D), mod, gain2, out_weight, up_weight,
        up_bias[None], down_weight, down_bias[None], rows,
    )
    grad_down = weight_gradient(place, act, d_low, 768, "weight_down")
    grad_up = weight_gradient(place, hidden2, d_up, 256, "weight_up")
    grad_out = weight_gradient(place, att, d_attention, 768, "weight_out")
    early = gather_all(
        jnp.concatenate([d_mod2[:, :4].reshape(-1), d_gain2[0], d_bd[0], d_bu[0]])
    )

    dq, dk, dv, dkx, dvx, dks, dvs = attend_back_call(
        place, q, kv_long, kv_other, kv_short, d_att, lse, cos, sin, rows
    )
    ek = ev = None
    for step in range(1, span):
        back = [((i, (i + step) % span)) for i in range(span)]
        cut = slice((step - 1) * rows, step * rows)
        pk, pv = lax.ppermute((dkx[cut], dvx[cut]), "span", back)
        ek = pk if ek is None else (ek.astype(F32) + pk.astype(F32))
        ev = pv if ev is None else (ev.astype(F32) + pv.astype(F32))
    d_short = jnp.concatenate([dks, dvs], axis=1)
    for step in range(1, span):
        d_short = d_short + lax.ppermute(
            jnp.concatenate([dks, dvs], axis=1), "span", [(step, 0)]
        )
    d_qkv = join_call(
        place, dq, dk, dv, ek, ev, d_short[:, :D], d_short[:, D:], cos, sin, rows
    )
    grad_qkv = weight_gradient(place, hidden1, d_qkv, 384, "weight_qkv")
    grad_in, d_mod1, d_gain1 = last_call(
        place, tokens2, d_qkv, d_mid, mod, gain1, qkv_weight, rows
    )
    late = gather_all(jnp.concatenate([d_mod1[:, :2].reshape(-1), d_gain1[0]]))

    cut = slots * 4 * D
    mods2 = jnp.sum(early[:, :, :cut], axis=1).reshape(seq * slots, 4 * D)
    sums2 = jnp.sum(early[:, :, cut:], axis=(0, 1))
    cut = slots * 2 * D
    mods1 = jnp.sum(late[:, :, :cut], axis=1).reshape(seq * slots, 2 * D)
    gain1_sum = jnp.sum(late[:, :, cut:], axis=(0, 1))
    d_mods = jnp.concatenate([mods1, mods2], axis=1)
    grad_ada_bias = jnp.sum(d_mods, axis=0)
    cond_all = table[:, :slots].reshape(seq * slots, 128)
    assign_all = table[:, slots : 2 * slots, 0].reshape(seq * slots)
    number = jnp.arange(seq * slots, dtype=jnp.int32).astype(F32)
    picker = (assign_all[:, None] == number[None, :]).astype(F32)
    exact = partial(lax.dot_general, precision=HIGHEST, preferred_element_type=F32)
    cond_rows = exact(picker, cond_all, (((1,), (0,)), ((), ())))
    silu_low = jax.nn.silu(cond_rows).astype(BF16).astype(F32)
    ada_rows, ada_cols = 128 // seq, 6 * D // span
    grad_ada = exact(
        lax.dynamic_slice_in_dim(silu_low, seq_at * ada_rows, ada_rows, 1),
        lax.dynamic_slice_in_dim(d_mods, span_at * ada_cols, ada_cols, 1),
        (((0,), (0,)), ((), ())),
    )
    wanted = lax.dynamic_slice_in_dim(picker, seq_at * slots, slots, 1)
    own_mods = exact(wanted, d_mods, (((0,), (0,)), ((), ())))
    d_silu = exact(own_mods, ada_weight.astype(F32), (((1,), (1,)), ((), ())))
    grad_cond = jax.vjp(jax.nn.silu, cond)[1](d_silu)[0]
    return (
        out.reshape(tokens.shape),
        grad_in.reshape(tokens.shape),
        grad_cond,
        gain1_sum,
        grad_ada,
        grad_ada_bias,
        grad_qkv,
        grad_out,
        sums2[:D],
        grad_up,
        sums2[2 * D :],
        grad_down,
        sums2[D : 2 * D],
    )


def solution(mesh):
    data, table, one = P("seq", "span", None), P("seq", None), P("seq")
    tile = P("seq", "span")
    in_specs = (data, table, one, one) + (P(),) * 10 + (data,)
    out_specs = (data, data, table, P(), tile, P(), tile, tile, P(), tile, P(), tile, P())
    return jax.shard_map(shards, mesh=mesh, in_specs=in_specs, out_specs=out_specs, check_vma=False)
```

time: 1140 us -> 389 us (0.34)
  waiting for transfers between devices: 502 us -> 36.2 us
  matrix products: 337 us -> 5.83 us
  Pallas kernels: 0 us -> 164 us
  local copies, waits for them, and re-layouts: 101 us -> 36 us
  other arithmetic: 88.1 us -> 37.7 us
  starting transfers between devices: 1.37 us -> 45.8 us
  blocking collectives: 84.5 us -> 41.8 us
    reduce_scatter x7 -> x0, waiting for transfers between devices: 486 us -> none  [the longest x1 141 us: shards(): lax.psum_scatter(weight_tiles(grad_down, seq_count, span_count), ('seq',...]
    dot_general x31 -> x4, matrix products: 337 us -> 5.83 us  [the longest x1 1.95 us: shards(): exact(lax.dynamic_slice_in_dim(silu_low, seq_at * ada_rows, ada_rows, 1),...]
    pallas_call x0 -> x11, Pallas kernels: none -> 164 us  [the longest x4 42.3 us: weight_call(): pl.pallas_call(weight_kernel, name=name, out_shape=(jax.ShapeDtypeStruct(...]
    ppermute x0 -> x37, starting transfers between devices: none -> 45.7 us  [the longest x12 22.7 us: reduce_tiles(): lax.ppermute(pick(quarter, 0, (z + step) % 4).astype(BF16), 'seq', [(i, (...]
    psum x1 -> x0, blocking collectives: 42.1 us -> none  [shards(): lax.psum((grad_gain_one, grad_gain_two, grad_up_bias, grad_down_bias, gra...]
    ppermute x0 -> x37, waiting for transfers between devices: none -> 36.2 us  [the longest x12 15 us: reduce_tiles(): lax.ppermute(pick(quarter, 0, (z + step) % 4).astype(BF16), 'seq', [(i, (...]
    reduce_sum x11 -> x5, other arithmetic: 40 us -> 7.15 us  [the longest x1 2.62 us: shards(): mods2 = jnp.sum(early[:, :, :cut], axis=1).reshape(seq * slots, 4 * D)]
    convert_element_type x10 -> x7, other arithmetic: 27.8 us -> 1.83 us  [the longest x1 0.66 us: shards(): asked = jnp.broadcast_to(assignment.astype(F32)[:, None], (slots, 128))]
  transfers between devices with their start and end apart: 9 -> 38, of which waited for: 5 -> 10; matrix products, arithmetic and copies ran while one was open for 11% -> 17% of each run, Pallas kernels for 0% -> 22%
where the time goes in v1:
time: 389 us; the launch traced here: 384 us
  Pallas kernels  164 us (42%)
  starting transfers between devices  45.8 us (12%)
  blocking collectives  41.8 us (11%)
  other arithmetic  37.7 us (10%)
  waiting for transfers between devices  36.2 us (9%)
  local copies, waits for them, and re-layouts  36 us (9%)
  between operations  16.4 us (4%)
  matrix products  5.83 us (1%)
    pallas_call x4, Pallas kernels, weight_call(): pl.pallas_call(weight_kernel, name=name, out_shape=(jax.ShapeDtypeStruct(...  42.3 us
    all_gather x1, blocking collectives, gather_all(): lax.all_gather(flat, ('seq', 'span'), axis=0)  41.8 us
    pallas_call x1, Pallas kernels, feed_call(): pl.pallas_call(feed_kernel, name='feed', out_shape=(jax.ShapeDtypeStruct(...  37.1 us
    pallas_call x1, Pallas kernels, attend_back_call(): pl.pallas_call(attend_back_kernel, name='attend_back', out_shape=(jax.Sha...  28.9 us
    ppermute x12, starting transfers between devices, reduce_tiles(): lax.ppermute(pick(quarter, 0, (z + step) % 4).astype(BF16), 'seq', [(i, (...  22.7 us
    pallas_call x1, Pallas kernels, attend_call(): pl.pallas_call(attend_kernel, name='attend', grid=(PAIRS,), out_shape=(ja...  16.8 us
    ppermute x12, waiting for transfers between devices, reduce_tiles(): lax.ppermute(pick(quarter, 0, (z + step) % 4).astype(BF16), 'seq', [(i, (...  15 us
    ppermute x4, waiting for transfers between devices, reduce_tiles(): sent_b = lax.ppermute(pick(second, 1, 1 - x).astype(BF16), 'seq', along_x)  13.8 us
  transfers between devices with their start and end apart: 38, of which 10 were waited for; matrix products, arithmetic and copies ran while one was open for 17% of the time, Pallas kernels for 22%

profile of v1, /device:TPU:0, one launch (start us, length us, event | category | flops | bytes accessed | tf_op | source)
XLA Modules:
  0.0 384.2 jit_solution(10849460781620531478)
XLA Ops:
  15.3 10.1 %modulation.1 = (f32[8,4608]{1,0:T(8,128)S(1)}, f32[16,8,128]{2,1,0:T(8,128)S(1)}) custom-call(f32[8,128]{1,0:T(8,128)S(1)} %maximum_maximum_fusion.own_ref, bf16[128,4608]{1,0:T(8,128)(2,1)S(1)} %copy-done, bf16[1,4608]{1,0:T(2,128)(2,1)S(1)} %broadcast_in_dim.27.bias_ref), custom_call_target="tpu_custom_call" | custom-call | flops 10000000 | bytes 2000000 | tf_op jit(solution)/shard_map/modulation/pallas_call | solution.py:132
  26.0 10.8 %project.1 = (bf16[1024,768]{1,0:T(8,128)(2,1)}, bf16[1024,768]{1,0:T(8,128)(2,1)}, bf16[512,1536]{1,0:T(8,128)(2,1)}, bf16[512,1536]{1,0:T(8,128)(2,1)}) custom-call(s32[3]{0:T(128)} %pad_add_fusion.order.place, bf16[1024,768]{1,0:T(8,128)(2,1)} %bitcast.158, f32[8,4608]{1,0:T(8,128)} %copy-done.2, bf16[1,768]{1,0:T(2,128)(2,1)} %broadcast_in_dim.28.gain_ref, ...), custom_call_target="tpu_custom_call" | custom-call | flops 3623878656 | bytes 14000000 | tf_op jit(solution)/shard_map/project/pallas_call | solution.py:185
  46.5 16.8 %attend.1 = (bf16[1024,768]{1,0:T(8,128)(2,1)}, f32[6,4,512]{2,1,0:T(4,128)}) custom-call(bf16[1024,768]{1,0:T(8,128)(2,1)} %get-tuple-element.52.ql.qs, bf16[1024,768]{1,0:T(8,128)(2,1)} %get-tuple-element.52.ql.qs, bf16[512,1536]{1,0:T(8,128)(2,1)} %get-tuple-element.53.ko.vo, bf16[512,1536]{1,0:T(8,128)(2,1)} %get-tuple-element.53.ko.vo, ...), custom_call_target="tpu_custom_call" | custom-call | flops 7247757312 | bytes 9000000 | tf_op jit(solution)/shard_map/attend/pallas_call | solution.py:266
  63.3 37.1 %feed.1 = (bf16[1024,768]{1,0:T(8,128)(2,1)}, f32[1024,768]{1,0:T(8,128)}, bf16[1024,768]{1,0:T(8,128)(2,1)}, bf16[1024,3072]{1,0:T(8,128)(2,1)}, bf16[1024,768]...) custom-call(s32[3]{0:T(128)} %pad_add_fusion.order.place, ...), custom_call_target="tpu_custom_call" | custom-call | flops 21743271936 | bytes 40000000 | tf_op jit(solution)/shard_map/feed/pallas_call | solution.py:466
  100.5 5.7 %weight_out.1 = (bf16[768,384]{1,0:T(8,128)(2,1)}, bf16[768,384]{1,0:T(8,128)(2,1)}) custom-call(s32[3]{0:T(128)} %pad_add_fusion.order.place, bf16[1024,768]{1,0:T(8,128)(2,1)} %get-tuple-element.55.att_ref.left_ref, bf16[1024,768]{1,0:T(8,128)(2,1)} %get-tuple-element.78.right_ref), custom_call_target="tpu_custom_call" | custom-call | flops 1207959552 | bytes 4325376 | tf_op jit(solution)/shard_map/weight_out/pallas_call | solution.py:534
  107.0 28.9 %attend_back.1 = (bf16[1024,768]{1,0:T(8,128)(2,1)}, f32[512,768]{1,0:T(8,128)}, f32[512,768]{1,0:T(8,128)}, bf16[512,768]{1,0:T(8,128)(2,1)}, bf16[512,768]{1,0...) custom-call(s32[3]{0:T(128)} %pad_add_fusion.order.place, bf16[1024,768]{1,0:T(8,128)(2,1)} %get-tuple-element.52.ql.qs, ...), custom_call_target="tpu_custom_call" | custom-call | flops 18119393280 | bytes 16000000 | tf_op jit(solution)/shard_map/attend_back/pallas_call | solution.py:337
  141.4 14.3 %weight_down.1 = (bf16[3072,384]{1,0:T(8,128)(2,1)}, bf16[3072,384]{1,0:T(8,128)(2,1)}) custom-call(s32[3]{0:T(128)} %pad_add_fusion.order.place, bf16[1024,3072]{1,0:T(8,128)(2,1)} %get-tuple-element.85.left_ref, bf16[1024,768]{1,0:T(8,128)(2,1)} %get-tuple-element.86.right_ref), custom_call_target="tpu_custom_call" | custom-call | flops 4831838208 | bytes 12582912 | tf_op jit(solution)/shard_map/weight_down/pallas_call | solution.py:534
  158.7 12.1 %weight_up.1 = (bf16[768,1536]{1,0:T(8,128)(2,1)}, bf16[768,1536]{1,0:T(8,128)(2,1)}) custom-call(s32[3]{0:T(128)} %pad_add_fusion.order.place, bf16[1024,768]{1,0:T(8,128)(2,1)} %get-tuple-element.81.left_ref, bf16[1024,3072]{1,0:T(8,128)(2,1)} %get-tuple-element.82.right_ref), custom_call_target="tpu_custom_call" | custom-call | flops 4831838208 | bytes 12582912 | tf_op jit(solution)/shard_map/weight_up/pallas_call | solution.py:534
  181.2 7.4 %join.1.dqkv_ref.right_ref = bf16[1024,2304]{1,0:T(8,128)(2,1)} custom-call(s32[3]{0:T(128)} %pad_add_fusion.order.place, bf16[1024,768]{1,0:T(8,128)(2,1)} %get-tuple-element.59.dq_ref, f32[512,768]{1,0:T(8,128)} %get-tuple-element.60.dk_ref, f32[512,768]{1,0:T(8,128)} %get-tuple-element.61.dv_ref, bf16[512,768]{1,0:T(8,128)(2,1)} %collective-permute-done.2.ek_ref, ...), custom_call_target="tpu_custom_call" | custom-call | flops 10000000 | bytes 12000000 | tf_op jit(solution)/shard_map/join/pallas_call | solution.py:638
  188.6 11.0 %last.1 = (f32[1024,768]{1,0:T(8,128)}, f32[2,8,768]{2,1,0:T(8,128)}, f32[1,768]{1,0:T(1,128)}) custom-call(s32[3]{0:T(128)} %pad_add_fusion.order.place, bf16[1024,768]{1,0:T(8,128)(2,1)} %bitcast.160, bf16[1024,2304]{1,0:T(8,128)(2,1)} %join.1.dqkv_ref.right_ref, f32[1024,768]{1,0:T(8,128)} %get-tuple-element.66.dmid_ref, f32[8,4608]{1,0:T(8,128)} %copy-done.2, ...), custom_call_target="tpu_custom_call" | custom-call | flops 3623878656 | bytes 18000000 | tf_op jit(solution)/shard_map/last/pallas_call | solution.py:691
  201.2 41.8 %all-gather.2 = f32[32,1,3840]{2,1,0:T(1,128)S(1)} all-gather(f32[1,1,3840]{2,1,0:T(1,128)S(1)} %reshape.134), channel_id=2, replica_groups=mesh['seq'=16,'span'=2] {'seq','span'}, dimensions={0}, use_global_device_ids=true | all-gather | bytes 506880 | tf_op jit(solution)/shard_map/all_gather | solution.py:730
  244.9 10.2 %weight_qkv.1 = (bf16[768,1152]{1,0:T(8,128)(2,1)}, bf16[768,1152]{1,0:T(8,128)(2,1)}) custom-call(s32[3]{0:T(128)} %pad_add_fusion.order.place, bf16[1024,768]{1,0:T(8,128)(2,1)} %get-tuple-element.75.left_ref, bf16[1024,2304]{1,0:T(8,128)(2,1)} %join.1.dqkv_ref.right_ref), custom_call_target="tpu_custom_call" | custom-call | flops 3623878656 | bytes 9830400 | tf_op jit(solution)/shard_map/weight_qkv/pallas_call | solution.py:534
  257.0 3.9 %collective-permute-start.20 = (bf16[48,384]{1,0:T(8,128)(2,1)S(1)}, bf16[48,384]{1,0:T(8,128)(2,1)S(1)}, u32[]{:S(2)}, u32[]{:S(2)}) collective-permute-start(bf16[48,384]{1,0:T(8,128)(2,1)S(1)} %get-tuple-element.110), channel_id=1, source_target_pairs={{0,24},{2,26},{4,28},{6,30},{8,0},{10,2},{12,4},{14,6},{16,8},{18,... | collective-permute-start | bytes 110600 | tf_op jit(solution)/shard_map/ppermute | solution.py:584
  264.0 2.8 convert_add_fusion
  281.0 5.7 %reduce.5 = f32[32,10752]{1,0:T(8,128)} reduce(f32[32,1,10752]{2,1,0:T(1,128)} %all-gather.6.cloned.1.call-done, f32[]{:T(128)} %constant.268), dimensions={1}, to_apply=%all-gather.3.reduce_sub_computation | reduce | bytes 2752516 | tf_op jit(solution)/shard_map/all_gather | solution.py:730
  286.7 3.3 reshape.127
  291.8 2.6 slice_reduce_fusion
  322.5 13.8 %collective-permute-done.9 = bf16[2,48,1152]{2,1,0:T(8,128)(2,1)S(1)} collective-permute-done((bf16[2,48,1152]{2,1,0:T(8,128)(2,1)S(1)}, bf16[2,48,1152]{2,1,0:T(8,128)(2,1)S(1)}, u32[]{:S(2)}, u32[]{:S(2)}) %collective-permute-start.9) | collective-permute-done | bytes 221216 | tf_op jit(solution)/shard_map/ppermute | solution.py:578
  337.9 4.3 %collective-permute-done.7 = bf16[2,48,1152]{2,1,0:T(8,128)(2,1)S(1)} collective-permute-done((bf16[2,48,1152]{2,1,0:T(8,128)(2,1)S(1)}, bf16[2,48,1152]{2,1,0:T(8,128)(2,1)S(1)}, u32[]{:S(2)}, u32[]{:S(2)}) %collective-permute-start.7) | collective-permute-done | bytes 221216 | tf_op jit(solution)/shard_map/ppermute | solution.py:577
  352.0 4.4 %collective-permute-done.11 = bf16[48,1152]{1,0:T(8,128)(2,1)S(1)} collective-permute-done((bf16[48,1152]{1,0:T(8,128)(2,1)S(1)}, bf16[48,1152]{1,0:T(8,128)(2,1)S(1)}, u32[]{:S(2)}, u32[]{:S(2)}) %collective-permute-start.11) | collective-permute-done | bytes 110624 | tf_op jit(solution)/shard_map/ppermute | solution.py:584
  356.4 7.5 %collective-permute-start.27 = (bf16[48,1536]{1,0:T(8,128)(2,1)S(1)}, bf16[48,1536]{1,0:T(8,128)(2,1)S(1)}, u32[]{:S(2)}, u32[]{:S(2)}) collective-permute-start(bf16[48,1536]{1,0:T(8,128)(2,1)S(1)} %get-tuple-element.99), channel_id=1, source_target_pairs={{0,16},{2,18},{4,20},{6,22},{8,24},{10,26},{12,28},{14,30},{16,0},... | collective-permute-start | bytes 442376 | tf_op jit(solution)/shard_map/ppermute | solution.py:584
  364.7 3.4 collective-permute-start.28
  368.1 2.6 collective-permute-done.35
  371.5 4.8 %collective-permute-done.27 = bf16[48,1536]{1,0:T(8,128)(2,1)S(1)} collective-permute-done((bf16[48,1536]{1,0:T(8,128)(2,1)S(1)}, bf16[48,1536]{1,0:T(8,128)(2,1)S(1)}, u32[]{:S(2)}, u32[]{:S(2)}) %collective-permute-start.27) | collective-permute-done | bytes 147488 | tf_op jit(solution)/shard_map/ppermute | solution.py:584
  (221 shorter events, 102.4 us)
Async XLA Ops:
  7.2 273.8 %all-gather.6.cloned.1.call-start = ((), (), s32[]{:S(2)}) async-start(), calls=%async_computation | async-start | bytes 1419264 | tf_op jit(solution)/shard_map/all_gather | solution.py:730
  107.0 49.1 %collective-permute-start.13 = (bf16[768,384]{1,0:T(8,128)(2,1)}, bf16[768,384]{1,0:T(8,128)(2,1)S(1)}, u32[]{:S(2)}, u32[]{:S(2)}) collective-permute-start(bf16[768,384]{1,0:T(8,128)(2,1)} %get-tuple-element.80), channel_id=1, source_target_pairs={{0,1},{1,0},{2,3},{3,2},{4,5},{5,4},{6,7},{7,6},{8,9},{9,8},{10,11... | collective-permute-start | bytes 1769480 | tf_op jit(solution)/shard_map/ppermute | solution.py:564
  138.0 39.1 %collective-permute-start.4 = (f32[128,1536]{1,0:T(8,128)S(1)}, f32[128,1536]{1,0:T(8,128)}, u32[]{:S(2)}, u32[]{:S(2)}) collective-permute-start(f32[128,1536]{1,0:T(8,128)S(1)} %constant_dynamic-update-slice_fusion), channel_id=1, source_target_pairs={{1,0},{3,2},{5,4},{7,6},{9,8},{11,10},{13,12},{15,14},{17,16},{19,... | collective-permute-start | bytes 2359304 | tf_op jit(solution)/shard_map/ppermute | solution.py:785
  139.3 41.4 %collective-permute-start.2 = (bf16[512,768]{1,0:T(8,128)(2,1)}, bf16[512,768]{1,0:T(8,128)(2,1)}, u32[]{:S(2)}, u32[]{:S(2)}) collective-permute-start(bf16[512,768]{1,0:T(8,128)(2,1)} %get-tuple-element.62), channel_id=1, source_target_pairs={{0,1},{1,0},{2,3},{3,2},{4,5},{5,4},{6,7},{7,6},{8,9},{9,8},{10,11... | collective-permute-start | bytes 2359304 | tf_op jit(solution)/shard_map/ppermute | solution.py:780
  141.4 39.8 %collective-permute-start.3 = (bf16[512,768]{1,0:T(8,128)(2,1)}, bf16[512,768]{1,0:T(8,128)(2,1)}, u32[]{:S(2)}, u32[]{:S(2)}) collective-permute-start(bf16[512,768]{1,0:T(8,128)(2,1)} %get-tuple-element.63), channel_id=1, source_target_pairs={{0,1},{1,0},{2,3},{3,2},{4,5},{5,4},{6,7},{7,6},{8,9},{9,8},{10,11... | collective-permute-start | bytes 2359304 | tf_op jit(solution)/shard_map/ppermute | solution.py:780
  155.7 108.3 %collective-permute-start.29 = (bf16[3072,384]{1,0:T(8,128)(2,1)}, bf16[3072,384]{1,0:T(8,128)(2,1)}, u32[]{:S(2)}, u32[]{:S(2)}) collective-permute-start(bf16[3072,384]{1,0:T(8,128)(2,1)} %get-tuple-element.88), channel_id=1, source_target_pairs={{0,1},{1,0},{2,3},{3,2},{4,5},{5,4},{6,7},{7,6},{8,9},{9,8},{10,11... | collective-permute-start | bytes 7077896 | tf_op jit(solution)/shard_map/ppermute | solution.py:564
  176.4 92.6 %collective-permute-start.21 = (bf16[768,1536]{1,0:T(8,128)(2,1)}, bf16[768,1536]{1,0:T(8,128)(2,1)}, u32[]{:S(2)}, u32[]{:S(2)}) collective-permute-start(bf16[768,1536]{1,0:T(8,128)(2,1)} %get-tuple-element.84), channel_id=1, source_target_pairs={{0,1},{1,0},{2,3},{3,2},{4,5},{5,4},{6,7},{7,6},{8,9},{9,8},{10,11... | collective-permute-start | bytes 7077896 | tf_op jit(solution)/shard_map/ppermute | solution.py:564
  177.1 78.7 %collective-permute-start.17 = (bf16[2,48,384]{2,1,0:T(8,128)(2,1)}, bf16[2,48,384]{2,1,0:T(8,128)(2,1)}, u32[]{:S(2)}, u32[]{:S(2)}) collective-permute-start(bf16[2,48,384]{2,1,0:T(8,128)(2,1)} %fusion.59), channel_id=1, source_target_pairs={{0,2},{2,0},{4,6},{6,4},{8,10},{10,8},{12,14},{14,12},{16,18},{18,... | collective-permute-start | bytes 221192 | tf_op jit(solution)/shard_map/ppermute | solution.py:578
  180.7 76.0 %collective-permute-start.15 = (bf16[2,48,384]{2,1,0:T(8,128)(2,1)}, bf16[2,48,384]{2,1,0:T(8,128)(2,1)S(1)}, u32[]{:S(2)}, u32[]{:S(2)}) collective-permute-start(bf16[2,48,384]{2,1,0:T(8,128)(2,1)} %fusion.58), channel_id=1, source_target_pairs={{0,4},{2,6},{4,0},{6,2},{8,12},{10,14},{12,8},{14,10},{16,20},{18,... | collective-permute-start | bytes 221192 | tf_op jit(solution)/shard_map/ppermute | solution.py:577
  268.1 39.4 %collective-permute-start.32 = (bf16[2,2,192,384]{3,2,0,1:T(8,128)(2,1)}, bf16[2,2,192,384]{3,2,0,1:T(8,128)(2,1)}, u32[]{:S(2)}, u32[]{:S(2)}) collective-permute-start(bf16[2,2,192,384]{3,2,0,1:T(8,128)(2,1)} %fusion.3), channel_id=1, source_target_pairs={{0,4},{2,6},{4,0},{6,2},{8,12},{10,14},{12,8},{14,10},{16,20},{18,... | collective-permute-start | bytes 1769480 | tf_op jit(solution)/shard_map/ppermute | solution.py:574
  269.0 41.9 %collective-permute-start.30 = (bf16[2,2,192,384]{3,2,0,1:T(8,128)(2,1)}, bf16[2,2,192,384]{3,2,0,1:T(8,128)(2,1)}, u32[]{:S(2)}, u32[]{:S(2)}) collective-permute-start(bf16[2,2,192,384]{3,2,0,1:T(8,128)(2,1)} %fusion.2), channel_id=1, source_target_pairs={{0,2},{2,0},{4,6},{6,4},{8,10},{10,8},{12,14},{14,12},{16,18},{18,... | collective-permute-start | bytes 1769480 | tf_op jit(solution)/shard_map/ppermute | solution.py:573
  274.2 38.6 %collective-permute-start.24 = (bf16[2,2,48,1536]{3,2,0,1:T(8,128)(2,1)}, bf16[2,2,48,1536]{3,2,0,1:T(8,128)(2,1)}, u32[]{:S(2)}, u32[]{:S(2)}) collective-permute-start(bf16[2,2,48,1536]{3,2,0,1:T(8,128)(2,1)} %fusion.1), channel_id=1, source_target_pairs={{0,4},{2,6},{4,0},{6,2},{8,12},{10,14},{12,8},{14,10},{16,20},{18,... | collective-permute-start | bytes 1769480 | tf_op jit(solution)/shard_map/ppermute | solution.py:574
  275.5 40.4 %collective-permute-start.22 = (bf16[2,2,48,1536]{3,2,0,1:T(8,128)(2,1)}, bf16[2,2,48,1536]{3,2,0,1:T(8,128)(2,1)}, u32[]{:S(2)}, u32[]{:S(2)}) collective-permute-start(bf16[2,2,48,1536]{3,2,0,1:T(8,128)(2,1)} %fusion), channel_id=1, source_target_pairs={{0,2},{2,0},{4,6},{6,4},{8,10},{10,8},{12,14},{14,12},{16,18},{18,... | collective-permute-start | bytes 1769480 | tf_op jit(solution)/shard_map/ppermute | solution.py:573
  280.2 37.5 %collective-permute-start.8 = (bf16[2,2,48,1152]{3,2,0,1:T(8,128)(2,1)}, bf16[2,2,48,1152]{3,2,0,1:T(8,128)(2,1)}, u32[]{:S(2)}, u32[]{:S(2)}) collective-permute-start(bf16[2,2,48,1152]{3,2,0,1:T(8,128)(2,1)} %fusion.5), channel_id=1, source_target_pairs={{0,4},{2,6},{4,0},{6,2},{8,12},{10,14},{12,8},{14,10},{16,20},{18,... | collective-permute-start | bytes 1327112 | tf_op jit(solution)/shard_map/ppermute | solution.py:574
  310.9 32.3 %collective-permute-start.33 = (bf16[2,192,384]{2,1,0:T(8,128)(2,1)S(1)}, bf16[2,192,384]{2,1,0:T(8,128)(2,1)S(1)}, u32[]{:S(2)}, u32[]{:S(2)}) collective-permute-start(bf16[2,192,384]{2,1,0:T(8,128)(2,1)S(1)} %fusion.9), channel_id=1, source_target_pairs={{0,2},{2,0},{4,6},{6,4},{8,10},{10,8},{12,14},{14,12},{16,18},{18,... | collective-permute-start | bytes 884744 | tf_op jit(solution)/shard_map/ppermute | solution.py:578
  312.8 32.3 %collective-permute-start.31 = (bf16[2,192,384]{2,1,0:T(8,128)(2,1)S(1)}, bf16[2,192,384]{2,1,0:T(8,128)(2,1)S(1)}, u32[]{:S(2)}, u32[]{:S(2)}) collective-permute-start(bf16[2,192,384]{2,1,0:T(8,128)(2,1)S(1)} %fusion.8), channel_id=1, source_target_pairs={{0,4},{2,6},{4,0},{6,2},{8,12},{10,14},{12,8},{14,10},{16,20},{18,... | collective-permute-start | bytes 884744 | tf_op jit(solution)/shard_map/ppermute | solution.py:577
  316.0 30.6 %collective-permute-start.25 = (bf16[2,48,1536]{2,1,0:T(8,128)(2,1)S(1)}, bf16[2,48,1536]{2,1,0:T(8,128)(2,1)S(1)}, u32[]{:S(2)}, u32[]{:S(2)}) collective-permute-start(bf16[2,48,1536]{2,1,0:T(8,128)(2,1)S(1)} %fusion.7), channel_id=1, source_target_pairs={{0,2},{2,0},{4,6},{6,4},{8,10},{10,8},{12,14},{14,12},{16,18},{18,... | collective-permute-start | bytes 884744 | tf_op jit(solution)/shard_map/ppermute | solution.py:578
  317.7 29.8 %collective-permute-start.23 = (bf16[2,48,1536]{2,1,0:T(8,128)(2,1)S(1)}, bf16[2,48,1536]{2,1,0:T(8,128)(2,1)S(1)}, u32[]{:S(2)}, u32[]{:S(2)}) collective-permute-start(bf16[2,48,1536]{2,1,0:T(8,128)(2,1)S(1)} %fusion.6), channel_id=1, source_target_pairs={{0,4},{2,6},{4,0},{6,2},{8,12},{10,14},{12,8},{14,10},{16,20},{18,... | collective-permute-start | bytes 884744 | tf_op jit(solution)/shard_map/ppermute | solution.py:577
  320.7 15.5 %collective-permute-start.9 = (bf16[2,48,1152]{2,1,0:T(8,128)(2,1)S(1)}, bf16[2,48,1152]{2,1,0:T(8,128)(2,1)S(1)}, u32[]{:S(2)}, u32[]{:S(2)}) collective-permute-start(bf16[2,48,1152]{2,1,0:T(8,128)(2,1)S(1)} %fusion.35), channel_id=1, source_target_pairs={{0,2},{2,0},{4,6},{6,4},{8,10},{10,8},{12,14},{14,12},{16,18},{18,... | collective-permute-start | bytes 663560 | tf_op jit(solution)/shard_map/ppermute | solution.py:578
  346.6 18.1 %collective-permute-start.34 = (bf16[192,384]{1,0:T(8,128)(2,1)S(1)}, bf16[192,384]{1,0:T(8,128)(2,1)S(1)}, u32[]{:S(2)}, u32[]{:S(2)}) collective-permute-start(bf16[192,384]{1,0:T(8,128)(2,1)S(1)} %get-tuple-element.95), channel_id=1, source_target_pairs={{0,8},{2,10},{4,12},{6,14},{8,16},{10,18},{12,20},{14,22},{16,24},... | collective-permute-start | bytes 442376 | tf_op jit(solution)/shard_map/ppermute | solution.py:584
  347.6 23.1 %collective-permute-start.35 = (bf16[192,384]{1,0:T(8,128)(2,1)S(1)}, bf16[192,384]{1,0:T(8,128)(2,1)S(1)}, u32[]{:S(2)}, u32[]{:S(2)}) collective-permute-start(bf16[192,384]{1,0:T(8,128)(2,1)S(1)} %get-tuple-element.96), channel_id=1, source_target_pairs={{0,16},{2,18},{4,20},{6,22},{8,24},{10,26},{12,28},{14,30},{16,0},... | collective-permute-start | bytes 442376 | tf_op jit(solution)/shard_map/ppermute | solution.py:584
  350.4 20.3 %collective-permute-start.36 = (bf16[192,384]{1,0:T(8,128)(2,1)S(1)}, bf16[192,384]{1,0:T(8,128)(2,1)S(1)}, u32[]{:S(2)}, u32[]{:S(2)}) collective-permute-start(bf16[192,384]{1,0:T(8,128)(2,1)S(1)} %get-tuple-element.97), channel_id=1, source_target_pairs={{0,24},{2,26},{4,28},{6,30},{8,0},{10,2},{12,4},{14,6},{16,8},{18,... | collective-permute-start | bytes 442376 | tf_op jit(solution)/shard_map/ppermute | solution.py:584
  356.4 15.1 %collective-permute-start.26 = (bf16[48,1536]{1,0:T(8,128)(2,1)S(1)}, bf16[48,1536]{1,0:T(8,128)(2,1)S(1)}, u32[]{:S(2)}, u32[]{:S(2)}) collective-permute-start(bf16[48,1536]{1,0:T(8,128)(2,1)S(1)} %get-tuple-element.98), channel_id=1, source_target_pairs={{0,8},{2,10},{4,12},{6,14},{8,16},{10,18},{12,20},{14,22},{16,24},... | collective-permute-start | bytes 442376 | tf_op jit(solution)/shard_map/ppermute | solution.py:584
  356.4 19.9 %collective-permute-start.27 = (bf16[48,1536]{1,0:T(8,128)(2,1)S(1)}, bf16[48,1536]{1,0:T(8,128)(2,1)S(1)}, u32[]{:S(2)}, u32[]{:S(2)}) collective-permute-start(bf16[48,1536]{1,0:T(8,128)(2,1)S(1)} %get-tuple-element.99), channel_id=1, source_target_pairs={{0,16},{2,18},{4,20},{6,22},{8,24},{10,26},{12,28},{14,30},{16,0},... | collective-permute-start | bytes 442376 | tf_op jit(solution)/shard_map/ppermute | solution.py:584
  (41 other events, 296.5 us)
Sparse Core Ops, SparseCore 0:
  107.1 55.4 all-gather.5

commit v2 on v1

--- a/solution.py
+++ b/solution.py
@@ -89,7 +89,9 @@
     return jnp.where(lane < HEAD, x, zero), jnp.where(lane < HEAD, zero, x)
 
 
-def modulation_kernel(n, own_ref, weight_ref, bias_ref, mod_ref, table_ref, send, recv, local):
+def modulation_kernel(
+    n, own_ref, weight_ref, bias_ref, mod_ref, table_ref, silu_ref, send, recv, local
+):
     me = lax.axis_index("seq")
     barrier = pltpu.get_barrier_semaphore()
     for step in range(1, n):
@@ -125,6 +127,13 @@
     cond = jnp.concatenate(rows + [jnp.zeros((8 - SLOTS, 128), F32)], axis=0)
     silu = (cond / (1.0 + jnp.exp(-cond))).astype(BF16)
     mod_ref[...] = nn(silu, weight_ref[...]) + bias_ref[...].astype(F32)
+    for slot in range(SLOTS):
+        wanted = table_ref[:, SLOTS + slot, :]
+        rows = jnp.zeros((n, 128), F32)
+        for k in range(SLOTS * n):
+            row = table_ref[k // SLOTS, k % SLOTS : k % SLOTS + 1, :]
+            rows += jnp.where(wanted == k, row, 0.0)
+        silu_ref[slot] = (rows / (1.0 + jnp.exp(-rows))).astype(BF16).astype(F32)
 
 
 def modulation_call(own, ada_weight, ada_bias, n):
@@ -135,9 +144,10 @@
         out_shape=(
             jax.ShapeDtypeStruct((8, 6 * D), F32),
             jax.ShapeDtypeStruct((n, 8, 128), F32),
+            jax.ShapeDtypeStruct((SLOTS, n, 128), F32),
         ),
         in_specs=[vmem] * 3,
-        out_specs=(vmem, vmem),
+        out_specs=(vmem, vmem, vmem),
         scratch_shapes=[
             pltpu.SemaphoreType.DMA((n,)),
             pltpu.SemaphoreType.DMA((n,)),
@@ -152,9 +162,10 @@
 
 def project_kernel(
     order, tok_ref, mod_ref, gain_ref, weight_ref, cos_ref, sin_ref,
-    q_ref, h_ref, kvl_ref, kvs_ref,
+    q_ref, h_ref, kvl_ref, kvs_ref, sorted_ref,
 ):
     j = pl.program_id(0)
+    sorted_ref[...] = tok_ref[...]
     row = mod_ref[pl.ds(order[j], 1), :]
     shift, scale = row[:, :D], row[:, D : 2 * D]
     x = tok_ref[...].astype(F32)
@@ -190,6 +201,7 @@
             jax.ShapeDtypeStruct((SLOTS * rows, D), BF16),
             jax.ShapeDtypeStruct((rows, 2 * D), BF16),
             jax.ShapeDtypeStruct((rows, 2 * D), BF16),
+            jax.ShapeDtypeStruct((SLOTS * rows, D), BF16),
         ),
         grid_spec=pltpu.PrefetchScalarGridSpec(
             num_scalar_prefetch=1,
@@ -207,6 +219,7 @@
                 pl.BlockSpec((tile, D), lambda j, t, o: (j * tiles + t, 0)),
                 pl.BlockSpec((tile, 2 * D), lambda j, t, o: (t + j * (tiles - 1 - t), 0)),
                 pl.BlockSpec((tile, 2 * D), lambda j, t, o: (j * t, 0)),
+                pl.BlockSpec((tile, D), lambda j, t, o: (j * tiles + t, 0)),
             ],
         ),
         compiler_params=pltpu.CompilerParams(vmem_limit_bytes=BIG),
@@ -375,6 +388,12 @@
     )
 
 
+def part_of(index, size):
+    if isinstance(index, int):
+        return pl.ds(index * size, size)
+    return pl.ds(pl.multiple_of(index * size, size), size)
+
+
 def add_to(ref, value, first):
     @pl.when(first)
     def _():
@@ -386,7 +405,7 @@
 
 
 def feed_kernel(
-    order, tok_ref, att_ref, cot_ref, mod_ref, gain_ref, wo_ref, wu_ref, bu_ref, wd_ref, bd_ref,
+    halves, order, tok_ref, att_ref, cot_ref, mod_ref, gain_ref, wo_ref, wu_ref, bu_ref, wd_ref, bd_ref,
     out_ref, dmid_ref, datt_ref, act_ref, dlow_ref, h_ref, dup_ref, dattn_ref,
     dmod_ref, dgain_ref, dbd_ref, dbu_ref,
 ):
@@ -404,7 +423,9 @@
     h_ref[...] = hidden
     dy = cot_ref[...].astype(F32)
     d_low = (gate2 * dy).astype(BF16)
-    dlow_ref[...] = d_low
+    at = [h * order[2] + (1 - h) * (1 - order[2]) if halves else h for h in range(2)]
+    for h in range(2):
+        dlow_ref[:, part_of(at[h], D // 2)] = d_low[:, h * (D // 2) : (h + 1) * (D // 2)]
     lowered, d_hidden = None, None
     sums = []
     for f in range(0, FF, CHUNK):
@@ -420,7 +441,8 @@
         )
         d_up = (d_act * slope).astype(BF16)
         act_ref[:, cols] = act
-        dup_ref[:, cols] = d_up
+        place = at[f // (FF // 2)] * (FF // 2) + f % (FF // 2)
+        dup_ref[:, pl.ds(pl.multiple_of(place, CHUNK) if halves else place, CHUNK)] = d_up
         sums.append(col_sum(d_up.astype(F32)))
         low = nn(act, wd_ref[cols, :])
         dh = nt(d_up, wu_ref[:, cols])
@@ -437,7 +459,8 @@
     dmid_ref[...] = d_mid
     d_gate1 = col_sum(d_mid * attention)
     d_attention = (gate1 * d_mid).astype(BF16)
-    dattn_ref[...] = d_attention
+    for h in range(2):
+        dattn_ref[:, part_of(at[h], D // 2)] = d_attention[:, h * (D // 2) : (h + 1) * (D // 2)]
     datt_ref[...] = nt(d_attention, wo_ref[...]).astype(BF16)
     first = jnp.logical_and(j == 0, t == 0)
     add_to(
@@ -452,7 +475,7 @@
     add_to(dbu_ref, jnp.concatenate(sums, axis=1), first)
 
 
-def feed_call(place, tokens, att, cot, mod, gain, wo, wu, bu, wd, bd, rows):
+def feed_call(halves, place, tokens, att, cot, mod, gain, wo, wu, bu, wd, bd, rows):
     tile = min(256, rows)
     tiles = rows // tile
 
@@ -464,7 +487,7 @@
 
     n = SLOTS * rows
     return pl.pallas_call(
-        feed_kernel,
+        partial(feed_kernel, halves),
         name="feed",
         out_shape=(
             jax.ShapeDtypeStruct((n, D), BF16),
@@ -540,7 +563,7 @@
             grid=(2, tiles),
             in_specs=[
                 pl.BlockSpec((n, tile), lambda c, m, o: (0, m)),
-                pl.BlockSpec((n, half), lambda c, m, o: (0, c * o[2] + (1 - c) * (1 - o[2]))),
+                pl.BlockSpec((n, half), lambda c, m, o: (0, c)),
             ],
             out_specs=[
                 pl.BlockSpec((tile, half), lambda c, m, o: (m + c * (tiles - 1 - m), 0)),
@@ -552,48 +575,8 @@
     )(place, left, right)
 
 
-def flip(index, bit):
-    return index + bit - 2 * bit * ((index // bit) % 2)
-
-
-def reduce_tiles(other, mine):
-    s = lax.axis_index("seq")
-    x, y, z = s % 2, (s // 2) % 2, s // 4
-    rows, cols = mine.shape
-    part = rows // 16
-    came = lax.ppermute(other, "span", [(0, 1), (1, 0)])
-    pair = (mine.astype(F32) + came.astype(F32)).reshape(2, 2, 2, 2, part, cols)
-    along_x = [(i, flip(i, 1)) for i in range(16)]
-    along_y = [(i, flip(i, 2)) for i in range(16)]
-
-    def pick(array, axis, index):
-        return lax.dynamic_index_in_dim(array, index, axis, keepdims=False)
-
-    first, second = pair[0], pair[1]
-    sent_a = lax.ppermute(pick(first, 2, 1 - x).astype(BF16), "seq", along_x)
-    sent_b = lax.ppermute(pick(second, 1, 1 - y).astype(BF16), "seq", along_y)
-    first = pick(first, 2, x) + sent_a.astype(F32)
-    second = pick(second, 1, y) + sent_b.astype(F32)
-    sent_a = lax.ppermute(pick(first, 1, 1 - y).astype(BF16), "seq", along_y)
-    sent_b = lax.ppermute(pick(second, 1, 1 - x).astype(BF16), "seq", along_x)
-    first = pick(first, 1, y) + sent_a.astype(F32)
-    second = pick(second, 1, x) + sent_b.astype(F32)
-    quarter = jnp.concatenate([first, second], axis=0)
-    total = pick(quarter, 0, z)
-    for step in range(1, 4):
-        came = lax.ppermute(
-            pick(quarter, 0, (z + step) % 4).astype(BF16),
-            "seq",
-            [(i, (i + 4 * step) % 16) for i in range(16)],
-        )
-        total = total + came.astype(F32)
-    return total
-
-
-def weight_gradient(place, left, right, tile, name):
+def weight_gradient(left, right):
     seq, span = lax.axis_size("seq"), lax.axis_size("span")
-    if seq == 16 and span == 2:
-        return reduce_tiles(*weight_call(place, left, right, tile, name))
     grad = tn(left, right)
     rows, cols = grad.shape
     shaped = grad.reshape(seq, rows // seq, span, cols // span).transpose(0, 2, 1, 3)
@@ -718,6 +701,755 @@
     )(place, tokens, dqkv, dmid, mod, gain, weight)
 
 
+def flip(index, bit):
+    return index + bit - 2 * bit * ((index // bit) % 2)
+
+
+def add_low(a, b):
+    return (a.astype(F32) + b.astype(F32)).astype(BF16)
+
+
+def plane_peers():
+    s, c = lax.axis_index("seq"), lax.axis_index("span")
+    return [{"span": 1 - c}, {"seq": flip(s, 1)}, {"seq": flip(s, 2)}]
+
+
+def line_peers():
+    s = lax.axis_index("seq")
+    return [{"seq": lax.rem(s + 4 * step, 16)} for step in range(1, 4)]
+
+
+def greet(peers):
+    barrier = pltpu.get_barrier_semaphore()
+    for peer in peers:
+        pl.semaphore_signal(barrier, inc=1, device_id=peer, device_id_type=MESH)
+    pl.semaphore_wait(barrier, len(peers))
+
+
+class Scatter:
+    def __init__(self, send, recv, base, other=None, own=None, came0=None, a1=None, b1=None,
+                 came2=None, came3=None):
+        self.send, self.recv, self.base = send, recv, base
+        self.other, self.own, self.came0 = other, own, came0
+        self.a1, self.b1, self.came2, self.came3 = a1, b1, came2, came3
+        s = lax.axis_index("seq")
+        self.x, self.y, self.z = lax.rem(s, 2), lax.rem(s // 2, 2), s // 4
+        self.core_peer, self.x_peer, self.y_peer = plane_peers()
+        self.z_peers = line_peers()
+
+    def copy(self, i):
+        x, y, z = self.x, self.y, self.z
+        if i == 0:
+            src, dst, peer = self.other, self.came0, self.core_peer
+        elif i == 1:
+            src, dst, peer = self.own.at[0:2, :, 1 - x], self.a1, self.x_peer
+        elif i == 2:
+            src, dst, peer = self.own.at[2:4, 1 - y], self.b1, self.y_peer
+        elif i == 3:
+            src, dst, peer = self.a1.at[:, 1 - y], self.came2.at[0:2], self.y_peer
+        elif i == 4:
+            src, dst, peer = self.b1.at[:, 1 - x], self.came2.at[2:4], self.x_peer
+        else:
+            step = i - 4
+            src, dst = self.came2.at[lax.rem(z + step, 4)], self.came3.at[step - 1]
+            peer = self.z_peers[step - 1]
+        return pltpu.make_async_remote_copy(
+            src_ref=src,
+            dst_ref=dst,
+            send_sem=self.send.at[self.base + i],
+            recv_sem=self.recv.at[self.base + i],
+            device_id=peer,
+            device_id_type=MESH,
+        )
+
+    def start(self, *which):
+        for i in which:
+            self.copy(i).start()
+
+    def arrive(self, *which):
+        for i in which:
+            self.copy(i).wait_recv()
+
+    def drain(self, *which):
+        for i in which:
+            self.copy(i).wait_send()
+
+    def add0(self):
+        self.arrive(0)
+
+        def body(i, _):
+            z, y, x = i // 4, lax.rem(i // 2, 2), lax.rem(i, 2)
+            self.own[z, y, x] = add_low(self.own[z, y, x], self.came0[z, y, x])
+            return 0
+
+        lax.fori_loop(0, 16, body, 0)
+
+    def add1(self, a_ref, b_ref):
+        self.arrive(1, 2)
+
+        def body(i, _):
+            z, k = i // 2, lax.rem(i, 2)
+            a_ref[z, k] = add_low(self.own[z, k, self.x], self.a1[z, k])
+            b_ref[z, k] = add_low(self.own[2 + z, self.y, k], self.b1[z, k])
+            return 0
+
+        lax.fori_loop(0, 4, body, 0)
+
+    def add2(self, out_ref):
+        self.arrive(3, 4)
+
+        def body(z, _):
+            out_ref[z] = add_low(self.a1[z, self.y], self.came2[z])
+            out_ref[2 + z] = add_low(self.b1[z, self.x], self.came2[2 + z])
+            return 0
+
+        lax.fori_loop(0, 2, body, 0)
+
+    def total(self):
+        self.arrive(5, 6, 7)
+        total = self.came2[self.z].astype(F32)
+        for step in range(3):
+            total = total + self.came3[step].astype(F32)
+        return total
+
+    def scatter0(self):
+        self.start(0)
+
+    def scatter1(self):
+        self.add0()
+        self.start(1, 2)
+
+    def scatter2(self):
+        self.add1(self.a1, self.b1)
+        self.start(3, 4)
+
+    def scatter3(self):
+        self.add2(self.came2)
+        self.start(5, 6, 7)
+
+
+def half_shape(rows, cols):
+    return (4, 2, 2, rows, cols)
+
+
+def scatter_scratch(rows, cols, first=True, middle=True, last=True):
+    shapes = []
+    if first:
+        shapes += [half_shape(rows, cols)] * 2
+    if first or middle:
+        shapes += [(2, 2, rows, cols)] * 2
+    if middle or last:
+        shapes += [(4, rows, cols)]
+    if last:
+        shapes += [(3, rows, cols)]
+    return [pltpu.VMEM(shape, BF16) for shape in shapes]
+
+
+ANY = pl.BlockSpec(memory_space=pl.ANY)
+DMA = pltpu.SemaphoreType.DMA
+
+
+def weights_kernel(
+    h_ref, dup_ref, att_ref, dattn_ref, other_ref, mine_ref,
+    up_other, up_mine, out_other, out_mine, a_ref, b_ref,
+    own, came0, a1, b1, send, recv, local,
+):
+    step = pl.program_id(0)
+    down = Scatter(send, recv, 0, other=other_ref, own=own, came0=came0, a1=a1, b1=b1)
+    load = pltpu.make_async_copy(mine_ref, own, local)
+
+    @pl.when(step == 0)
+    def _():
+        load.start()
+        greet(plane_peers())
+        down.scatter0()
+
+    @pl.when(step == 2)
+    def _():
+        load.wait()
+        down.scatter1()
+
+    @pl.when(step < 6)
+    def _():
+        value = tn(h_ref[...], dup_ref[...]).astype(BF16)
+
+        @pl.when(step < 3)
+        def _():
+            up_other[...] = value
+
+        @pl.when(step >= 3)
+        def _():
+            up_mine[...] = value
+
+    @pl.when(step >= 6)
+    def _():
+        value = tn(att_ref[...], dattn_ref[...]).astype(BF16)
+
+        @pl.when(step == 6)
+        def _():
+            out_other[...] = value
+
+        @pl.when(step == 7)
+        def _():
+            out_mine[...] = value
+            down.add1(a_ref, b_ref)
+            down.drain(0, 1, 2)
+
+
+def weights_call(hidden, d_up, att, d_attention, other, mine):
+    n = hidden.shape[0]
+    half = FF // 2
+    rows, cols = D * 4 // 16, D // 2
+
+    def clamp(s, low, high):
+        return jnp.minimum(jnp.maximum(s, low), high)
+
+    def fixed(shape):
+        return pl.BlockSpec(shape, lambda s: (0,) * len(shape))
+
+    handed = (2, 2, rows, cols)
+    return pl.pallas_call(
+        weights_kernel,
+        name="weights",
+        grid=(8,),
+        out_shape=(
+            jax.ShapeDtypeStruct((D, half), BF16),
+            jax.ShapeDtypeStruct((D, half), BF16),
+            jax.ShapeDtypeStruct((D, D // 2), BF16),
+            jax.ShapeDtypeStruct((D, D // 2), BF16),
+            jax.ShapeDtypeStruct(handed, BF16),
+            jax.ShapeDtypeStruct(handed, BF16),
+        ),
+        in_specs=[
+            pl.BlockSpec((n, 256), lambda s: (0, jnp.where(s < 6, lax.rem(s, 3), 2))),
+            pl.BlockSpec((n, half), lambda s: (0, jnp.where(s < 3, 0, 1))),
+            whole((n, D)),
+            pl.BlockSpec((n, D // 2), lambda s: (0, jnp.where(s < 7, 0, 1))),
+            ANY,
+            ANY,
+        ],
+        out_specs=(
+            pl.BlockSpec((256, half), lambda s: (clamp(s, 0, 2), 0)),
+            pl.BlockSpec((256, half), lambda s: (clamp(s - 3, 0, 2), 0)),
+            fixed((D, D // 2)),
+            fixed((D, D // 2)),
+            fixed(handed),
+            fixed(handed),
+        ),
+        scratch_shapes=scatter_scratch(rows, cols, middle=False, last=False)
+        + [DMA((3,)), DMA((3,)), DMA],
+        compiler_params=pltpu.CompilerParams(
+            collective_id=1, has_side_effects=True, vmem_limit_bytes=BIG
+        ),
+        cost_estimate=cost(2 * n * D * (FF + D), 30e6),
+    )(
+        hidden, d_up, att, d_attention,
+        other.reshape(half_shape(rows, cols)), mine.reshape(half_shape(rows, cols)),
+    )
+
+
+def back_kernel(
+    ql, qs, ko, vo, kx, vx, ks, vs, dol, dos, lse, cos_ref, sin_ref,
+    a_in, b_in, up_other, up_mine, out_other, out_mine,
+    dq_ref, dk_ref, dv_ref, down_ref, up_ref, out_ref,
+    down_a, down_b, down2, down3,
+    up_own, up_came, up_a, up_b, up2,
+    out_own, out_came, out_a, out_b, out2,
+    leave, come, keep_k, keep_v, keep_sk, keep_sv,
+    send, recv, send_kv, recv_kv, local,
+):
+    step = pl.program_id(0)
+    me = lax.axis_index("span")
+    rows = ql.shape[0]
+    down = Scatter(send, recv, 0, a1=down_a, b1=down_b, came2=down2, came3=down3)
+    up = Scatter(
+        send, recv, 8, other=up_other, own=up_own, came0=up_came, a1=up_a, b1=up_b, came2=up2
+    )
+    out = Scatter(
+        send, recv, 13, other=out_other, own=out_own, came0=out_came, a1=out_a, b1=out_b,
+        came2=out2,
+    )
+    loads = [
+        pltpu.make_async_copy(src, dst, local.at[i])
+        for i, (src, dst) in enumerate(
+            [(a_in, down_a), (b_in, down_b), (up_mine, up_own), (out_mine, out_own)]
+        )
+    ]
+    cos = cos_ref[pl.ds(pl.multiple_of(me * rows, rows), rows), :]
+    sin = sin_ref[pl.ds(pl.multiple_of(me * rows, rows), rows), :]
+
+    def kv_copy(pair):
+        return pltpu.make_async_remote_copy(
+            src_ref=leave.at[pair],
+            dst_ref=come.at[pair],
+            send_sem=send_kv.at[pair],
+            recv_sem=recv_kv.at[pair],
+            device_id={"span": 1 - me},
+            device_id_type=MESH,
+        )
+
+    @pl.when(step == 0)
+    def _():
+        for load in loads:
+            load.start()
+        greet(plane_peers() + line_peers())
+        up.scatter0()
+        out.scatter0()
+        loads[0].wait()
+        loads[1].wait()
+        down.start(3, 4)
+
+    @pl.when(step == 1)
+    def _():
+        loads[2].wait()
+        loads[3].wait()
+        up.scatter1()
+        out.scatter1()
+
+    @pl.when(step == 3)
+    def _():
+        down.scatter3()
+
+    @pl.when(step == 5)
+    def _():
+        up.scatter2()
+        out.scatter2()
+
+    @pl.when(step > 0)
+    def _():
+        pair = step - 1
+        kv_copy(pair).wait_recv()
+        dk = keep_k[...] + come[pair, :rows, :PAIR].astype(F32)
+        dk_ref[:rows, :] = turn_back(dk, cos, sin).astype(BF16)
+        dv = keep_v[...] + come[pair, :rows, PAIR:].astype(F32)
+        dv_ref[:rows, :] = dv.astype(BF16)
+        zero = jnp.zeros((SHORT, PAIR), F32)
+        sk = keep_sk[...] + come[pair, rows:, :PAIR].astype(F32)
+        sk = jnp.where(me == 0, turn_back(sk, cos[:SHORT], sin[:SHORT]), zero)
+        sv = jnp.where(me == 0, keep_sv[...] + come[pair, rows:, PAIR:].astype(F32), zero)
+        dk_ref[rows : rows + SHORT, :] = sk.astype(BF16)
+        dv_ref[rows : rows + SHORT, :] = sv.astype(BF16)
+        rest = jnp.zeros((rows - SHORT, PAIR), BF16)
+        dk_ref[rows + SHORT :, :] = rest
+        dv_ref[rows + SHORT :, :] = rest
+
+    @pl.when(step < PAIRS)
+    def _():
+        stats = lse[0]
+        dq, dk, dv = attend_back_slot(
+            ql[...], [ko[...], kx[...]], [vo[...], vx[...]], dol[...], [stats[0:1], stats[1:2]]
+        )
+        dq_ref[:rows, :] = turn_back(dq, cos, sin).astype(BF16)
+        keep_k[...] = dk[0]
+        keep_v[...] = dv[0]
+        leave[step, :rows, :PAIR] = dk[1].astype(BF16)
+        leave[step, :rows, PAIR:] = dv[1].astype(BF16)
+        dq, dk, dv = attend_back_slot(
+            qs[...], [ks[...]], [vs[...]], dos[...], [stats[2:3], stats[3:4]]
+        )
+        dq_ref[rows:, :] = turn_back(dq, cos, sin).astype(BF16)
+        keep_sk[...] = dk[0]
+        keep_sv[...] = dv[0]
+        leave[step, rows:, :PAIR] = dk[0].astype(BF16)
+        leave[step, rows:, PAIR:] = dv[0].astype(BF16)
+        kv_copy(step).start()
+
+    @pl.when(step == PAIRS)
+    def _():
+        down_ref[...] = down.total()
+        up.add2(up_ref)
+        out.add2(out_ref)
+        down.drain(3, 4, 5, 6, 7)
+        up.drain(0, 1, 2, 3, 4)
+        out.drain(0, 1, 2, 3, 4)
+        for pair in range(PAIRS):
+            kv_copy(pair).wait_send()
+
+
+def back_call(q, kv_own, kv_other, kv_short, d_att, lse, cos, sin, handed, up, out, rows):
+    last = PAIRS - 1
+
+    def late(s):
+        return jnp.minimum(s, last)
+
+    def early(s):
+        return jnp.maximum(s - 1, 0)
+
+    def fixed(shape):
+        return pl.BlockSpec(shape, lambda s: (0,) * len(shape))
+
+    specs = [
+        pl.BlockSpec(s.block_shape, partial(lambda m, h: m(late(h)), s.index_map))
+        for s in pair_specs(rows)
+    ]
+    n = SLOTS * rows
+    dr, dc = FF // 16, D // 2
+    ur, uc = D // 16, FF // 2
+    wr, wc = D // 16, D // 2
+    return pl.pallas_call(
+        back_kernel,
+        name="attend_back",
+        grid=(PAIRS + 1,),
+        out_shape=(
+            jax.ShapeDtypeStruct((n, D), BF16),
+            jax.ShapeDtypeStruct((n, D), BF16),
+            jax.ShapeDtypeStruct((n, D), BF16),
+            jax.ShapeDtypeStruct((dr, dc), F32),
+            jax.ShapeDtypeStruct((4, ur, uc), BF16),
+            jax.ShapeDtypeStruct((4, wr, wc), BF16),
+        ),
+        in_specs=specs
+        + [
+            pl.BlockSpec((rows, PAIR), lambda s: (0, late(s))),
+            pl.BlockSpec((rows, PAIR), lambda s: (1, late(s))),
+            pl.BlockSpec((1, 4, rows), lambda s: (late(s), 0, 0)),
+            whole((LEN, PAIR)),
+            whole((LEN, PAIR)),
+        ]
+        + [ANY] * 6,
+        out_specs=(
+            pl.BlockSpec((n, PAIR), lambda s: (0, late(s))),
+            pl.BlockSpec((n, PAIR), lambda s: (0, early(s))),
+            pl.BlockSpec((n, PAIR), lambda s: (0, early(s))),
+            fixed((dr, dc)),
+            fixed((4, ur, uc)),
+            fixed((4, wr, wc)),
+        ),
+        scratch_shapes=[
+            pltpu.VMEM((2, 2, dr, dc), BF16),
+            pltpu.VMEM((2, 2, dr, dc), BF16),
+            pltpu.VMEM((4, dr, dc), BF16),
+            pltpu.VMEM((3, dr, dc), BF16),
+        ]
+        + scatter_scratch(ur, uc, last=False)
+        + scatter_scratch(wr, wc, last=False)
+        + [
+            pltpu.VMEM((PAIRS, rows + SHORT, 2 * PAIR), BF16),
+            pltpu.VMEM((PAIRS, rows + SHORT, 2 * PAIR), BF16),
+            pltpu.VMEM((rows, PAIR), F32),
+            pltpu.VMEM((rows, PAIR), F32),
+            pltpu.VMEM((SHORT, PAIR), F32),
+            pltpu.VMEM((SHORT, PAIR), F32),
+            DMA((18,)),
+            DMA((18,)),
+            DMA((PAIRS,)),
+            DMA((PAIRS,)),
+            DMA((4,)),
+        ],
+        compiler_params=pltpu.CompilerParams(
+            collective_id=2, has_side_effects=True, vmem_limit_bytes=BIG
+        ),
+        cost_estimate=cost(40 * D * rows * (LEN + SHORT), 30e6, HEADS * rows * (LEN + SHORT)),
+    )(
+        q, q, kv_own, kv_own, kv_other, kv_other, kv_short, kv_short, d_att, d_att, lse, cos, sin,
+        *handed, *(w.reshape(half_shape(ur, uc)) for w in up),
+        *(w.reshape(half_shape(wr, wc)) for w in out),
+    )
+
+
+BLOCKS = 3
+TILES = 4
+
+
+def end_kernel(
+    tok_ref, dmid_ref, hidden_ref, mod_ref, gain_ref, weight_ref, flag_ref,
+    dq_any, dk_any, dv_any, up_any, out_any,
+    grad_ref, gqkv_ref, gup_ref, gout_ref, late_ref,
+    dqkv, hidden_t,
+    up2, up3, out2, out3,
+    other, own, came0, a1, b1, came2, came3,
+    sums, sums_came, sums_all, late_came,
+    send, recv, send_late, recv_late, local,
+):
+    step = pl.program_id(0)
+    s, me = lax.axis_index("seq"), lax.axis_index("span")
+    up = Scatter(send, recv, 0, came2=up2, came3=up3)
+    out = Scatter(send, recv, 8, came2=out2, came3=out3)
+    blocks = [
+        Scatter(
+            send, recv, 16 + 8 * b, other=other.at[b], own=own.at[b], came0=came0.at[b],
+            a1=a1.at[b], b1=b1.at[b], came2=came2.at[b], came3=came3.at[b],
+        )
+        for b in range(BLOCKS)
+    ]
+    loads = [
+        pltpu.make_async_copy(src, dst, local.at[i])
+        for i, (src, dst) in enumerate(
+            [(up_any, up2), (out_any, out2)]
+            + [
+                (a, dqkv.at[:, pl.ds(k * D, D)])
+                for k, a in enumerate([dq_any, dk_any, dv_any])
+            ]
+        )
+    ]
+    wide = 3 * D // 2 // BLOCKS
+
+    def product(core, b):
+        start = pl.multiple_of(core * (3 * D // 2) + b * wide, 128)
+        value = nn(hidden_t[...], dqkv[:, pl.ds(start, wide)]).astype(BF16)
+        return value.reshape(half_shape(D // 16, wide))
+
+    def late_copy(k):
+        if k == 0:
+            src, dst, peer = sums, sums_came, {"span": 1 - me}
+        else:
+            src, dst, peer = sums_all, late_came.at[s], {"seq": lax.rem(s + k, 16)}
+        return pltpu.make_async_remote_copy(
+            src_ref=src,
+            dst_ref=dst,
+            send_sem=send_late.at[k],
+            recv_sem=recv_late.at[k],
+            device_id=peer,
+            device_id_type=MESH,
+        )
+
+    @pl.when(step == 0)
+    def _():
+        for load in loads:
+            load.start()
+        hidden_t[...] = hidden_ref[...].T
+        greet([{"span": 1 - me}] + [{"seq": lax.rem(s + k, 16)} for k in range(1, 16)])
+        loads[0].wait()
+        loads[1].wait()
+        up.start(5, 6, 7)
+        out.start(5, 6, 7)
+        for load in loads[2:]:
+            load.wait()
+        sums[...] = jnp.zeros_like(sums)
+
+    for b in range(BLOCKS):
+        @pl.when(step == b)
+        def _():
+            other[b] = product(1 - me, b)
+            blocks[b].scatter0()
+            if b > 0:
+                blocks[b - 1].scatter1()
+            own[b] = product(me, b)
+
+    @pl.when(step == 3)
+    def _():
+        blocks[2].scatter1()
+        blocks[0].scatter2()
+
+    @pl.when(step == 4)
+    def _():
+        blocks[1].scatter2()
+
+    @pl.when(step == 5)
+    def _():
+        blocks[2].scatter2()
+        blocks[0].scatter3()
+
+    @pl.when(step == 6)
+    def _():
+        blocks[1].scatter3()
+
+    @pl.when(step >= BLOCKS)
+    def _():
+        t = step - BLOCKS
+        j = t // 2
+        size = tok_ref.shape[0]
+        scale = mod_ref[pl.ds(j, 1), :][:, D : 2 * D]
+        gain = gain_ref[...].astype(F32)
+        start = pl.multiple_of(t * size, size)
+        d_hidden = nt(dqkv[pl.ds(start, size), :], weight_ref[...])
+        x = tok_ref[...].astype(F32)
+        center = x - row_mean(x)
+        r = lax.rsqrt(row_mean(center * center) + EPSILON)
+        xhat = center * r
+        hx = col_sum(d_hidden * xhat)
+        fx = d_hidden * (1.0 + scale) * gain
+        grad_ref[...] = dmid_ref[...] + r * (fx - row_mean(fx) - xhat * row_mean(fx * xhat))
+        flag = flag_ref[...]
+        mine = jnp.where(j == 0, flag, 1.0 - flag)
+        shift = col_sum(d_hidden)
+        none = jnp.zeros((3, D), F32)
+        first, second = mine == 0.0, mine != 0.0
+        zero = jnp.zeros((1, D), F32)
+        sums[...] += jnp.concatenate(
+            [
+                jnp.where(first, shift, zero), jnp.where(first, hx * gain, zero),
+                jnp.where(second, shift, zero), jnp.where(second, hx * gain, zero),
+                hx * (1.0 + scale), none,
+            ],
+            axis=0,
+        )
+
+    @pl.when(step == BLOCKS + TILES - 1)
+    def _():
+        late_copy(0).start()
+        blocks[2].scatter3()
+        late_copy(0).wait_recv()
+        sums_all[...] = sums[...] + sums_came[...]
+        for k in range(1, 16):
+            late_copy(k).start()
+        late_came[s] = sums_all[...]
+        gup_ref[...] = up.total()
+        gout_ref[...] = out.total()
+        for b in range(BLOCKS):
+            gqkv_ref[:, b * wide : (b + 1) * wide] = blocks[b].total()
+        up.drain(5, 6, 7)
+        out.drain(5, 6, 7)
+        for block in blocks:
+            block.drain(*range(8))
+        for k in range(16):
+            if k > 0:
+                late_copy(k).wait_recv()
+            late_copy(k).wait_send()
+        late_ref[...] = late_came[...]
+
+
+def end_call(tokens, d_mid, hidden, mods, gain, weight, flag, dq, dk, dv, up2, out2, rows):
+    n = SLOTS * rows
+    size = n // TILES
+    r = D // 16
+    wide = 3 * D // 2 // BLOCKS
+
+    def tile(s):
+        return (jnp.maximum(s - BLOCKS, 0), 0)
+
+    def fixed(shape):
+        return pl.BlockSpec(shape, lambda s: (0,) * len(shape))
+
+    def each(shape):
+        return pltpu.VMEM((BLOCKS,) + shape, BF16)
+
+    return pl.pallas_call(
+        end_kernel,
+        name="end",
+        grid=(BLOCKS + TILES,),
+        out_shape=(
+            jax.ShapeDtypeStruct((n, D), F32),
+            jax.ShapeDtypeStruct((r, 3 * D // 2), F32),
+            jax.ShapeDtypeStruct((r, FF // 2), F32),
+            jax.ShapeDtypeStruct((r, D // 2), F32),
+            jax.ShapeDtypeStruct((16, 8, D), F32),
+        ),
+        in_specs=[
+            pl.BlockSpec((size, D), tile),
+            pl.BlockSpec((size, D), tile),
+            whole((n, D)),
+            whole((8, 6 * D)),
+            whole((1, D)),
+            whole((D, 3 * D)),
+            whole((1, D)),
+        ]
+        + [ANY] * 5,
+        out_specs=(
+            pl.BlockSpec((size, D), tile),
+            fixed((r, 3 * D // 2)),
+            fixed((r, FF // 2)),
+            fixed((r, D // 2)),
+            fixed((16, 8, D)),
+        ),
+        scratch_shapes=[
+            pltpu.VMEM((n, 3 * D), BF16),
+            pltpu.VMEM((D, n), BF16),
+            pltpu.VMEM((4, r, FF // 2), BF16),
+            pltpu.VMEM((3, r, FF // 2), BF16),
+            pltpu.VMEM((4, r, D // 2), BF16),
+            pltpu.VMEM((3, r, D // 2), BF16),
+            each(half_shape(r, wide)),
+            each(half_shape(r, wide)),
+            each(half_shape(r, wide)),
+            each((2, 2, r, wide)),
+            each((2, 2, r, wide)),
+            each((4, r, wide)),
+            each((3, r, wide)),
+            pltpu.VMEM((8, D), F32),
+            pltpu.VMEM((8, D), F32),
+            pltpu.VMEM((8, D), F32),
+            pltpu.VMEM((16, 8, D), F32),
+            DMA((16 + 8 * BLOCKS,)),
+            DMA((16 + 8 * BLOCKS,)),
+            DMA((16,)),
+            DMA((16,)),
+            DMA((5,)),
+        ],
+        compiler_params=pltpu.CompilerParams(
+            collective_id=3, has_side_effects=True, vmem_limit_bytes=BIG
+        ),
+        cost_estimate=cost(4 * n * D * 3 * D, 30e6),
+    )(tokens, d_mid, hidden, mods, gain, weight, flag, dq, dk, dv, up2, out2)
+
+
+def exact(left, right, over):
+    return lax.dot_general(
+        left, right, (over, ((), ())), precision=HIGHEST, preferred_element_type=F32
+    )
+
+
+def condition_kernel(
+    place, early_ref, late_ref, table_ref, silu_ref, weight_ref, cond_ref,
+    ada_ref, bias_ref, gcond_ref, gain1_ref, gain2_ref, bd_ref, bu_ref,
+):
+    seq = late_ref.shape[0]
+    me, s = place[2], place[3]
+    early = early_ref[...].reshape(seq, 2, 16, D)
+    early = early[:, 0] + early[:, 1]
+    late = late_ref[...]
+    mods = []
+    for k in range(SLOTS):
+        mods.append(
+            [late[:, 2 * k], late[:, 2 * k + 1]] + [early[:, 4 * k + b] for b in range(4)]
+        )
+    gain1_ref[...] = col_sum(late[:, 4])
+    gain2_ref[...] = col_sum(early[:, 8])
+    bd_ref[...] = col_sum(early[:, 9])
+    for f in range(4):
+        bu_ref[:, f * D : (f + 1) * D] = col_sum(early[:, 10 + f])
+    own = [jnp.zeros((8, D), F32)] * 6
+    row = lax.broadcasted_iota(jnp.int32, (8, seq), 0)
+    wanted = (s * SLOTS + row).astype(F32)
+    for k in range(SLOTS):
+        asked = table_ref[:, SLOTS + k, :].T[:8]
+        chosen = jnp.where(jnp.logical_and(asked == wanted, row < SLOTS), 1.0, 0.0)
+        for b in range(6):
+            own[b] = own[b] + exact(chosen, mods[k][b], ((1,), (0,)))
+    d_silu = jnp.zeros((8, 128), F32)
+    for b in range(6):
+        cols = slice(b * D, (b + 1) * D)
+        bias_ref[:, cols] = col_sum(mods[0][b]) + col_sum(mods[1][b])
+        d_silu += exact(own[b], weight_ref[:, cols].astype(F32), ((1,), (1,)))
+    v = cond_ref[...]
+    sig = 1.0 / (1.0 + jnp.exp(-v))
+    gcond_ref[...] = d_silu * (sig * (1.0 + v * (1.0 - sig)))
+    rows = 128 // seq
+    pick = lax.broadcasted_iota(jnp.int32, (rows, 128), 1) == (
+        s * rows + lax.broadcasted_iota(jnp.int32, (rows, 128), 0)
+    )
+    pick = jnp.where(pick, 1.0, 0.0)
+    silu = [exact(pick, silu_ref[k], ((1,), (1,))) for k in range(SLOTS)]
+    for b in range(3):
+        total = jnp.zeros((rows, D), F32)
+        for k in range(SLOTS):
+            block = jnp.where(me == 0, mods[k][b], mods[k][3 + b])
+            total += exact(silu[k], block, ((1,), (0,)))
+        ada_ref[:, b * D : (b + 1) * D] = total
+
+
+def condition_call(place, early, late, table, silu, ada_weight, cond):
+    seq = late.shape[0]
+
+    def all_of(a):
+        return whole(a.shape)
+
+    outs = ((128 // seq, 3 * D), (1, 6 * D), (8, 128), (1, D), (1, D), (1, D), (1, FF))
+    return pl.pallas_call(
+        condition_kernel,
+        name="condition",
+        out_shape=tuple(jax.ShapeDtypeStruct(o, F32) for o in outs),
+        grid_spec=pltpu.PrefetchScalarGridSpec(
+            num_scalar_prefetch=1,
+            grid=(1,),
+            in_specs=[all_of(a) for a in (early, late, table, silu, ada_weight, cond)],
+            out_specs=[pl.BlockSpec(o, lambda i, p: (0, 0)) for o in outs],
+        ),
+        compiler_params=pltpu.CompilerParams(vmem_limit_bytes=32 << 20),
+        cost_estimate=cost(1e7, 4e6),
+    )(place, early, late, table, silu, ada_weight, cond)
+
+
 def from_peers(array, span):
     return [
         lax.ppermute(array, "span", [((i + step) % span, i) for i in range(span)])
@@ -739,16 +1471,19 @@
     seq_at, span_at = lax.axis_index("seq"), lax.axis_index("span")
     flat = slots * rows
     longest = (lengths[1] > lengths[0]).astype(jnp.int32)
-    place = jnp.stack([longest, 1 - longest, span_at.astype(jnp.int32)])
+    place = jnp.stack(
+        [longest, 1 - longest, span_at.astype(jnp.int32), seq_at.astype(jnp.int32)]
+    )
+    fast = seq == 16 and span == 2
     cos, sin = (jnp.asarray(table) for table in rotary(LEN))
     cond = conditions.astype(F32)
     asked = jnp.broadcast_to(assignment.astype(F32)[:, None], (slots, 128))
     own = jnp.concatenate([cond, asked, jnp.zeros((8 - 2 * slots, 128), F32)], axis=0)
-    mod, table = modulation_call(own, ada_weight, ada_bias[None], seq)
+    mod, table, silu_all = modulation_call(own, ada_weight, ada_bias[None], seq)
 
     tokens2 = tokens.reshape(flat, D)
     gain1, gain2 = norm1_gain[None], norm2_gain[None]
-    q, hidden1, kv_long, kv_tail = project_call(
+    q, hidden1, kv_long, kv_tail, tokens_sorted = project_call(
         place, tokens2, mod, gain1, qkv_weight, cos, sin, rows
     )
     pieces = from_peers(kv_long, span)
@@ -760,12 +1495,44 @@
     (
         out, d_mid, d_att, act, d_low, hidden2, d_up, d_attention, d_mod2, d_gain2, d_bd, d_bu,
     ) = feed_call(
-        place, tokens2, att, cotangent.reshape(flat, D), mod, gain2, out_weight, up_weight,
+        fast, place, tokens2, att, cotangent.reshape(flat, D), mod, gain2, out_weight, up_weight,
         up_bias[None], down_weight, down_bias[None], rows,
     )
-    grad_down = weight_gradient(place, act, d_low, 768, "weight_down")
-    grad_up = weight_gradient(place, hidden2, d_up, 256, "weight_up")
-    grad_out = weight_gradient(place, att, d_attention, 768, "weight_out")
+    if fast:
+        payload = jnp.concatenate(
+            [
+                d_mod2[:, :4].reshape(8, D), d_gain2, d_bd, d_bu.reshape(4, D),
+                jnp.zeros((2, D), F32),
+            ],
+            axis=0,
+        )
+        early = lax.all_gather(payload, ("seq", "span"), axis=0)
+        down = weight_call(place, act, d_low, 768, "weight_down")
+        uo, um, wo, wm, *handed = weights_call(hidden2, d_up, att, d_attention, *down)
+        dq, dk, dv, grad_down, up2, out2 = back_call(
+            q, kv_long, kv_other, kv_short, d_att, lse, cos, sin, handed, (uo, um), (wo, wm), rows
+        )
+        swapped = longest == 1
+        mods = jnp.where(swapped, mod[jnp.array([1, 0, 2, 3, 4, 5, 6, 7])], mod)
+        flag = jnp.broadcast_to(longest.astype(F32), (1, D))
+        grad_in, grad_qkv, grad_up, grad_out, late = end_call(
+            tokens_sorted, d_mid, hidden1, mods, gain1, qkv_weight, flag, dq, dk, dv, up2, out2,
+            rows,
+        )
+        grad_in = grad_in.reshape(tokens.shape)
+        grad_in = jnp.where(swapped, grad_in[::-1], grad_in)
+        padded = jnp.concatenate([cond, jnp.zeros((8 - slots, 128), F32)], axis=0)
+        grad_ada, ada_bias_sum, grad_cond, gain1_sum, gain2_sum, bd_sum, bu_sum = condition_call(
+            place, early, late, table, silu_all, ada_weight, padded
+        )
+        return (
+            out.reshape(tokens.shape), grad_in, grad_cond[:slots], gain1_sum[0], grad_ada,
+            ada_bias_sum[0], grad_qkv, grad_out, gain2_sum[0], grad_up, bu_sum[0], grad_down,
+            bd_sum[0],
+        )
+    grad_down = weight_gradient(act, d_low)
+    grad_up = weight_gradient(hidden2, d_up)
+    grad_out = weight_gradient(att, d_attention)
     early = gather_all(
         jnp.concatenate([d_mod2[:, :4].reshape(-1), d_gain2[0], d_bd[0], d_bu[0]])
     )
@@ -788,7 +1555,7 @@
     d_qkv = join_call(
         place, dq, dk, dv, ek, ev, d_short[:, :D], d_short[:, D:], cos, sin, rows
     )
-    grad_qkv = weight_gradient(place, hidden1, d_qkv, 384, "weight_qkv")
+    grad_qkv = weight_gradient(hidden1, d_qkv)
     grad_in, d_mod1, d_gain1 = last_call(
         place, tokens2, d_qkv, d_mid, mod, gain1, qkv_weight, rows
     )

time: 389 us -> 261 us (0.67); the launches traced: 384 us -> 260 us
  Pallas kernels: 164 us -> 210 us
  starting transfers between devices: 45.8 us -> 2.53 us
  blocking collectives: 41.8 us -> 0 us
  waiting for transfers between devices: 36.2 us -> 0.02 us
  other arithmetic: 37.7 us -> 13.3 us
  local copies, waits for them, and re-layouts: 36 us -> 18.6 us
  matrix products: 5.83 us -> 0 us
    pallas_call x4 -> x5, Pallas kernels: 84.4 us -> 158 us  [the longest x1 46.3 us: back_call(): pl.pallas_call(back_kernel, name='attend_back', grid=(PAIRS + 1,), out_sh...]
    ppermute x35 -> x0, starting transfers between devices: 43.1 us -> none  [the longest x12 22.7 us: reduce_tiles(): lax.ppermute(pick(quarter, 0, (z + step) % 4).astype(BF16), 'seq', [(i, (...]
    all_gather x1 -> x0, blocking collectives: 41.8 us -> none  [gather_all(): lax.all_gather(flat, ('seq', 'span'), axis=0)]
    ppermute x35 -> x0, waiting for transfers between devices: 36.2 us -> none  [the longest x12 15 us: reduce_tiles(): lax.ppermute(pick(quarter, 0, (z + step) % 4).astype(BF16), 'seq', [(i, (...]
    pallas_call x4 -> x1, Pallas kernels: 42.3 us -> 14 us  [weight_call(): pl.pallas_call(weight_kernel, name=name, out_shape=(jax.ShapeDtypeStruct(...]
    add x25 -> x0, other arithmetic: 18.5 us -> none  [the longest x4 5.63 us: reduce_tiles(): pair = (mine.astype(F32) + came.astype(F32)).reshape(2, 2, 2, 2, part, cols)]
    convert_element_type x16 -> x0, local copies, waits for them, and re-layouts: 7.51 us -> none  [the longest x4 3.31 us: reduce_tiles(): sent_b = lax.ppermute(pick(second, 1, 1 - y).astype(BF16), 'seq', along_y)]
    reduce_sum x5 -> x0, other arithmetic: 7.15 us -> none  [the longest x1 2.62 us: shards(): mods2 = jnp.sum(early[:, :, :cut], axis=1).reshape(seq * slots, 4 * D)]
  transfers between devices with their start and end apart: 38 -> 3, of which waited for: 10 -> 0; matrix products, arithmetic and copies ran while one was open for 17% -> 4% of each run, Pallas kernels for 22% -> 50%
where the time goes in v2:
time: 261 us; the launch traced here: 260 us
  Pallas kernels  210 us (80%)
  local copies, waits for them, and re-layouts  18.6 us (7%)
  between operations  15.6 us (6%)
  other arithmetic  13.3 us (5%)
    pallas_call x1, Pallas kernels, back_call(): pl.pallas_call(back_kernel, name='attend_back', grid=(PAIRS + 1,), out_sh...  46.3 us
    pallas_call x1, Pallas kernels, end_call(): pl.pallas_call(end_kernel, name='end', grid=(BLOCKS + TILES,), out_shape=...  42 us
    pallas_call x1, Pallas kernels, feed_call(): pl.pallas_call(partial(feed_kernel, halves), name='feed', out_shape=(jax....  37.6 us
    pallas_call x1, Pallas kernels, weights_call(): pl.pallas_call(weights_kernel, name='weights', grid=(8,), out_shape=(jax....  27.2 us
    pallas_call x1, Pallas kernels, attend_call(): pl.pallas_call(attend_kernel, name='attend', grid=(PAIRS,), out_shape=(ja...  16.8 us
    pallas_call x1, Pallas kernels, weight_call(): pl.pallas_call(weight_kernel, name=name, out_shape=(jax.ShapeDtypeStruct(...  14 us
    pallas_call x1, Pallas kernels, project_call(): pl.pallas_call(project_kernel, name='project', out_shape=(jax.ShapeDtypeS...  11 us
    pallas_call x1, Pallas kernels, modulation_call(): pl.pallas_call(partial(modulation_kernel, n), name='modulation', out_shap...  10.5 us
  transfers between devices with their start and end apart: 3, of which 0 were waited for; matrix products, arithmetic and copies ran while one was open for 4% of the time, Pallas kernels for 50%

profile of v2, /device:TPU:0, one launch (start us, length us, event | category | flops | bytes accessed | tf_op | source)
XLA Modules:
  0.0 260.2 jit_solution(2402256125641849784)
XLA Ops:
  7.2 1.3 fusion
  11.3 0.7 broadcast_in_dim.36.bias_ref
  12.0 1.3 broadcast_in_dim.37.gain_ref
  13.9 1.3 copy-done.2
  15.2 10.5 %modulation.1 = (f32[8,4608]{1,0:T(8,128)S(1)}, f32[16,8,128]{2,1,0:T(8,128)S(1)}, f32[2,16,128]{2,1,0:T(8,128)S(1)}) custom-call(f32[8,128]{1,0:T(8,128)S(1)} %maximum_maximum_fusion.own_ref, bf16[128,4608]{1,0:T(8,128)(2,1)S(1)} %copy-done.2, bf16[1,4608]{1,0:T(2,128)(2,1)S(1)} %broadcast_in_dim.36.bias_ref), custom_call_target="tpu_custom_call" | custom-call | flops 10000000 | bytes 2000000 | tf_op jit(solution)/shard_map/modulation/pallas_call | solution.py:141
  26.4 11.0 %project.1 = (bf16[1024,768]{1,0:T(8,128)(2,1)}, bf16[1024,768]{1,0:T(8,128)(2,1)}, bf16[512,1536]{1,0:T(8,128)(2,1)}, bf16[512,1536]{1,0:T(8,128)(2,1)}, bf16[1024,768]{1,0:T(8,128)(2,1)}) custom-call(s32[4]{0:T(128)} %pad_add_fusion.order.place, bf16[1024,768]{1,0:T(8,128)(2,1)} %bitcast.18, f32[8,4608]{1,0:T(8,128)} %copy-done, ...), custom_call_target="tpu_custom_call" | custom-call | flops 3623878656 | bytes 14000000 | tf_op jit(solution)/shard_map/project/pallas_call | solution.py:196
  37.5 1.0 slice.17
  38.6 2.4 collective-permute-start.1
  44.1 1.8 broadcast_select_fusion.ks.vs
  45.9 1.2 copy-done.16
  47.1 16.8 %attend.1 = (bf16[1024,768]{1,0:T(8,128)(2,1)}, f32[6,4,512]{2,1,0:T(4,128)}) custom-call(bf16[1024,768]{1,0:T(8,128)(2,1)} %get-tuple-element.62.ql.qs, bf16[1024,768]{1,0:T(8,128)(2,1)} %get-tuple-element.62.ql.qs, bf16[512,1536]{1,0:T(8,128)(2,1)} %get-tuple-element.63.ko.vo, bf16[512,1536]{1,0:T(8,128)(2,1)} %get-tuple-element.63.ko.vo, ...), custom_call_target="tpu_custom_call" | custom-call | flops 7247757312 | bytes 9000000 | tf_op jit(solution)/shard_map/attend/pallas_call | solution.py:279
  64.0 37.6 %feed.1 = (bf16[1024,768]{1,0:T(8,128)(2,1)}, f32[1024,768]{1,0:T(8,128)}, bf16[1024,768]{1,0:T(8,128)(2,1)}, bf16[1024,3072]{1,0:T(8,128)(2,1)}, bf16[1024,768]...) custom-call(s32[4]{0:T(128)} %pad_add_fusion.order.place, ...), custom_call_target="tpu_custom_call" | custom-call | flops 21743271936 | bytes 40000000 | tf_op jit(solution)/shard_map/feed/pallas_call | solution.py:489
  101.6 0.8 slice.18
  102.9 1.4 reduce.7
  104.3 1.9 concatenate.10
  106.3 14.0 %weight_down.1 = (bf16[3072,384]{1,0:T(8,128)(2,1)}, bf16[3072,384]{1,0:T(8,128)(2,1)}) custom-call(s32[4]{0:T(128)} %pad_add_fusion.order.place, bf16[1024,3072]{1,0:T(8,128)(2,1)} %get-tuple-element.75.left_ref, bf16[1024,768]{1,0:T(8,128)(2,1)} %get-tuple-element.76.right_ref), custom_call_target="tpu_custom_call" | custom-call | flops 4831838208 | bytes 12582912 | tf_op jit(solution)/shard_map/weight_down/pallas_call | solution.py:557
  120.3 27.2 %weights.1 = (bf16[768,1536]{1,0:T(8,128)(2,1)}, bf16[768,1536]{1,0:T(8,128)(2,1)}, bf16[768,384]{1,0:T(8,128)(2,1)}, bf16[768,384]{1,0:T(8,128)(2,1)}, bf16[2,2...) custom-call(bf16[1024,768]{1,0:T(8,128)(2,1)} %get-tuple-element.72.h_ref, ...), custom_call_target="tpu_custom_call" | custom-call | flops 6039797760 | bytes 30000000 | tf_op jit(solution)/shard_map/weights/pallas_call | solution.py:911
  147.5 46.3 %attend_back.1 = (bf16[1024,768]{1,0:T(8,128)(2,1)}, bf16[1024,768]{1,0:T(8,128)(2,1)}, bf16[1024,768]{1,0:T(8,128)(2,1)}, f32[192,384]{1,0:T(8,128)}, bf16[4,48...) custom-call(bf16[1024,768]{1,0:T(8,128)(2,1)} %get-tuple-element.62.ql.qs, bf16[1024,768]{1,0:T(8,128)(2,1)} %get-tuple-element.62.ql.qs, ...), custom_call_target="tpu_custom_call" | custom-call | flops 18119393280 | bytes 30000000 | tf_op jit(solution)/shard_map/attend_back/pallas_call | solution.py:1089
  194.4 42.0 %end.1 = (f32[1024,768]{1,0:T(8,128)}, f32[48,1152]{1,0:T(8,128)}, f32[48,1536]{1,0:T(8,128)}, f32[48,384]{1,0:T(8,128)}, f32[16,8,768]{2,1,0:T(8,128)}) custom-call(bf16[1024,768]{1,0:T(8,128)(2,1)} %get-tuple-element.67.tok_ref, f32[1024,768]{1,0:T(8,128)} %get-tuple-element.68.dmid_ref, bf16[1024,768]{1,0:T(8,128)(2,1)} %get-tuple-element.69.hidden_ref, ...), custom_call_target="tpu_custom_call" | custom-call | flops 7247757312 | bytes 30000000 | tf_op jit(solution)/shard_map/end/pallas_call | solution.py:1317
  236.4 5.0 %reverse_select_fusion = f32[2,512,768]{2,1,0:T(8,128)} fusion(f32[2,512,768]{2,1,0:T(8,128)} %bitcast.17, pred[]{:T(512)} %bitcast.5), kind=kLoop, calls=%fused_computation.1 | loop fusion | flops 786432 | bytes 6291457 | tf_op jit(solution)/shard_map/jit(_where)/select_n | solution.py:1523
  241.4 1.4 copy-done.4
  242.8 4.7 %condition.1 = (f32[8,2304]{1,0:T(8,128)}, f32[1,4608]{1,0:T(1,128)S(1)}, f32[8,128]{1,0:T(8,128)S(1)}, f32[1,768]{1,0:T(1,128)S(1)}, f32[1,768]{1,0:T(1,128)S(1...) custom-call(s32[4]{0:T(128)S(1)} %copy-done.6, f32[32,16,768]{2,1,0:T(8,128)S(1)} %bitcast.16, f32[16,8,768]{2,1,0:T(8,128)S(1)} %copy-done.5, ...), custom_call_target="tpu_custom_call" | custom-call | flops 10000000 | bytes 4000000 | tf_op jit(solution)/shard_map/condition/pallas_call | solution.py:1438
  251.9 0.7 copy.37
  252.6 0.7 copy.38
  (63 shorter events, 11.5 us)
Async XLA Ops:
  7.2 234.2 %all-gather.3.cloned.1.call-start = ((), (), s32[]{:S(2)}) async-start(), calls=%async_computation | async-start | bytes 1622016 | tf_op jit(solution)/shard_map/all_gather | solution.py:1509
  13.9 1.3 copy-start.2
  25.7 0.7 copy-start
  26.4 14.6 %copy-start.15 = (s32[8]{0:T(128)S(1)}, s32[8]{0:T(128)}, u32[]{:S(2)}) copy-start(s32[8]{0:T(128)} %constant.41) | copy-start | bytes 100
  37.4 3.6 %copy-start.1 = (f32[8,4608]{1,0:T(8,128)S(1)}, f32[8,4608]{1,0:T(8,128)}, u32[]{:S(2)}) copy-start(f32[8,4608]{1,0:T(8,128)} %copy-done) | copy-start | bytes 442372
  37.4 4.9 %copy-start.14 = (bf16[2,128]{1,0:T(2,128)(2,1)S(1)}, bf16[2,128]{1,0:T(2,128)(2,1)}, u32[]{:S(2)}) copy-start(bf16[2,128]{1,0:T(2,128)(2,1)} %param.19) | copy-start | bytes 1540
  37.4 4.9 %copy-start.12 = (bf16[768]{0:T(1024)(128)(2,1)S(1)}, bf16[768]{0:T(1024)(128)(2,1)}, u32[]{:S(2)}) copy-start(bf16[768]{0:T(1024)(128)(2,1)} %param.27) | copy-start | bytes 4612
  37.4 5.5 %copy-start.11 = (bf16[3072]{0:T(1024)(128)(2,1)S(1)}, bf16[3072]{0:T(1024)(128)(2,1)}, u32[]{:S(2)}) copy-start(bf16[3072]{0:T(1024)(128)(2,1)} %param.29) | copy-start | bytes 18436
  37.4 6.1 %copy-start.13 = (bf16[768]{0:T(1024)(128)(2,1)S(1)}, bf16[768]{0:T(1024)(128)(2,1)}, u32[]{:S(2)}) copy-start(bf16[768]{0:T(1024)(128)(2,1)} %param.31) | copy-start | bytes 4612
  37.5 8.5 %collective-permute-start = (bf16[512,1536]{1,0:T(8,128)(2,1)}, bf16[512,1536]{1,0:T(8,128)(2,1)S(1)}, u32[]{:S(2)}, u32[]{:S(2)}) collective-permute-start(bf16[512,1536]{1,0:T(8,128)(2,1)} %get-tuple-element.63.ko.vo), channel_id=1, source_target_pairs={{1,0},{0,1},{3,2},{2,3},{5,4},{4,5},{7,6},{6,7},{9,8},{8,9},{11,10... | collective-permute-start | bytes 4718600 | tf_op jit(solution)/shard_map/ppermute | solution.py:1455
  38.6 5.6 %collective-permute-start.1 = (bf16[128,1536]{1,0:T(8,128)(2,1)S(1)}, bf16[128,1536]{1,0:T(8,128)(2,1)S(1)}, u32[]{:S(2)}, u32[]{:S(2)}) collective-permute-start(bf16[128,1536]{1,0:T(8,128)(2,1)S(1)} %slice.17), channel_id=1, source_target_pairs={{0,1},{2,3},{4,5},{6,7},{8,9},{10,11},{12,13},{14,15},{16,17},{18,... | collective-permute-start | bytes 1179656 | tf_op jit(solution)/shard_map/ppermute | solution.py:1492
  45.9 1.2 copy-start.16
  236.4 5.0 %copy-start.3 = (bf16[128,4608]{1,0:T(8,128)(2,1)S(1)}, bf16[128,4608]{1,0:T(8,128)(2,1)}, u32[]{:S(2)}) copy-start(bf16[128,4608]{1,0:T(8,128)(2,1)} %weight_ref.7) | copy-start | bytes 3538948
  236.4 5.0 %copy-start.5 = (f32[16,8,768]{2,1,0:T(8,128)S(1)}, f32[16,8,768]{2,1,0:T(8,128)}, u32[]{:S(2)}) copy-start(f32[16,8,768]{2,1,0:T(8,128)} %get-tuple-element.95.late_ref) | copy-start | bytes 1179652
  236.4 5.0 %copy-start.6 = (s32[4]{0:T(128)S(1)}, s32[4]{0:T(128)}, u32[]{:S(2)}) copy-start(s32[4]{0:T(128)} %pad_add_fusion.order.place) | copy-start | bytes 52
  241.4 1.4 copy-start.4
  242.8 7.7 %copy-start.9 = (f32[48,1152]{1,0:T(8,128)S(1)}, f32[48,1152]{1,0:T(8,128)}, u32[]{:S(2)}) copy-start(f32[48,1152]{1,0:T(8,128)} %get-tuple-element.130) | copy-start | bytes 663556
  242.8 8.4 %copy-start.10 = (f32[48,384]{1,0:T(8,128)S(1)}, f32[48,384]{1,0:T(8,128)}, u32[]{:S(2)}) copy-start(f32[48,384]{1,0:T(8,128)} %get-tuple-element.131) | copy-start | bytes 221188
  242.8 9.0 %copy-start.8 = (f32[48,1536]{1,0:T(8,128)S(1)}, f32[48,1536]{1,0:T(8,128)}, u32[]{:S(2)}) copy-start(f32[48,1536]{1,0:T(8,128)} %get-tuple-element.133) | copy-start | bytes 884740
  242.8 9.8 %copy-start.7 = (f32[192,384]{1,0:T(8,128)S(1)}, f32[192,384]{1,0:T(8,128)}, u32[]{:S(2)}) copy-start(f32[192,384]{1,0:T(8,128)} %get-tuple-element.135) | copy-start | bytes 884740
Sparse Core Ops, SparseCore 0:
  106.4 57.1 all-gather.2

commit v3 on v2

--- a/solution.py
+++ b/solution.py
@@ -54,6 +54,10 @@
     return jnp.sum(x, axis=0, keepdims=True)
 
 
+def wide_row(ref):
+    return ref[...].astype(F32).reshape(1, ref.shape[0])
+
+
 def row_mean(x):
     return jnp.mean(x, axis=-1, keepdims=True)
 
@@ -83,6 +87,11 @@
     return x * cos - swap_halves(x) * sin
 
 
+def slot_of(lengths, j):
+    long = jnp.where(lengths[1] > lengths[0], 1, 0)
+    return j + long - 2 * j * long
+
+
 def heads_of(x):
     lane = lax.broadcasted_iota(jnp.int32, x.shape, 1)
     zero = jnp.zeros_like(x)
@@ -90,9 +99,14 @@
 
 
 def modulation_kernel(
-    n, own_ref, weight_ref, bias_ref, mod_ref, table_ref, silu_ref, send, recv, local
+    n, cond_ref, assign_ref, weight_ref, bias_ref, mod_ref, table_ref, silu_ref,
+    own_ref, send, recv, local,
 ):
     me = lax.axis_index("seq")
+    asked = [jnp.full((1, 128), assign_ref[k].astype(F32)) for k in range(SLOTS)]
+    own_ref[...] = jnp.concatenate(
+        [cond_ref[...].astype(F32)] + asked + [jnp.zeros((8 - 2 * SLOTS, 128), F32)], axis=0
+    )
     barrier = pltpu.get_barrier_semaphore()
     for step in range(1, n):
         pl.semaphore_signal(
@@ -126,7 +140,7 @@
         rows.append(row)
     cond = jnp.concatenate(rows + [jnp.zeros((8 - SLOTS, 128), F32)], axis=0)
     silu = (cond / (1.0 + jnp.exp(-cond))).astype(BF16)
-    mod_ref[...] = nn(silu, weight_ref[...]) + bias_ref[...].astype(F32)
+    mod_ref[...] = nn(silu, weight_ref[...]) + bias_ref[...].astype(F32).reshape(1, 6 * D)
     for slot in range(SLOTS):
         wanted = table_ref[:, SLOTS + slot, :]
         rows = jnp.zeros((n, 128), F32)
@@ -136,7 +150,7 @@
         silu_ref[slot] = (rows / (1.0 + jnp.exp(-rows))).astype(BF16).astype(F32)
 
 
-def modulation_call(own, ada_weight, ada_bias, n):
+def modulation_call(cond, assignment, ada_weight, ada_bias, n):
     vmem = pl.BlockSpec(memory_space=pltpu.VMEM)
     return pl.pallas_call(
         partial(modulation_kernel, n),
@@ -146,9 +160,10 @@
             jax.ShapeDtypeStruct((n, 8, 128), F32),
             jax.ShapeDtypeStruct((SLOTS, n, 128), F32),
         ),
-        in_specs=[vmem] * 3,
+        in_specs=[vmem, pl.BlockSpec(memory_space=pltpu.SMEM), vmem, vmem],
         out_specs=(vmem, vmem, vmem),
         scratch_shapes=[
+            pltpu.VMEM((8, 128), F32),
             pltpu.SemaphoreType.DMA((n,)),
             pltpu.SemaphoreType.DMA((n,)),
             pltpu.SemaphoreType.DMA,
@@ -157,21 +172,20 @@
             collective_id=0, has_side_effects=True, vmem_limit_bytes=16 << 20
         ),
         cost_estimate=cost(1e7, 2e6),
-    )(own, ada_weight, ada_bias)
+    )(cond, assignment, ada_weight, ada_bias)
 
 
 def project_kernel(
     order, tok_ref, mod_ref, gain_ref, weight_ref, cos_ref, sin_ref,
-    q_ref, h_ref, kvl_ref, kvs_ref, sorted_ref,
+    q_ref, h_ref, kvl_ref, kvs_ref,
 ):
     j = pl.program_id(0)
-    sorted_ref[...] = tok_ref[...]
-    row = mod_ref[pl.ds(order[j], 1), :]
+    row = mod_ref[pl.ds(slot_of(order, j), 1), :]
     shift, scale = row[:, :D], row[:, D : 2 * D]
     x = tok_ref[...].astype(F32)
     center = x - row_mean(x)
     xhat = center * lax.rsqrt(row_mean(center * center) + EPSILON)
-    hidden = (xhat * gain_ref[...].astype(F32) * (1.0 + scale) + shift).astype(BF16)
+    hidden = (xhat * wide_row(gain_ref) * (1.0 + scale) + shift).astype(BF16)
     h_ref[...] = hidden
     cos = jnp.concatenate([cos_ref[...]] * PAIRS, axis=1)
     sin = jnp.concatenate([sin_ref[...]] * PAIRS, axis=1)
@@ -201,15 +215,14 @@
             jax.ShapeDtypeStruct((SLOTS * rows, D), BF16),
             jax.ShapeDtypeStruct((rows, 2 * D), BF16),
             jax.ShapeDtypeStruct((rows, 2 * D), BF16),
-            jax.ShapeDtypeStruct((SLOTS * rows, D), BF16),
         ),
         grid_spec=pltpu.PrefetchScalarGridSpec(
             num_scalar_prefetch=1,
             grid=(SLOTS, tiles),
             in_specs=[
-                pl.BlockSpec((tile, D), lambda j, t, o: (o[j] * tiles + t, 0)),
+                pl.BlockSpec((tile, D), lambda j, t, o: (slot_of(o, j) * tiles + t, 0)),
                 whole((8, 6 * D)),
-                whole((1, D)),
+                whole((D,)),
                 whole((D, 3 * D)),
                 pl.BlockSpec((tile, PAIR), lambda j, t, o: (o[2] * tiles + t, 0)),
                 pl.BlockSpec((tile, PAIR), lambda j, t, o: (o[2] * tiles + t, 0)),
@@ -219,7 +232,6 @@
                 pl.BlockSpec((tile, D), lambda j, t, o: (j * tiles + t, 0)),
                 pl.BlockSpec((tile, 2 * D), lambda j, t, o: (t + j * (tiles - 1 - t), 0)),
                 pl.BlockSpec((tile, 2 * D), lambda j, t, o: (j * t, 0)),
-                pl.BlockSpec((tile, D), lambda j, t, o: (j * tiles + t, 0)),
             ],
         ),
         compiler_params=pltpu.CompilerParams(vmem_limit_bytes=BIG),
@@ -405,15 +417,17 @@
 
 
 def feed_kernel(
-    halves, order, tok_ref, att_ref, cot_ref, mod_ref, gain_ref, wo_ref, wu_ref, bu_ref, wd_ref, bd_ref,
+    halves, order, tok_ref, att_ref, cot_ref, hid1_ref, mod_ref, gain_ref, wo_ref, wu_ref, bu_ref, wd_ref, bd_ref,
     out_ref, dmid_ref, datt_ref, act_ref, dlow_ref, h_ref, dup_ref, dattn_ref,
-    dmod_ref, dgain_ref, dbd_ref, dbu_ref,
+    payload_ref, toks_ref, hid1s_ref,
 ):
     j, t = pl.program_id(0), pl.program_id(1)
-    row = mod_ref[pl.ds(order[j], 1), :]
+    toks_ref[...] = tok_ref[...]
+    hid1s_ref[...] = hid1_ref[...]
+    row = mod_ref[pl.ds(slot_of(order, j), 1), :]
     gate1, shift2 = row[:, 2 * D : 3 * D], row[:, 3 * D : 4 * D]
     scale2, gate2 = row[:, 4 * D : 5 * D], row[:, 5 * D :]
-    gain = gain_ref[...].astype(F32)
+    gain, up_bias = wide_row(gain_ref), wide_row(bu_ref)
     attention = nn(att_ref[...], wo_ref[...])
     middle = tok_ref[...].astype(F32) + gate1 * attention
     center = middle - row_mean(middle)
@@ -423,14 +437,15 @@
     h_ref[...] = hidden
     dy = cot_ref[...].astype(F32)
     d_low = (gate2 * dy).astype(BF16)
-    at = [h * order[2] + (1 - h) * (1 - order[2]) if halves else h for h in range(2)]
+    me = lax.axis_index("span")
+    at = [h * me + (1 - h) * (1 - me) if halves else h for h in range(2)]
     for h in range(2):
         dlow_ref[:, part_of(at[h], D // 2)] = d_low[:, h * (D // 2) : (h + 1) * (D // 2)]
     lowered, d_hidden = None, None
     sums = []
     for f in range(0, FF, CHUNK):
         cols = slice(f, f + CHUNK)
-        up = nn(hidden, wu_ref[:, cols]) + bu_ref[:, cols].astype(F32)
+        up = nn(hidden, wu_ref[:, cols]) + up_bias[:, cols]
         d_act = nt(d_low, wd_ref[cols, :])
         square = up * up
         bend = jnp.tanh(up * (GELU_C + (GELU_C * 0.044715) * square))
@@ -448,7 +463,7 @@
         dh = nt(d_up, wu_ref[:, cols])
         lowered = low if lowered is None else lowered + low
         d_hidden = dh if d_hidden is None else d_hidden + dh
-    lowered = lowered + bd_ref[...].astype(F32)
+    lowered = lowered + wide_row(bd_ref)
     out_ref[...] = (middle + gate2 * lowered).astype(BF16)
     d_gate2 = col_sum(dy * lowered)
     d_shift2 = col_sum(d_hidden)
@@ -463,24 +478,28 @@
         dattn_ref[:, part_of(at[h], D // 2)] = d_attention[:, h * (D // 2) : (h + 1) * (D // 2)]
     datt_ref[...] = nt(d_attention, wo_ref[...]).astype(BF16)
     first = jnp.logical_and(j == 0, t == 0)
+    slot = slot_of(order, j)
+    four = jnp.concatenate([d_gate1, d_shift2, hx * gain, d_gate2], axis=0)
+    none = jnp.zeros((4, D), F32)
     add_to(
-        dmod_ref,
+        payload_ref,
         jnp.concatenate(
-            [d_gate1, d_shift2, hx * gain, d_gate2, jnp.zeros((4, D), F32)], axis=0
-        )[None],
-        t == 0,
+            [
+                jnp.where(slot == 0, four, none), jnp.where(slot == 0, none, four),
+                hx * (1.0 + scale2), col_sum(d_low.astype(F32)), *sums, jnp.zeros((2, D), F32),
+            ],
+            axis=0,
+        ),
+        first,
     )
-    add_to(dgain_ref, hx * (1.0 + scale2), first)
-    add_to(dbd_ref, col_sum(d_low.astype(F32)), first)
-    add_to(dbu_ref, jnp.concatenate(sums, axis=1), first)
-
-
-def feed_call(halves, place, tokens, att, cot, mod, gain, wo, wu, bu, wd, bd, rows):
+
+
+def feed_call(halves, place, tokens, att, cot, hidden1, mod, gain, wo, wu, bu, wd, bd, rows):
     tile = min(256, rows)
     tiles = rows // tile
 
     def own(j, t, o):
-        return (o[j] * tiles + t, 0)
+        return (slot_of(o, j) * tiles + t, 0)
 
     def sorted_(j, t, o):
         return (j * tiles + t, 0)
@@ -498,10 +517,9 @@
             jax.ShapeDtypeStruct((n, D), BF16),
             jax.ShapeDtypeStruct((n, FF), BF16),
             jax.ShapeDtypeStruct((n, D), BF16),
-            jax.ShapeDtypeStruct((SLOTS, 8, D), F32),
-            jax.ShapeDtypeStruct((1, D), F32),
-            jax.ShapeDtypeStruct((1, D), F32),
-            jax.ShapeDtypeStruct((1, FF), F32),
+            jax.ShapeDtypeStruct((16, D), F32),
+            jax.ShapeDtypeStruct((n, D), BF16),
+            jax.ShapeDtypeStruct((n, D), BF16),
         ),
         grid_spec=pltpu.PrefetchScalarGridSpec(
             num_scalar_prefetch=1,
@@ -510,13 +528,14 @@
                 pl.BlockSpec((tile, D), own),
                 pl.BlockSpec((tile, D), sorted_),
                 pl.BlockSpec((tile, D), own),
+                pl.BlockSpec((tile, D), own if halves else sorted_),
                 whole((8, 6 * D)),
-                whole((1, D)),
+                whole((D,)),
                 whole((D, D)),
                 whole((D, FF)),
-                whole((1, FF)),
+                whole((FF,)),
                 whole((FF, D)),
-                whole((1, D)),
+                whole((D,)),
             ],
             out_specs=[
                 pl.BlockSpec((tile, D), own),
@@ -527,52 +546,14 @@
                 pl.BlockSpec((tile, D), sorted_),
                 pl.BlockSpec((tile, FF), sorted_),
                 pl.BlockSpec((tile, D), sorted_),
-                pl.BlockSpec((1, 8, D), lambda j, t, o: (o[j], 0, 0)),
-                pl.BlockSpec((1, D), lambda j, t, o: (0, 0)),
-                pl.BlockSpec((1, D), lambda j, t, o: (0, 0)),
-                pl.BlockSpec((1, FF), lambda j, t, o: (0, 0)),
+                pl.BlockSpec((16, D), lambda j, t, o: (0, 0)),
+                pl.BlockSpec((tile, D), sorted_),
+                pl.BlockSpec((tile, D), sorted_),
             ],
         ),
         compiler_params=pltpu.CompilerParams(vmem_limit_bytes=BIG),
         cost_estimate=cost(2 * n * D * (4 * FF + 2 * D), 40e6, n * FF),
-    )(place, tokens, att, cot, mod, gain, wo, wu, bu, wd, bd)
-
-
-def weight_kernel(place, left_ref, right_ref, other_ref, mine_ref):
-    value = tn(left_ref[...], right_ref[...]).astype(BF16)
-
-    @pl.when(pl.program_id(0) == 0)
-    def _():
-        other_ref[...] = value
-
-    @pl.when(pl.program_id(0) == 1)
-    def _():
-        mine_ref[...] = value
-
-
-def weight_call(place, left, right, tile, name):
-    n, rows = left.shape
-    half = right.shape[1] // 2
-    tiles = rows // tile
-    return pl.pallas_call(
-        weight_kernel,
-        name=name,
-        out_shape=(jax.ShapeDtypeStruct((rows, half), BF16),) * 2,
-        grid_spec=pltpu.PrefetchScalarGridSpec(
-            num_scalar_prefetch=1,
-            grid=(2, tiles),
-            in_specs=[
-                pl.BlockSpec((n, tile), lambda c, m, o: (0, m)),
-                pl.BlockSpec((n, half), lambda c, m, o: (0, c)),
-            ],
-            out_specs=[
-                pl.BlockSpec((tile, half), lambda c, m, o: (m + c * (tiles - 1 - m), 0)),
-                pl.BlockSpec((tile, half), lambda c, m, o: (c * m, 0)),
-            ],
-        ),
-        compiler_params=pltpu.CompilerParams(vmem_limit_bytes=BIG),
-        cost_estimate=cost(2 * n * rows * 2 * half, 2 * (n * rows + 2 * (n + rows) * half)),
-    )(place, left, right)
+    )(place, tokens, att, cot, hidden1, mod, gain, wo, wu, bu, wd, bd)
 
 
 def weight_gradient(left, right):
@@ -641,8 +622,8 @@
     out_ref, dmod_ref, dgain_ref,
 ):
     j, t = pl.program_id(0), pl.program_id(1)
-    scale = mod_ref[pl.ds(order[j], 1), :][:, D : 2 * D]
-    gain = gain_ref[...].astype(F32)
+    scale = mod_ref[pl.ds(slot_of(order, j), 1), :][:, D : 2 * D]
+    gain = wide_row(gain_ref)
     d_hidden = nt(dqkv_ref[...], weight_ref[...])
     x = tok_ref[...].astype(F32)
     center = x - row_mean(x)
@@ -665,7 +646,7 @@
     tiles = rows // tile
 
     def own(j, t, o):
-        return (o[j] * tiles + t, 0)
+        return (slot_of(o, j) * tiles + t, 0)
 
     def sorted_(j, t, o):
         return (j * tiles + t, 0)
@@ -687,18 +668,172 @@
                 pl.BlockSpec((tile, 3 * D), sorted_),
                 pl.BlockSpec((tile, D), sorted_),
                 whole((8, 6 * D)),
-                whole((1, D)),
+                whole((D,)),
                 whole((D, 3 * D)),
             ],
             out_specs=[
                 pl.BlockSpec((tile, D), own),
-                pl.BlockSpec((1, 8, D), lambda j, t, o: (o[j], 0, 0)),
+                pl.BlockSpec((1, 8, D), lambda j, t, o: (slot_of(o, j), 0, 0)),
                 pl.BlockSpec((1, D), lambda j, t, o: (0, 0)),
             ],
         ),
         compiler_params=pltpu.CompilerParams(vmem_limit_bytes=BIG),
         cost_estimate=cost(2 * n * D * 3 * D, 18e6),
     )(place, tokens, dqkv, dmid, mod, gain, weight)
+
+
+def share_kernel(
+    tok_ref, mod_ref, gain_ref, weight_ref, cos_ref, sin_ref,
+    q_ref, h_ref, kv_ref, kvx_any, stage, send, recv,
+):
+    step = pl.program_id(0)
+    steps = stage.shape[0]
+    tile = tok_ref.shape[0]
+    me = lax.axis_index("span")
+
+    def copy(i):
+        return pltpu.make_async_remote_copy(
+            src_ref=stage.at[i],
+            dst_ref=kvx_any.at[pl.ds(pl.multiple_of(i * tile, tile), tile)],
+            send_sem=send.at[i],
+            recv_sem=recv.at[i],
+            device_id={"span": 1 - me},
+            device_id_type=MESH,
+        )
+
+    row = mod_ref[pl.ds(step // (steps // SLOTS), 1), :]
+    shift, scale = row[:, :D], row[:, D : 2 * D]
+    x = tok_ref[...].astype(F32)
+    center = x - row_mean(x)
+    xhat = center * lax.rsqrt(row_mean(center * center) + EPSILON)
+    hidden = (xhat * wide_row(gain_ref) * (1.0 + scale) + shift).astype(BF16)
+    h_ref[...] = hidden
+    start = (me * (steps // SLOTS) + lax.rem(step, steps // SLOTS)) * tile
+    start = pl.multiple_of(start, tile)
+    cos = jnp.concatenate([cos_ref[pl.ds(start, tile), :]] * PAIRS, axis=1)
+    sin = jnp.concatenate([sin_ref[pl.ds(start, tile), :]] * PAIRS, axis=1)
+    k = turn(nn(hidden, weight_ref[:, D : 2 * D]), cos, sin).astype(BF16)
+    v = nn(hidden, weight_ref[:, 2 * D :]).astype(BF16)
+    kv_ref[:, :D] = k
+    kv_ref[:, D:] = v
+    stage[step, :, :D] = k
+    stage[step, :, D:] = v
+
+    @pl.when(step == 0)
+    def _():
+        greet([{"span": 1 - me}])
+
+    copy(step).start()
+    q_ref[...] = turn(nn(hidden, weight_ref[:, :D]), cos, sin).astype(BF16)
+
+    @pl.when(step == steps - 1)
+    def _():
+        for i in range(steps):
+            copy(i).wait()
+
+
+def share_call(tokens, mod, gain, weight, cos, sin, rows):
+    tile = 256
+    n = SLOTS * rows
+    steps = n // tile
+
+    def at(width):
+        return pl.BlockSpec((tile, width), lambda s: (s, 0))
+
+    return pl.pallas_call(
+        share_kernel,
+        name="project",
+        grid=(steps,),
+        out_shape=(
+            jax.ShapeDtypeStruct((n, D), BF16),
+            jax.ShapeDtypeStruct((n, D), BF16),
+            jax.ShapeDtypeStruct((n, 2 * D), BF16),
+            jax.ShapeDtypeStruct((n, 2 * D), BF16),
+        ),
+        in_specs=[
+            at(D),
+            whole((8, 6 * D)),
+            whole((D,)),
+            whole((D, 3 * D)),
+            whole((LEN, PAIR)),
+            whole((LEN, PAIR)),
+        ],
+        out_specs=(at(D), at(D), at(2 * D), pl.BlockSpec(memory_space=pl.ANY)),
+        scratch_shapes=[
+            pltpu.VMEM((steps, tile, 2 * D), BF16),
+            pltpu.SemaphoreType.DMA((steps,)),
+            pltpu.SemaphoreType.DMA((steps,)),
+        ],
+        compiler_params=pltpu.CompilerParams(
+            collective_id=4, has_side_effects=True, vmem_limit_bytes=BIG
+        ),
+        cost_estimate=cost(2 * n * D * 3 * D, 14e6),
+    )(tokens, mod, gain, weight, cos, sin)
+
+
+def attend_sorted_kernel(
+    lengths, ql, qs, ko, vo, kx, vx, ks_own, vs_own, ks_other, vs_other,
+    out_ref, lse_ref, q_ref, ko_ref, vo_ref, kx_ref, vx_ref, ks_ref, vs_ref,
+):
+    rows = ql.shape[0]
+    first = lax.axis_index("span") == 0
+    ks = jnp.where(first, ks_own[...], ks_other[...])
+    vs = jnp.where(first, vs_own[...], vs_other[...])
+    q_ref[:rows, :] = ql[...]
+    q_ref[rows:, :] = qs[...]
+    ks_ref[...] = ks
+    vs_ref[...] = vs
+    for ref, given in ((ko_ref, ko), (vo_ref, vo), (kx_ref, kx), (vx_ref, vx)):
+        ref[...] = given[...]
+    out, stats = attend_slot(ql[...], [ko[...], kx[...]], [vo[...], vx[...]])
+    out_ref[:rows, :] = out
+    lse_ref[0, 0:1, :] = stats[0]
+    lse_ref[0, 1:2, :] = stats[1]
+    out, stats = attend_slot(qs[...], [ks], [vs])
+    out_ref[rows:, :] = out
+    lse_ref[0, 2:3, :] = stats[0]
+    lse_ref[0, 3:4, :] = stats[1]
+
+
+def attend_sorted_call(lengths, q, kv, kvx, rows):
+    n = SLOTS * rows
+    per = rows // SHORT
+
+    def long(base):
+        return pl.BlockSpec((rows, PAIR), lambda h, o: (slot_of(o, 0), base + h))
+
+    def short(base):
+        return pl.BlockSpec((SHORT, PAIR), lambda h, o: (slot_of(o, 1) * per, base + h))
+
+    def out(size):
+        return pl.BlockSpec((size, PAIR), lambda h, o: (0, h))
+
+    return pl.pallas_call(
+        attend_sorted_kernel,
+        name="attend",
+        out_shape=(
+            jax.ShapeDtypeStruct((n, D), BF16),
+            jax.ShapeDtypeStruct((PAIRS, 4, rows), F32),
+            jax.ShapeDtypeStruct((n, D), BF16),
+        )
+        + (jax.ShapeDtypeStruct((rows, D), BF16),) * 4
+        + (jax.ShapeDtypeStruct((SHORT, D), BF16),) * 2,
+        grid_spec=pltpu.PrefetchScalarGridSpec(
+            num_scalar_prefetch=1,
+            grid=(PAIRS,),
+            in_specs=[
+                long(0),
+                pl.BlockSpec((rows, PAIR), lambda h, o: (slot_of(o, 1), h)),
+                long(0), long(PAIRS), long(0), long(PAIRS),
+                short(0), short(PAIRS), short(0), short(PAIRS),
+            ],
+            out_specs=[out(n), pl.BlockSpec((1, 4, rows), lambda h, o: (h, 0, 0)), out(n)]
+            + [out(rows)] * 4
+            + [out(SHORT)] * 2,
+        ),
+        compiler_params=pltpu.CompilerParams(vmem_limit_bytes=BIG),
+        cost_estimate=cost(16 * D * rows * (LEN + SHORT), 16e6, HEADS * rows * (LEN + SHORT)),
+    )(lengths, q, q, kv, kv, kvx, kvx, kv, kv, kvx, kvx)
 
 
 def flip(index, bit):
@@ -850,111 +985,140 @@
 
 
 def weights_kernel(
-    h_ref, dup_ref, att_ref, dattn_ref, other_ref, mine_ref,
-    up_other, up_mine, out_other, out_mine, a_ref, b_ref,
-    own, came0, a1, b1, send, recv, local,
+    act_ref, dlow_ref, att_ref, dattn_ref, h_ref, dup_ref,
+    a_ref, b_ref, out_ref, up_ref,
+    other, own, came0, a1, b1, out_other, out_came, up_other, up_came, send, recv,
 ):
     step = pl.program_id(0)
-    down = Scatter(send, recv, 0, other=other_ref, own=own, came0=came0, a1=a1, b1=b1)
-    load = pltpu.make_async_copy(mine_ref, own, local)
+    down = Scatter(send, recv, 0, other=other, own=own, came0=came0, a1=a1, b1=b1)
+    out = Scatter(send, recv, 3, other=out_other, own=out_ref, came0=out_came)
+    up = Scatter(send, recv, 4, other=up_other, own=up_ref, came0=up_came)
 
     @pl.when(step == 0)
     def _():
-        load.start()
         greet(plane_peers())
+
+    @pl.when(step == 8)
+    def _():
+        down.scatter1()
+
+    @pl.when(step == 10)
+    def _():
+        out.add0()
+
+    @pl.when(step < 8)
+    def _():
+        value = tn(act_ref[...], dlow_ref[...]).astype(BF16)
+        value = value.reshape((2, 2) + own.shape[3:])
+
+        @pl.when(step < 4)
+        def _():
+            other[step] = value
+
+        @pl.when(step >= 4)
+        def _():
+            own[step - 4] = value
+
+    @pl.when(step == 3)
+    def _():
         down.scatter0()
 
-    @pl.when(step == 2)
-    def _():
-        load.wait()
-        down.scatter1()
-
-    @pl.when(step < 6)
-    def _():
-        value = tn(h_ref[...], dup_ref[...]).astype(BF16)
-
-        @pl.when(step < 3)
-        def _():
-            up_other[...] = value
-
-        @pl.when(step >= 3)
-        def _():
-            up_mine[...] = value
-
-    @pl.when(step >= 6)
-    def _():
-        value = tn(att_ref[...], dattn_ref[...]).astype(BF16)
-
-        @pl.when(step == 6)
+    @pl.when(jnp.logical_and(step >= 8, step < 10))
+    def _():
+        value = tn(att_ref[...], dattn_ref[...]).astype(BF16).reshape(out_ref.shape)
+
+        @pl.when(step == 8)
         def _():
             out_other[...] = value
-
-        @pl.when(step == 7)
+            out.scatter0()
+
+        @pl.when(step == 9)
         def _():
-            out_mine[...] = value
-            down.add1(a_ref, b_ref)
-            down.drain(0, 1, 2)
-
-
-def weights_call(hidden, d_up, att, d_attention, other, mine):
+            out_ref[...] = value
+
+    @pl.when(step >= 10)
+    def _():
+        value = tn(h_ref[...], dup_ref[...]).astype(BF16)
+        value = value.reshape((2,) + up_ref.shape[1:])
+        z = lax.rem(step, 2) * 2
+
+        @pl.when(step < 12)
+        def _():
+            up_other[pl.ds(z, 2)] = value
+
+        @pl.when(step >= 12)
+        def _():
+            up_ref[pl.ds(z, 2)] = value
+
+    @pl.when(step == 11)
+    def _():
+        up.scatter0()
+
+    @pl.when(step == 13)
+    def _():
+        up.add0()
+        down.add1(a_ref, b_ref)
+        down.drain(0, 1, 2)
+        out.drain(0)
+        up.drain(0)
+
+
+def weights_call(act, d_low, att, d_attention, hidden, d_up):
     n = hidden.shape[0]
     half = FF // 2
-    rows, cols = D * 4 // 16, D // 2
+    dr, dc = FF // 16, D // 2
+    ur, wr = D // 16, D // 16
+    down, up, out = half_shape(dr, dc), half_shape(ur, half), half_shape(wr, dc)
 
     def clamp(s, low, high):
         return jnp.minimum(jnp.maximum(s, low), high)
 
     def fixed(shape):
-        return pl.BlockSpec(shape, lambda s: (0,) * len(shape))
-
-    handed = (2, 2, rows, cols)
+        return whole(shape)
+
+    handed = (2, 2, dr, dc)
+    shapes = (handed, handed, out, up)
     return pl.pallas_call(
         weights_kernel,
         name="weights",
-        grid=(8,),
-        out_shape=(
-            jax.ShapeDtypeStruct((D, half), BF16),
-            jax.ShapeDtypeStruct((D, half), BF16),
-            jax.ShapeDtypeStruct((D, D // 2), BF16),
-            jax.ShapeDtypeStruct((D, D // 2), BF16),
-            jax.ShapeDtypeStruct(handed, BF16),
-            jax.ShapeDtypeStruct(handed, BF16),
-        ),
+        grid=(14,),
+        out_shape=tuple(jax.ShapeDtypeStruct(o, BF16) for o in shapes),
         in_specs=[
-            pl.BlockSpec((n, 256), lambda s: (0, jnp.where(s < 6, lax.rem(s, 3), 2))),
-            pl.BlockSpec((n, half), lambda s: (0, jnp.where(s < 3, 0, 1))),
-            whole((n, D)),
-            pl.BlockSpec((n, D // 2), lambda s: (0, jnp.where(s < 7, 0, 1))),
-            ANY,
-            ANY,
+            pl.BlockSpec((n, D), lambda s: (0, jnp.where(s < 8, lax.rem(s, 4), 3))),
+            pl.BlockSpec((n, dc), lambda s: (0, jnp.where(s < 4, 0, 1))),
+            fixed((n, D)),
+            pl.BlockSpec((n, dc), lambda s: (0, jnp.where(s < 9, 0, 1))),
+            pl.BlockSpec((n, dc), lambda s: (0, jnp.where(s < 10, 0, lax.rem(s, 2)))),
+            pl.BlockSpec((n, half), lambda s: (0, jnp.where(s < 12, 0, 1))),
         ],
-        out_specs=(
-            pl.BlockSpec((256, half), lambda s: (clamp(s, 0, 2), 0)),
-            pl.BlockSpec((256, half), lambda s: (clamp(s - 3, 0, 2), 0)),
-            fixed((D, D // 2)),
-            fixed((D, D // 2)),
-            fixed(handed),
-            fixed(handed),
-        ),
-        scratch_shapes=scatter_scratch(rows, cols, middle=False, last=False)
-        + [DMA((3,)), DMA((3,)), DMA],
+        out_specs=tuple(fixed(o) for o in shapes),
+        scratch_shapes=[
+            pltpu.VMEM(down, BF16),
+            pltpu.VMEM(down, BF16),
+            pltpu.VMEM(down, BF16),
+            pltpu.VMEM(handed, BF16),
+            pltpu.VMEM(handed, BF16),
+            pltpu.VMEM(out, BF16),
+            pltpu.VMEM(out, BF16),
+            pltpu.VMEM(up, BF16),
+            pltpu.VMEM(up, BF16),
+            DMA((5,)),
+            DMA((5,)),
+        ],
         compiler_params=pltpu.CompilerParams(
             collective_id=1, has_side_effects=True, vmem_limit_bytes=BIG
         ),
-        cost_estimate=cost(2 * n * D * (FF + D), 30e6),
-    )(
-        hidden, d_up, att, d_attention,
-        other.reshape(half_shape(rows, cols)), mine.reshape(half_shape(rows, cols)),
-    )
+        cost_estimate=cost(2 * n * D * (2 * FF + D), 30e6),
+    )(act, d_low, att, d_attention, hidden, d_up)
 
 
 def back_kernel(
     ql, qs, ko, vo, kx, vx, ks, vs, dol, dos, lse, cos_ref, sin_ref,
-    a_in, b_in, up_other, up_mine, out_other, out_mine,
+    a_in, b_in, up_in, out_in,
     dq_ref, dk_ref, dv_ref, down_ref, up_ref, out_ref,
     down_a, down_b, down2, down3,
-    up_own, up_came, up_a, up_b, up2,
-    out_own, out_came, out_a, out_b, out2,
+    up_own, up_a, up_b, up2,
+    out_own, out_a, out_b, out2,
     leave, come, keep_k, keep_v, keep_sk, keep_sv,
     send, recv, send_kv, recv_kv, local,
 ):
@@ -962,17 +1126,12 @@
     me = lax.axis_index("span")
     rows = ql.shape[0]
     down = Scatter(send, recv, 0, a1=down_a, b1=down_b, came2=down2, came3=down3)
-    up = Scatter(
-        send, recv, 8, other=up_other, own=up_own, came0=up_came, a1=up_a, b1=up_b, came2=up2
-    )
-    out = Scatter(
-        send, recv, 13, other=out_other, own=out_own, came0=out_came, a1=out_a, b1=out_b,
-        came2=out2,
-    )
+    up = Scatter(send, recv, 8, own=up_own, a1=up_a, b1=up_b, came2=up2)
+    out = Scatter(send, recv, 13, own=out_own, a1=out_a, b1=out_b, came2=out2)
     loads = [
         pltpu.make_async_copy(src, dst, local.at[i])
         for i, (src, dst) in enumerate(
-            [(a_in, down_a), (b_in, down_b), (up_mine, up_own), (out_mine, out_own)]
+            [(a_in, down_a), (b_in, down_b), (up_in, up_own), (out_in, out_own)]
         )
     ]
     cos = cos_ref[pl.ds(pl.multiple_of(me * rows, rows), rows), :]
@@ -993,8 +1152,6 @@
         for load in loads:
             load.start()
         greet(plane_peers() + line_peers())
-        up.scatter0()
-        out.scatter0()
         loads[0].wait()
         loads[1].wait()
         down.start(3, 4)
@@ -1003,10 +1160,10 @@
     def _():
         loads[2].wait()
         loads[3].wait()
-        up.scatter1()
-        out.scatter1()
-
-    @pl.when(step == 3)
+        out.start(1, 2)
+        up.start(1, 2)
+
+    @pl.when(step == 2)
     def _():
         down.scatter3()
 
@@ -1015,58 +1172,58 @@
         up.scatter2()
         out.scatter2()
 
+    @pl.when(step < PAIRS)
+    def _():
+        stats = lse[0]
+        dq, dk, dv = attend_back_slot(
+            ql[...], [ko[...], kx[...]], [vo[...], vx[...]], dol[...], [stats[0:1], stats[1:2]]
+        )
+        dq_ref[:rows, :] = turn_back(dq, cos, sin).astype(BF16)
+        keep_k[lax.rem(step, 2)] = dk[0]
+        keep_v[lax.rem(step, 2)] = dv[0]
+        leave[step, :rows, :PAIR] = dk[1].astype(BF16)
+        leave[step, :rows, PAIR:] = dv[1].astype(BF16)
+        dq, dk, dv = attend_back_slot(
+            qs[...], [ks[...]], [vs[...]], dos[...], [stats[2:3], stats[3:4]]
+        )
+        dq_ref[rows:, :] = turn_back(dq, cos, sin).astype(BF16)
+        keep_sk[lax.rem(step, 2)] = dk[0]
+        keep_sv[lax.rem(step, 2)] = dv[0]
+        leave[step, rows:, :PAIR] = dk[0].astype(BF16)
+        leave[step, rows:, PAIR:] = dv[0].astype(BF16)
+        kv_copy(step).start()
+
     @pl.when(step > 0)
     def _():
         pair = step - 1
         kv_copy(pair).wait_recv()
-        dk = keep_k[...] + come[pair, :rows, :PAIR].astype(F32)
+        dk = keep_k[lax.rem(pair, 2)] + come[pair, :rows, :PAIR].astype(F32)
         dk_ref[:rows, :] = turn_back(dk, cos, sin).astype(BF16)
-        dv = keep_v[...] + come[pair, :rows, PAIR:].astype(F32)
+        dv = keep_v[lax.rem(pair, 2)] + come[pair, :rows, PAIR:].astype(F32)
         dv_ref[:rows, :] = dv.astype(BF16)
         zero = jnp.zeros((SHORT, PAIR), F32)
-        sk = keep_sk[...] + come[pair, rows:, :PAIR].astype(F32)
+        sk = keep_sk[lax.rem(pair, 2)] + come[pair, rows:, :PAIR].astype(F32)
         sk = jnp.where(me == 0, turn_back(sk, cos[:SHORT], sin[:SHORT]), zero)
-        sv = jnp.where(me == 0, keep_sv[...] + come[pair, rows:, PAIR:].astype(F32), zero)
+        sv = jnp.where(me == 0, keep_sv[lax.rem(pair, 2)] + come[pair, rows:, PAIR:].astype(F32), zero)
         dk_ref[rows : rows + SHORT, :] = sk.astype(BF16)
         dv_ref[rows : rows + SHORT, :] = sv.astype(BF16)
         rest = jnp.zeros((rows - SHORT, PAIR), BF16)
         dk_ref[rows + SHORT :, :] = rest
         dv_ref[rows + SHORT :, :] = rest
 
-    @pl.when(step < PAIRS)
-    def _():
-        stats = lse[0]
-        dq, dk, dv = attend_back_slot(
-            ql[...], [ko[...], kx[...]], [vo[...], vx[...]], dol[...], [stats[0:1], stats[1:2]]
-        )
-        dq_ref[:rows, :] = turn_back(dq, cos, sin).astype(BF16)
-        keep_k[...] = dk[0]
-        keep_v[...] = dv[0]
-        leave[step, :rows, :PAIR] = dk[1].astype(BF16)
-        leave[step, :rows, PAIR:] = dv[1].astype(BF16)
-        dq, dk, dv = attend_back_slot(
-            qs[...], [ks[...]], [vs[...]], dos[...], [stats[2:3], stats[3:4]]
-        )
-        dq_ref[rows:, :] = turn_back(dq, cos, sin).astype(BF16)
-        keep_sk[...] = dk[0]
-        keep_sv[...] = dv[0]
-        leave[step, rows:, :PAIR] = dk[0].astype(BF16)
-        leave[step, rows:, PAIR:] = dv[0].astype(BF16)
-        kv_copy(step).start()
-
     @pl.when(step == PAIRS)
     def _():
         down_ref[...] = down.total()
         up.add2(up_ref)
         out.add2(out_ref)
         down.drain(3, 4, 5, 6, 7)
-        up.drain(0, 1, 2, 3, 4)
-        out.drain(0, 1, 2, 3, 4)
+        up.drain(1, 2, 3, 4)
+        out.drain(1, 2, 3, 4)
         for pair in range(PAIRS):
             kv_copy(pair).wait_send()
 
 
-def back_call(q, kv_own, kv_other, kv_short, d_att, lse, cos, sin, handed, up, out, rows):
+def back_call(q, kv, d_att, lse, cos, sin, handed, rows):
     last = PAIRS - 1
 
     def late(s):
@@ -1079,9 +1236,11 @@
         return pl.BlockSpec(shape, lambda s: (0,) * len(shape))
 
     specs = [
-        pl.BlockSpec(s.block_shape, partial(lambda m, h: m(late(h)), s.index_map))
-        for s in pair_specs(rows)
+        pl.BlockSpec((rows, PAIR), lambda s: (0, late(s))),
+        pl.BlockSpec((rows, PAIR), lambda s: (1, late(s))),
     ]
+    specs += [pl.BlockSpec((rows, PAIR), lambda s: (0, late(s)))] * 4
+    specs += [pl.BlockSpec((SHORT, PAIR), lambda s: (0, late(s)))] * 2
     n = SLOTS * rows
     dr, dc = FF // 16, D // 2
     ur, uc = D // 16, FF // 2
@@ -1106,7 +1265,7 @@
             whole((LEN, PAIR)),
             whole((LEN, PAIR)),
         ]
-        + [ANY] * 6,
+        + [ANY] * 4,
         out_specs=(
             pl.BlockSpec((n, PAIR), lambda s: (0, late(s))),
             pl.BlockSpec((n, PAIR), lambda s: (0, early(s))),
@@ -1121,15 +1280,17 @@
             pltpu.VMEM((4, dr, dc), BF16),
             pltpu.VMEM((3, dr, dc), BF16),
         ]
-        + scatter_scratch(ur, uc, last=False)
-        + scatter_scratch(wr, wc, last=False)
+        + [pltpu.VMEM(half_shape(ur, uc), BF16)]
+        + scatter_scratch(ur, uc, first=False, last=False)
+        + [pltpu.VMEM(half_shape(wr, wc), BF16)]
+        + scatter_scratch(wr, wc, first=False, last=False)
         + [
             pltpu.VMEM((PAIRS, rows + SHORT, 2 * PAIR), BF16),
             pltpu.VMEM((PAIRS, rows + SHORT, 2 * PAIR), BF16),
-            pltpu.VMEM((rows, PAIR), F32),
-            pltpu.VMEM((rows, PAIR), F32),
-            pltpu.VMEM((SHORT, PAIR), F32),
-            pltpu.VMEM((SHORT, PAIR), F32),
+            pltpu.VMEM((2,) + (rows, PAIR), F32),
+            pltpu.VMEM((2,) + (rows, PAIR), F32),
+            pltpu.VMEM((2,) + (SHORT, PAIR), F32),
+            pltpu.VMEM((2,) + (SHORT, PAIR), F32),
             DMA((18,)),
             DMA((18,)),
             DMA((PAIRS,)),
@@ -1140,11 +1301,7 @@
             collective_id=2, has_side_effects=True, vmem_limit_bytes=BIG
         ),
         cost_estimate=cost(40 * D * rows * (LEN + SHORT), 30e6, HEADS * rows * (LEN + SHORT)),
-    )(
-        q, q, kv_own, kv_own, kv_other, kv_other, kv_short, kv_short, d_att, d_att, lse, cos, sin,
-        *handed, *(w.reshape(half_shape(ur, uc)) for w in up),
-        *(w.reshape(half_shape(wr, wc)) for w in out),
-    )
+    )(q, q, *kv, d_att, d_att, lse, cos, sin, *handed)
 
 
 BLOCKS = 3
@@ -1152,7 +1309,7 @@
 
 
 def end_kernel(
-    tok_ref, dmid_ref, hidden_ref, mod_ref, gain_ref, weight_ref, flag_ref,
+    tok_ref, dmid_ref, hidden_ref, mod_ref, gain_ref, weight_ref, lengths,
     dq_any, dk_any, dv_any, up_any, out_any,
     grad_ref, gqkv_ref, gup_ref, gout_ref, late_ref,
     dqkv, hidden_t,
@@ -1249,8 +1406,10 @@
         t = step - BLOCKS
         j = t // 2
         size = tok_ref.shape[0]
-        scale = mod_ref[pl.ds(j, 1), :][:, D : 2 * D]
-        gain = gain_ref[...].astype(F32)
+        swapped = jnp.full((1, D), jnp.where(lengths[1] > lengths[0], 1.0, 0.0))
+        mine = jnp.where(j == 0, swapped, 1.0 - swapped)
+        scale = jnp.where(mine == 0.0, mod_ref[0:1, D : 2 * D], mod_ref[1:2, D : 2 * D])
+        gain = wide_row(gain_ref)
         start = pl.multiple_of(t * size, size)
         d_hidden = nt(dqkv[pl.ds(start, size), :], weight_ref[...])
         x = tok_ref[...].astype(F32)
@@ -1260,8 +1419,6 @@
         hx = col_sum(d_hidden * xhat)
         fx = d_hidden * (1.0 + scale) * gain
         grad_ref[...] = dmid_ref[...] + r * (fx - row_mean(fx) - xhat * row_mean(fx * xhat))
-        flag = flag_ref[...]
-        mine = jnp.where(j == 0, flag, 1.0 - flag)
         shift = col_sum(d_hidden)
         none = jnp.zeros((3, D), F32)
         first, second = mine == 0.0, mine != 0.0
@@ -1299,7 +1456,7 @@
         late_ref[...] = late_came[...]
 
 
-def end_call(tokens, d_mid, hidden, mods, gain, weight, flag, dq, dk, dv, up2, out2, rows):
+def end_call(tokens, d_mid, hidden, mod, gain, weight, lengths, dq, dk, dv, up2, out2, rows):
     n = SLOTS * rows
     size = n // TILES
     r = D // 16
@@ -1330,9 +1487,9 @@
             pl.BlockSpec((size, D), tile),
             whole((n, D)),
             whole((8, 6 * D)),
-            whole((1, D)),
+            whole((D,)),
             whole((D, 3 * D)),
-            whole((1, D)),
+            pl.BlockSpec(memory_space=pltpu.SMEM),
         ]
         + [ANY] * 5,
         out_specs=(
@@ -1370,7 +1527,7 @@
             collective_id=3, has_side_effects=True, vmem_limit_bytes=BIG
         ),
         cost_estimate=cost(4 * n * D * 3 * D, 30e6),
-    )(tokens, d_mid, hidden, mods, gain, weight, flag, dq, dk, dv, up2, out2)
+    )(tokens, d_mid, hidden, mod, gain, weight, lengths, dq, dk, dv, up2, out2)
 
 
 def exact(left, right, over):
@@ -1379,12 +1536,35 @@
     )
 
 
+def exact(left, right, over):
+    return lax.dot_general(
+        left, right, (over, ((), ())), precision=HIGHEST, preferred_element_type=F32
+    )
+
+
 def condition_kernel(
-    place, early_ref, late_ref, table_ref, silu_ref, weight_ref, cond_ref,
+    lengths, early_ref, late_ref, table_ref, silu_ref, weight_ref,
+    qkv_in, out_in, up_in, down_in, sorted_any,
     ada_ref, bias_ref, gcond_ref, gain1_ref, gain2_ref, bd_ref, bu_ref,
+    qkv_ref, out_ref, up_ref, down_ref, natural_any, moved,
 ):
     seq = late_ref.shape[0]
-    me, s = place[2], place[3]
+    me, s = lax.axis_index("span"), lax.axis_index("seq")
+    half = sorted_any.shape[0] // SLOTS
+    moves = [
+        pltpu.make_async_copy(
+            sorted_any.at[pl.ds(j * half, half)],
+            natural_any.at[pl.ds(pl.multiple_of(slot_of(lengths, j) * half, half), half)],
+            moved.at[j],
+        )
+        for j in range(SLOTS)
+    ]
+    for move in moves:
+        move.start()
+    qkv_ref[...] = qkv_in[...]
+    out_ref[...] = out_in[...]
+    up_ref[...] = up_in[...]
+    down_ref[...] = down_in[...]
     early = early_ref[...].reshape(seq, 2, 16, D)
     early = early[:, 0] + early[:, 1]
     late = late_ref[...]
@@ -1393,11 +1573,11 @@
         mods.append(
             [late[:, 2 * k], late[:, 2 * k + 1]] + [early[:, 4 * k + b] for b in range(4)]
         )
-    gain1_ref[...] = col_sum(late[:, 4])
-    gain2_ref[...] = col_sum(early[:, 8])
-    bd_ref[...] = col_sum(early[:, 9])
+    gain1_ref[...] = jnp.sum(late[:, 4], axis=0)
+    gain2_ref[...] = jnp.sum(early[:, 8], axis=0)
+    bd_ref[...] = jnp.sum(early[:, 9], axis=0)
     for f in range(4):
-        bu_ref[:, f * D : (f + 1) * D] = col_sum(early[:, 10 + f])
+        bu_ref[f * D : (f + 1) * D] = jnp.sum(early[:, 10 + f], axis=0)
     own = [jnp.zeros((8, D), F32)] * 6
     row = lax.broadcasted_iota(jnp.int32, (8, seq), 0)
     wanted = (s * SLOTS + row).astype(F32)
@@ -1409,11 +1589,11 @@
     d_silu = jnp.zeros((8, 128), F32)
     for b in range(6):
         cols = slice(b * D, (b + 1) * D)
-        bias_ref[:, cols] = col_sum(mods[0][b]) + col_sum(mods[1][b])
+        bias_ref[cols] = jnp.sum(mods[0][b] + mods[1][b], axis=0)
         d_silu += exact(own[b], weight_ref[:, cols].astype(F32), ((1,), (1,)))
-    v = cond_ref[...]
+    v = table_ref[s]
     sig = 1.0 / (1.0 + jnp.exp(-v))
-    gcond_ref[...] = d_silu * (sig * (1.0 + v * (1.0 - sig)))
+    gcond_ref[...] = (d_silu * (sig * (1.0 + v * (1.0 - sig))))[:SLOTS]
     rows = 128 // seq
     pick = lax.broadcasted_iota(jnp.int32, (rows, 128), 1) == (
         s * rows + lax.broadcasted_iota(jnp.int32, (rows, 128), 0)
@@ -1426,28 +1606,33 @@
             block = jnp.where(me == 0, mods[k][b], mods[k][3 + b])
             total += exact(silu[k], block, ((1,), (0,)))
         ada_ref[:, b * D : (b + 1) * D] = total
-
-
-def condition_call(place, early, late, table, silu, ada_weight, cond):
+    for move in moves:
+        move.wait()
+
+
+def condition_call(lengths, early, late, table, silu, ada_weight, tiles, grad_in):
     seq = late.shape[0]
 
-    def all_of(a):
-        return whole(a.shape)
-
-    outs = ((128 // seq, 3 * D), (1, 6 * D), (8, 128), (1, D), (1, D), (1, D), (1, FF))
+    def all_of(shape):
+        return pl.BlockSpec(shape, lambda i, p: (0,) * len(shape))
+
+    given = (early, late, table, silu, ada_weight) + tiles
+    outs = ((128 // seq, 3 * D), (6 * D,), (SLOTS, 128), (D,), (D,), (D,), (FF,))
+    outs += tuple(t.shape for t in tiles)
     return pl.pallas_call(
         condition_kernel,
         name="condition",
-        out_shape=tuple(jax.ShapeDtypeStruct(o, F32) for o in outs),
+        out_shape=tuple(jax.ShapeDtypeStruct(o, F32) for o in outs + (grad_in.shape,)),
         grid_spec=pltpu.PrefetchScalarGridSpec(
             num_scalar_prefetch=1,
             grid=(1,),
-            in_specs=[all_of(a) for a in (early, late, table, silu, ada_weight, cond)],
-            out_specs=[pl.BlockSpec(o, lambda i, p: (0, 0)) for o in outs],
+            in_specs=[whole(a.shape) for a in given] + [ANY],
+            out_specs=[all_of(o) for o in outs] + [ANY],
+            scratch_shapes=[DMA((SLOTS,))],
         ),
         compiler_params=pltpu.CompilerParams(vmem_limit_bytes=32 << 20),
-        cost_estimate=cost(1e7, 4e6),
-    )(place, early, late, table, silu, ada_weight, cond)
+        cost_estimate=cost(1e7, 12e6),
+    )(lengths, *given, grad_in)
 
 
 def from_peers(array, span):
@@ -1470,72 +1655,60 @@
     seq, span = lax.axis_size("seq"), lax.axis_size("span")
     seq_at, span_at = lax.axis_index("seq"), lax.axis_index("span")
     flat = slots * rows
-    longest = (lengths[1] > lengths[0]).astype(jnp.int32)
-    place = jnp.stack(
-        [longest, 1 - longest, span_at.astype(jnp.int32), seq_at.astype(jnp.int32)]
+    place = jnp.concatenate(
+        [lengths, jnp.stack([span_at.astype(jnp.int32), seq_at.astype(jnp.int32)])]
     )
     fast = seq == 16 and span == 2
     cos, sin = (jnp.asarray(table) for table in rotary(LEN))
-    cond = conditions.astype(F32)
-    asked = jnp.broadcast_to(assignment.astype(F32)[:, None], (slots, 128))
-    own = jnp.concatenate([cond, asked, jnp.zeros((8 - 2 * slots, 128), F32)], axis=0)
-    mod, table, silu_all = modulation_call(own, ada_weight, ada_bias[None], seq)
+    mod, table, silu_all = modulation_call(conditions, assignment, ada_weight, ada_bias, seq)
 
     tokens2 = tokens.reshape(flat, D)
-    gain1, gain2 = norm1_gain[None], norm2_gain[None]
-    q, hidden1, kv_long, kv_tail, tokens_sorted = project_call(
-        place, tokens2, mod, gain1, qkv_weight, cos, sin, rows
-    )
-    pieces = from_peers(kv_long, span)
-    kv_other = pieces[0] if span == 2 else jnp.concatenate(pieces, axis=0)
-    kv_short = kv_tail[:SHORT]
-    sent = [lax.ppermute(kv_short, "span", [(0, i)]) for i in range(1, span)]
-    kv_short = jnp.where(span_at == 0, kv_short, sum(sent[1:], sent[0]))
-    att, lse = attend_call(q, kv_long, kv_other, kv_short, rows)
+    gain1, gain2 = norm1_gain, norm2_gain
+    if fast:
+        q, hidden1, kv, kvx = share_call(tokens2, mod, gain1, qkv_weight, cos, sin, rows)
+        att, lse, q, *kv = attend_sorted_call(lengths, q, kv, kvx, rows)
+    else:
+        q, hidden1, kv_long, kv_tail = project_call(
+            place, tokens2, mod, gain1, qkv_weight, cos, sin, rows
+        )
+        kv_other = jnp.concatenate(from_peers(kv_long, span), axis=0)
+        kv_short = kv_tail[:SHORT]
+        sent = [lax.ppermute(kv_short, "span", [(0, i)]) for i in range(1, span)]
+        kv_short = jnp.where(span_at == 0, kv_short, sum(sent[1:], sent[0]))
+        att, lse = attend_call(q, kv_long, kv_other, kv_short, rows)
     (
-        out, d_mid, d_att, act, d_low, hidden2, d_up, d_attention, d_mod2, d_gain2, d_bd, d_bu,
+        out, d_mid, d_att, act, d_low, hidden2, d_up, d_attention, payload, tokens_sorted,
+        hidden1_sorted,
     ) = feed_call(
-        fast, place, tokens2, att, cotangent.reshape(flat, D), mod, gain2, out_weight, up_weight,
-        up_bias[None], down_weight, down_bias[None], rows,
+        fast, lengths, tokens2, att, cotangent.reshape(flat, D), hidden1, mod, gain2, out_weight,
+        up_weight, up_bias, down_weight, down_bias, rows,
     )
     if fast:
-        payload = jnp.concatenate(
-            [
-                d_mod2[:, :4].reshape(8, D), d_gain2, d_bd, d_bu.reshape(4, D),
-                jnp.zeros((2, D), F32),
-            ],
-            axis=0,
-        )
         early = lax.all_gather(payload, ("seq", "span"), axis=0)
-        down = weight_call(place, act, d_low, 768, "weight_down")
-        uo, um, wo, wm, *handed = weights_call(hidden2, d_up, att, d_attention, *down)
+        a1, b1, out0, up0 = weights_call(act, d_low, att, d_attention, hidden2, d_up)
         dq, dk, dv, grad_down, up2, out2 = back_call(
-            q, kv_long, kv_other, kv_short, d_att, lse, cos, sin, handed, (uo, um), (wo, wm), rows
-        )
-        swapped = longest == 1
-        mods = jnp.where(swapped, mod[jnp.array([1, 0, 2, 3, 4, 5, 6, 7])], mod)
-        flag = jnp.broadcast_to(longest.astype(F32), (1, D))
+            q, kv, d_att, lse, cos, sin, (a1, b1, up0, out0), rows
+        )
         grad_in, grad_qkv, grad_up, grad_out, late = end_call(
-            tokens_sorted, d_mid, hidden1, mods, gain1, qkv_weight, flag, dq, dk, dv, up2, out2,
-            rows,
-        )
-        grad_in = grad_in.reshape(tokens.shape)
-        grad_in = jnp.where(swapped, grad_in[::-1], grad_in)
-        padded = jnp.concatenate([cond, jnp.zeros((8 - slots, 128), F32)], axis=0)
-        grad_ada, ada_bias_sum, grad_cond, gain1_sum, gain2_sum, bd_sum, bu_sum = condition_call(
-            place, early, late, table, silu_all, ada_weight, padded
+            tokens_sorted, d_mid, hidden1_sorted, mod, gain1, qkv_weight, lengths, dq, dk, dv,
+            up2, out2, rows,
+        )
+        (
+            grad_ada, ada_bias_sum, grad_cond, gain1_sum, gain2_sum, bd_sum, bu_sum,
+            grad_qkv, grad_out, grad_up, grad_down, grad_in,
+        ) = condition_call(
+            lengths, early, late, table, silu_all, ada_weight,
+            (grad_qkv, grad_out, grad_up, grad_down), grad_in,
         )
         return (
-            out.reshape(tokens.shape), grad_in, grad_cond[:slots], gain1_sum[0], grad_ada,
-            ada_bias_sum[0], grad_qkv, grad_out, gain2_sum[0], grad_up, bu_sum[0], grad_down,
-            bd_sum[0],
+            out.reshape(tokens.shape), grad_in.reshape(tokens.shape), grad_cond, gain1_sum,
+            grad_ada, ada_bias_sum, grad_qkv, grad_out, gain2_sum, grad_up, bu_sum, grad_down,
+            bd_sum,
         )
     grad_down = weight_gradient(act, d_low)
     grad_up = weight_gradient(hidden2, d_up)
     grad_out = weight_gradient(att, d_attention)
-    early = gather_all(
-        jnp.concatenate([d_mod2[:, :4].reshape(-1), d_gain2[0], d_bd[0], d_bu[0]])
-    )
+    early = gather_all(payload[:14].reshape(-1))
 
     dq, dk, dv, dkx, dvx, dks, dvs = attend_back_call(
         place, q, kv_long, kv_other, kv_short, d_att, lse, cos, sin, rows
@@ -1585,7 +1758,7 @@
     wanted = lax.dynamic_slice_in_dim(picker, seq_at * slots, slots, 1)
     own_mods = exact(wanted, d_mods, (((0,), (0,)), ((), ())))
     d_silu = exact(own_mods, ada_weight.astype(F32), (((1,), (1,)), ((), ())))
-    grad_cond = jax.vjp(jax.nn.silu, cond)[1](d_silu)[0]
+    grad_cond = jax.vjp(jax.nn.silu, conditions.astype(F32))[1](d_silu)[0]
     return (
         out.reshape(tokens.shape),
         grad_in.reshape(tokens.shape),

time: 261 us -> 232 us (0.89)
  other arithmetic: 13.3 us -> 0 us
  local copies, waits for them, and re-layouts: 18.6 us -> 11 us
  Pallas kernels: 210 us -> 206 us
    select_n x3 -> x0, other arithmetic: 7.49 us -> none  [the longest x1 5.01 us: shards(): grad_in = jnp.where(swapped, grad_in[::-1], grad_in)]
    pallas_call x1, Pallas kernels: 46.3 us -> 41.5 us  [back_call(): pl.pallas_call(back_kernel, name='attend_back', grid=(PAIRS + 1,), out_sh...]
    broadcast_in_dim x8 -> x0, local copies, waits for them, and re-layouts: 4.34 us -> none  [the longest x2 1.85 us: shards(): gain1, gain2 = (norm1_gain[None], norm2_gain[None])]
    pallas_call x5 -> x0, other arithmetic: 3.85 us -> none  [the longest x4 2.46 us: condition_call(): pl.pallas_call(condition_kernel, name='condition', out_shape=tuple((jax.S...]
    slice x4 -> x0, local copies, waits for them, and re-layouts: 3.7 us -> none  [the longest x1 1.31 us: shards(): longest = (lengths[1] > lengths[0]).astype(jnp.int32)]
    unnamed x38 -> x28, local copies, waits for them, and re-layouts: 7.35 us -> 11 us
    pallas_call x4 -> x3, Pallas kernels: 69.1 us -> 66.8 us  [the longest x1 35.2 us: weights_call(): pl.pallas_call(weights_kernel, name='weights', grid=(14,), out_shape=tupl...]
  transfers between devices with their start and end apart: 3 -> 1, of which waited for: 0 -> 0; matrix products, arithmetic and copies ran while one was open for 4% -> 0% of each run, Pallas kernels for 50% -> 52%
where the time goes in v3:
time: 232 us; the launch traced here: 231 us
  Pallas kernels  206 us (89%)
  between operations  14.2 us (6%)
  local copies, waits for them, and re-layouts  11 us (5%)
    pallas_call x1, Pallas kernels, end_call(): pl.pallas_call(end_kernel, name='end', grid=(BLOCKS + TILES,), out_shape=...  42.5 us
    pallas_call x1, Pallas kernels, back_call(): pl.pallas_call(back_kernel, name='attend_back', grid=(PAIRS + 1,), out_sh...  41.5 us
    pallas_call x1, Pallas kernels, feed_call(): pl.pallas_call(partial(feed_kernel, halves), name='feed', out_shape=(jax....  37.6 us
    pallas_call x1, Pallas kernels, weights_call(): pl.pallas_call(weights_kernel, name='weights', grid=(14,), out_shape=tupl...  35.2 us
    pallas_call x1, Pallas kernels, attend_sorted_call(): pl.pallas_call(attend_sorted_kernel, name='attend', out_shape=(jax.ShapeD...  18.4 us
    pallas_call x1, Pallas kernels, share_call(): pl.pallas_call(share_kernel, name='project', grid=(steps,), out_shape=(ja...  13.2 us
    unnamed x28, local copies, waits for them, and re-layouts  11 us
    pallas_call x1, Pallas kernels, modulation_call(): pl.pallas_call(partial(modulation_kernel, n), name='modulation', out_shap...  11 us
  transfers between devices with their start and end apart: 1, of which 0 were waited for; matrix products, arithmetic and copies ran while one was open for 0% of the time, Pallas kernels for 52%

profile of v3, /device:TPU:0, one launch (start us, length us, event | category | flops | bytes accessed | tf_op | source)
XLA Modules:
  0.0 231.2 jit_solution(16984963324524784369)
XLA Ops:
  7.2 0.0 all-gather.3.cloned.1.call-start
  7.2 0.0 copy-start
  7.2 1.3 copy-done
  8.5 0.7 copy-done.9
  9.2 0.7 copy-done.11
  9.9 0.7 copy-done.12
  10.5 11.0 %modulation.1 = (f32[8,4608]{1,0:T(8,128)S(1)}, f32[16,8,128]{2,1,0:T(8,128)S(1)}, f32[2,16,128]{2,1,0:T(8,128)S(1)}) custom-call(bf16[2,128]{1,0:T(2,128)(2,1)S(1)} %copy-done.11, s32[2]{0:T(128)S(1)} %copy-done.12, bf16[128,4608]{1,0:T(8,128)(2,1)S(1)} %copy-done, bf16[4608]{0:T(1024)(128)(2,1)S(1)} %copy-done.9), custom_call_target="tpu_custom_call" | custom-call | flops 10000000 | bytes 2000000 | tf_op jit(solution)/shard_map/modulation/pallas_call | solution.py:155
  21.5 0.7 copy-done.13
  22.2 13.2 %project.1 = (bf16[1024,768]{1,0:T(8,128)(2,1)}, bf16[1024,768]{1,0:T(8,128)(2,1)}, bf16[1024,1536]{1,0:T(8,128)(2,1)}, bf16[1024,1536]{1,0:T(8,128)(2,1)}) custom-call(bf16[1024,768]{1,0:T(8,128)(2,1)} %bitcast.7, f32[8,4608]{1,0:T(8,128)} %copy-done.13, bf16[768]{0:T(1024)(128)(2,1)} %gain_ref.5, bf16[768,2304]{1,0:T(8,128)(2,1)} %weight_ref.6, ...), custom_call_target="tpu_custom_call" | custom-call | flops 3623878656 | bytes 14000000 | tf_op jit(solution)/shard_map/project/pallas_call | solution.py:743
  35.4 18.4 %attend.1 = (bf16[1024,768]{1,0:T(8,128)(2,1)}, f32[6,4,512]{2,1,0:T(4,128)}, bf16[1024,768]{1,0:T(8,128)(2,1)}, bf16[512,768]{1,0:T(8,128)(2,1)}, bf16[512,768]...) custom-call(s32[2]{0:T(128)} %lengths.5, ...), custom_call_target="tpu_custom_call" | custom-call | flops 7247757312 | bytes 16000000 | tf_op jit(solution)/shard_map/attend/pallas_call | solution.py:811
  53.7 37.6 %feed.1 = (bf16[1024,768]{1,0:T(8,128)(2,1)}, f32[1024,768]{1,0:T(8,128)}, bf16[1024,768]{1,0:T(8,128)(2,1)}, bf16[1024,3072]{1,0:T(8,128)(2,1)}, bf16[1024,768]...) custom-call(s32[2]{0:T(128)} %lengths.5, ...), custom_call_target="tpu_custom_call" | custom-call | flops 21743271936 | bytes 40000000 | tf_op jit(solution)/shard_map/feed/pallas_call | solution.py:508
  91.3 0.0 all-gather.3.cloned.1.call-update
  91.4 35.2 %weights.1 = (bf16[2,2,192,384]{3,2,1,0:T(8,128)(2,1)}, bf16[2,2,192,384]{3,2,1,0:T(8,128)(2,1)}, bf16[4,2,2,48,384]{4,3,2,1,0:T(8,128)(2,1)}, bf16[4,2,2,48,1536]{4,3,2,1,0:T(8,128)(2,1)}) custom-call(bf16[1024,3072]{1,0:T(8,128)(2,1)} %get-tuple-element.87.act_ref, bf16[1024,768]{1,0:T(8,128)(2,1)} %get-tuple-element.88.dlow_ref, ...), custom_call_target="tpu_custom_call" | custom-call | flops 10871635968 | bytes 30000000 | tf_op jit(solution)/shard_map/weights/pallas_call | solution.py:1081
  126.6 41.5 %attend_back.1 = (bf16[1024,768]{1,0:T(8,128)(2,1)}, bf16[1024,768]{1,0:T(8,128)(2,1)}, bf16[1024,768]{1,0:T(8,128)(2,1)}, f32[192,384]{1,0:T(8,128)}, bf16[4,48...) custom-call(bf16[1024,768]{1,0:T(8,128)(2,1)} %get-tuple-element.78.ql.qs, bf16[1024,768]{1,0:T(8,128)(2,1)} %get-tuple-element.78.ql.qs, ...), custom_call_target="tpu_custom_call" | custom-call | flops 18119393280 | bytes 30000000 | tf_op jit(solution)/shard_map/attend_back/pallas_call | solution.py:1248
  168.2 0.0 copy-start.1
  168.2 42.5 %end.1 = (f32[1024,768]{1,0:T(8,128)}, f32[48,1152]{1,0:T(8,128)}, f32[48,1536]{1,0:T(8,128)}, f32[48,384]{1,0:T(8,128)}, f32[16,8,768]{2,1,0:T(8,128)}) custom-call(bf16[1024,768]{1,0:T(8,128)(2,1)} %get-tuple-element.75.tok_ref, f32[1024,768]{1,0:T(8,128)} %get-tuple-element.76.dmid_ref, bf16[1024,768]{1,0:T(8,128)(2,1)} %get-tuple-element.77.hidden_ref, ...), custom_call_target="tpu_custom_call" | custom-call | flops 7247757312 | bytes 30000000 | tf_op jit(solution)/shard_map/end/pallas_call | solution.py:1474
  210.7 0.0 all-gather.3.cloned.1.call-done
  210.7 1.9 copy-done.2
  212.6 1.4 copy-done.3
  214.0 1.0 copy-done.4
  215.0 1.0 copy-done.6
  216.0 0.9 copy-done.7
  216.9 0.9 copy-done.8
  217.8 6.5 %condition.1 = (f32[8,2304]{1,0:T(8,128)}, f32[4608]{0:T(1024)}, f32[2,128]{1,0:T(2,128)}, f32[768]{0:T(1024)}, f32[768]{0:T(1024)}, /*index=5*/f32[768]{0:T(102...) custom-call(s32[2]{0:T(128)S(1)} %copy-done.10, ...), custom_call_target="tpu_custom_call" | custom-call | flops 10000000 | bytes 12000000 | tf_op jit(solution)/shard_map/condition/pallas_call | solution.py:1622
  (15 shorter events, 0.0 us)
Async XLA Ops:
  7.2 203.5 %all-gather.3.cloned.1.call-start = ((), (), s32[]{:S(2)}) async-start(), calls=%async_computation | async-start | bytes 1622016 | tf_op jit(solution)/shard_map/all_gather | solution.py:1687
  7.2 1.3 copy-start
  8.5 0.7 copy-start.9
  9.2 0.7 copy-start.11
  9.9 0.7 copy-start.12
  21.5 0.7 copy-start.13
  168.2 42.5 %copy-start.1 = (bf16[128,4608]{1,0:T(8,128)(2,1)S(1)}, bf16[128,4608]{1,0:T(8,128)(2,1)}, u32[]{:S(2)}) copy-start(bf16[128,4608]{1,0:T(8,128)(2,1)} %weight_ref.7) | copy-start | bytes 3538948
  168.2 42.5 %copy-start.5 = (f32[192,384]{1,0:T(8,128)S(1)}, f32[192,384]{1,0:T(8,128)}, u32[]{:S(2)}) copy-start(f32[192,384]{1,0:T(8,128)} %get-tuple-element.107.down_in) | copy-start | bytes 884740
  168.2 42.5 %copy-start.10 = (s32[2]{0:T(128)S(1)}, s32[2]{0:T(128)}, u32[]{:S(2)}) copy-start(s32[2]{0:T(128)} %lengths.5) | copy-start | bytes 28
  210.7 1.9 copy-start.2
  212.6 1.4 copy-start.3
  214.0 1.0 copy-start.4
  215.0 1.0 copy-start.6
  216.0 0.9 copy-start.7
  216.9 0.9 copy-start.8
Sparse Core Ops, SparseCore 0:
  91.5 61.0 all-gather.2

commit v4 on v3

--- a/solution.py
+++ b/solution.py
@@ -169,7 +169,7 @@
             pltpu.SemaphoreType.DMA,
         ],
         compiler_params=pltpu.CompilerParams(
-            collective_id=0, has_side_effects=True, vmem_limit_bytes=16 << 20
+            collective_id=0, has_side_effects=True, vmem_limit_bytes=BIG
         ),
         cost_estimate=cost(1e7, 2e6),
     )(cond, assignment, ada_weight, ada_bias)
@@ -241,8 +241,8 @@
 
 def attend_slot(q, keys, values):
     outs, stats = [], []
-    for head, qh in enumerate(heads_of(q)):
-        scores = [nt(k, qh) for k in keys]
+    all_scores = [[nt(k, qh) for k in keys] for qh in heads_of(q)]
+    for head, scores in enumerate(all_scores):
         top = jnp.max(scores[0], axis=0, keepdims=True)
         for s in scores[1:]:
             top = jnp.maximum(top, jnp.max(s, axis=0, keepdims=True))
@@ -306,39 +306,44 @@
     )(q, q, kv_own, kv_own, kv_other, kv_other, kv_short, kv_short)
 
 
-def attend_back_slot(q, keys, values, d_out, lse):
-    d_keys, d_values = [None] * len(keys), [None] * len(keys)
+def attend_back_slot(q, keys, values, d_out, out, lse, between=None):
+    count = len(keys)
+    d_keys, d_values = [None] * count, [None] * count
     d_query = []
     q_heads, d_heads = heads_of(q), heads_of(d_out)
+    inner = (d_out.astype(F32) * out.astype(F32)).T
+    all_scores = [[nt(k, qh) for k in keys] for qh in q_heads]
+    all_d_probs = [[nt(v, dh) for v in values] for dh in d_heads]
     for head in range(2):
+        if head == 1 and between is not None:
+            between()
         qh, dh = q_heads[head], d_heads[head]
-        probs = [jnp.exp2(nt(k, qh) * (0.125 * LOG2E) - lse[head]) for k in keys]
-        d_probs = [nt(v, dh) for v in values]
-        inner = None
-        for p, dp in zip(probs, d_probs):
-            part = col_sum(p * dp)
-            inner = part if inner is None else inner + part
+        delta = col_sum(inner[head * HEAD : (head + 1) * HEAD])
+        scores, d_probs = all_scores[head], all_d_probs[head]
         dq = None
-        for i in range(len(keys)):
-            d_scores = (probs[i] * (d_probs[i] - inner) * 0.125).astype(BF16)
-            dv = nn(probs[i].astype(BF16), dh)
+        for i in range(count):
+            probs = jnp.exp2(scores[i] * (0.125 * LOG2E) - lse[head])
+            d_scores = (probs * (d_probs[i] - delta)).astype(BF16)
+            dv = nn(probs.astype(BF16), dh)
             dk = nn(d_scores, qh)
             part = tn(keys[i], d_scores)
             dq = part if dq is None else dq + part
             d_values[i] = dv if head == 0 else d_values[i] + dv
             d_keys[i] = dk if head == 0 else d_keys[i] + dk
         d_query.append(dq[head * HEAD : (head + 1) * HEAD])
-    return jnp.concatenate(d_query, axis=0).T, d_keys, d_values
+    d_keys = [dk * 0.125 for dk in d_keys]
+    return (jnp.concatenate(d_query, axis=0) * 0.125).T, d_keys, d_values
 
 
 def attend_back_kernel(
-    place, ql, qs, ko, vo, kx, vx, ks, vs, dol, dos, lse, cos, sin,
+    place, ql, qs, ko, vo, kx, vx, ks, vs, dol, dos, al, as_, lse, cos, sin,
     dq_ref, dko, dvo, dkx, dvx, dks, dvs,
 ):
     rows = ql.shape[0]
     stats = lse[0]
     dq, dk, dv = attend_back_slot(
-        ql[...], [ko[...], kx[...]], [vo[...], vx[...]], dol[...], [stats[0:1], stats[1:2]]
+        ql[...], [ko[...], kx[...]], [vo[...], vx[...]], dol[...], al[...],
+        [stats[0:1], stats[1:2]],
     )
     dq_ref[:rows, :] = turn_back(dq, cos[...], sin[...]).astype(BF16)
     dko[...] = dk[0]
@@ -346,14 +351,14 @@
     dkx[...] = dk[1].astype(BF16)
     dvx[...] = dv[1].astype(BF16)
     dq, dk, dv = attend_back_slot(
-        qs[...], [ks[...]], [vs[...]], dos[...], [stats[2:3], stats[3:4]]
+        qs[...], [ks[...]], [vs[...]], dos[...], as_[...], [stats[2:3], stats[3:4]]
     )
     dq_ref[rows:, :] = turn_back(dq, cos[...], sin[...]).astype(BF16)
     dks[...] = dk[0]
     dvs[...] = dv[0]
 
 
-def attend_back_call(place, q, kv_own, kv_other, kv_short, d_att, lse, cos, sin, rows):
+def attend_back_call(place, q, kv_own, kv_other, kv_short, d_att, att, lse, cos, sin, rows):
     specs = [
         pl.BlockSpec(s.block_shape, partial(lambda m, h, o: m(h), s.index_map))
         for s in pair_specs(rows)
@@ -378,6 +383,8 @@
             + [
                 pl.BlockSpec((rows, PAIR), lambda h, o: (0, h)),
                 pl.BlockSpec((rows, PAIR), lambda h, o: (1, h)),
+                pl.BlockSpec((rows, PAIR), lambda h, o: (0, h)),
+                pl.BlockSpec((rows, PAIR), lambda h, o: (1, h)),
                 pl.BlockSpec((1, 4, rows), lambda h, o: (h, 0, 0)),
                 pl.BlockSpec((rows, PAIR), lambda h, o: (o[2], 0)),
                 pl.BlockSpec((rows, PAIR), lambda h, o: (o[2], 0)),
@@ -396,7 +403,7 @@
         cost_estimate=cost(40 * D * rows * (LEN + SHORT), 16e6, HEADS * rows * (LEN + SHORT)),
     )(
         place, q, q, kv_own, kv_own, kv_other, kv_other, kv_short, kv_short,
-        d_att, d_att, lse, cos, sin,
+        d_att, d_att, att, att, lse, cos, sin,
     )
 
 
@@ -876,6 +883,8 @@
         x, y, z = self.x, self.y, self.z
         if i == 0:
             src, dst, peer = self.other, self.came0, self.core_peer
+        elif i >= 8:
+            src, dst, peer = self.other.at[i - 8], self.came0.at[i - 8], self.core_peer
         elif i == 1:
             src, dst, peer = self.own.at[0:2, :, 1 - x], self.a1, self.x_peer
         elif i == 2:
@@ -909,9 +918,7 @@
         for i in which:
             self.copy(i).wait_send()
 
-    def add0(self):
-        self.arrive(0)
-
+    def merge0(self):
         def body(i, _):
             z, y, x = i // 4, lax.rem(i // 2, 2), lax.rem(i, 2)
             self.own[z, y, x] = add_low(self.own[z, y, x], self.came0[z, y, x])
@@ -951,7 +958,8 @@
         self.start(0)
 
     def scatter1(self):
-        self.add0()
+        self.arrive(0)
+        self.merge0()
         self.start(1, 2)
 
     def scatter2(self):
@@ -967,172 +975,51 @@
     return (4, 2, 2, rows, cols)
 
 
-def scatter_scratch(rows, cols, first=True, middle=True, last=True):
-    shapes = []
-    if first:
-        shapes += [half_shape(rows, cols)] * 2
-    if first or middle:
-        shapes += [(2, 2, rows, cols)] * 2
-    if middle or last:
-        shapes += [(4, rows, cols)]
-    if last:
-        shapes += [(3, rows, cols)]
-    return [pltpu.VMEM(shape, BF16) for shape in shapes]
-
-
 ANY = pl.BlockSpec(memory_space=pl.ANY)
 DMA = pltpu.SemaphoreType.DMA
 
 
-def weights_kernel(
-    act_ref, dlow_ref, att_ref, dattn_ref, h_ref, dup_ref,
-    a_ref, b_ref, out_ref, up_ref,
-    other, own, came0, a1, b1, out_other, out_came, up_other, up_came, send, recv,
+FIRST = 9
+ROUNDS = PAIRS // 2
+WIDE = 3 * PAIR
+
+
+def middle_kernel(
+    act_ref, dlow_ref, att_ref, dattn_ref, h_ref, dup_ref, hid1_ref, payload_ref,
+    ql, qs, ko, vo, kx, vx, ks, vs, dol, dos, al, as_, lse, cos_ref, sin_ref,
+    dq_ref, dk_ref, dv_ref, down_ref, out_ref, up_ref, ra_ref, rb_ref, rown_ref, early_ref,
+    down_other, down_own, down_came, down_a, down_b, down2, down3,
+    out_other, out_own, out_came, out_a, out_b, out2, out3,
+    up_other, up_own, up_came, up_a, up_b, up2,
+    round_came, round_a, round_b, d_round, keep_q,
+    leave, come, keep_k, keep_v, keep_sk, keep_sv, early_came, early_sum, early_all,
+    send, recv, send_kv, recv_kv, send_early, recv_early,
 ):
     step = pl.program_id(0)
-    down = Scatter(send, recv, 0, other=other, own=own, came0=came0, a1=a1, b1=b1)
-    out = Scatter(send, recv, 3, other=out_other, own=out_ref, came0=out_came)
-    up = Scatter(send, recv, 4, other=up_other, own=up_ref, came0=up_came)
-
-    @pl.when(step == 0)
-    def _():
-        greet(plane_peers())
-
-    @pl.when(step == 8)
-    def _():
-        down.scatter1()
-
-    @pl.when(step == 10)
-    def _():
-        out.add0()
-
-    @pl.when(step < 8)
-    def _():
-        value = tn(act_ref[...], dlow_ref[...]).astype(BF16)
-        value = value.reshape((2, 2) + own.shape[3:])
-
-        @pl.when(step < 4)
-        def _():
-            other[step] = value
-
-        @pl.when(step >= 4)
-        def _():
-            own[step - 4] = value
-
-    @pl.when(step == 3)
-    def _():
-        down.scatter0()
-
-    @pl.when(jnp.logical_and(step >= 8, step < 10))
-    def _():
-        value = tn(att_ref[...], dattn_ref[...]).astype(BF16).reshape(out_ref.shape)
-
-        @pl.when(step == 8)
-        def _():
-            out_other[...] = value
-            out.scatter0()
-
-        @pl.when(step == 9)
-        def _():
-            out_ref[...] = value
-
-    @pl.when(step >= 10)
-    def _():
-        value = tn(h_ref[...], dup_ref[...]).astype(BF16)
-        value = value.reshape((2,) + up_ref.shape[1:])
-        z = lax.rem(step, 2) * 2
-
-        @pl.when(step < 12)
-        def _():
-            up_other[pl.ds(z, 2)] = value
-
-        @pl.when(step >= 12)
-        def _():
-            up_ref[pl.ds(z, 2)] = value
-
-    @pl.when(step == 11)
-    def _():
-        up.scatter0()
-
-    @pl.when(step == 13)
-    def _():
-        up.add0()
-        down.add1(a_ref, b_ref)
-        down.drain(0, 1, 2)
-        out.drain(0)
-        up.drain(0)
-
-
-def weights_call(act, d_low, att, d_attention, hidden, d_up):
-    n = hidden.shape[0]
-    half = FF // 2
-    dr, dc = FF // 16, D // 2
-    ur, wr = D // 16, D // 16
-    down, up, out = half_shape(dr, dc), half_shape(ur, half), half_shape(wr, dc)
-
-    def clamp(s, low, high):
-        return jnp.minimum(jnp.maximum(s, low), high)
-
-    def fixed(shape):
-        return whole(shape)
-
-    handed = (2, 2, dr, dc)
-    shapes = (handed, handed, out, up)
-    return pl.pallas_call(
-        weights_kernel,
-        name="weights",
-        grid=(14,),
-        out_shape=tuple(jax.ShapeDtypeStruct(o, BF16) for o in shapes),
-        in_specs=[
-            pl.BlockSpec((n, D), lambda s: (0, jnp.where(s < 8, lax.rem(s, 4), 3))),
-            pl.BlockSpec((n, dc), lambda s: (0, jnp.where(s < 4, 0, 1))),
-            fixed((n, D)),
-            pl.BlockSpec((n, dc), lambda s: (0, jnp.where(s < 9, 0, 1))),
-            pl.BlockSpec((n, dc), lambda s: (0, jnp.where(s < 10, 0, lax.rem(s, 2)))),
-            pl.BlockSpec((n, half), lambda s: (0, jnp.where(s < 12, 0, 1))),
-        ],
-        out_specs=tuple(fixed(o) for o in shapes),
-        scratch_shapes=[
-            pltpu.VMEM(down, BF16),
-            pltpu.VMEM(down, BF16),
-            pltpu.VMEM(down, BF16),
-            pltpu.VMEM(handed, BF16),
-            pltpu.VMEM(handed, BF16),
-            pltpu.VMEM(out, BF16),
-            pltpu.VMEM(out, BF16),
-            pltpu.VMEM(up, BF16),
-            pltpu.VMEM(up, BF16),
-            DMA((5,)),
-            DMA((5,)),
-        ],
-        compiler_params=pltpu.CompilerParams(
-            collective_id=1, has_side_effects=True, vmem_limit_bytes=BIG
-        ),
-        cost_estimate=cost(2 * n * D * (2 * FF + D), 30e6),
-    )(act, d_low, att, d_attention, hidden, d_up)
-
-
-def back_kernel(
-    ql, qs, ko, vo, kx, vx, ks, vs, dol, dos, lse, cos_ref, sin_ref,
-    a_in, b_in, up_in, out_in,
-    dq_ref, dk_ref, dv_ref, down_ref, up_ref, out_ref,
-    down_a, down_b, down2, down3,
-    up_own, up_a, up_b, up2,
-    out_own, out_a, out_b, out2,
-    leave, come, keep_k, keep_v, keep_sk, keep_sv,
-    send, recv, send_kv, recv_kv, local,
-):
-    step = pl.program_id(0)
-    me = lax.axis_index("span")
+    s, me = lax.axis_index("seq"), lax.axis_index("span")
     rows = ql.shape[0]
-    down = Scatter(send, recv, 0, a1=down_a, b1=down_b, came2=down2, came3=down3)
-    up = Scatter(send, recv, 8, own=up_own, a1=up_a, b1=up_b, came2=up2)
-    out = Scatter(send, recv, 13, own=out_own, a1=out_a, b1=out_b, came2=out2)
-    loads = [
-        pltpu.make_async_copy(src, dst, local.at[i])
-        for i, (src, dst) in enumerate(
-            [(a_in, down_a), (b_in, down_b), (up_in, up_own), (out_in, out_own)]
-        )
+    down = Scatter(
+        send, recv, 0, other=down_other, own=down_own, came0=down_came, a1=down_a, b1=down_b,
+        came2=down2, came3=down3,
+    )
+    out = Scatter(
+        send, recv, 12, other=out_other, own=out_own, came0=out_came, a1=out_a, b1=out_b,
+        came2=out2, came3=out3,
+    )
+    up = Scatter(
+        send, recv, 20, other=up_other, own=up_own, came0=up_came, a1=up_a, b1=up_b, came2=up2,
+    )
+    part, wide = hid1_ref.shape[1] // 16, WIDE
+    rounds = [
+        Scatter(
+            send, recv, 28 + 3 * k,
+            other=down_other.at[:, :, :, k * part : (k + 1) * part],
+            own=rown_ref.at[k - 1] if k else up_other.at[:, :, :, :, :wide],
+            came0=round_came.at[k],
+            a1=round_a,
+            b1=round_b,
+        )
+        for k in range(ROUNDS)
     ]
     cos = cos_ref[pl.ds(pl.multiple_of(me * rows, rows), rows), :]
     sin = sin_ref[pl.ds(pl.multiple_of(me * rows, rows), rows), :]
@@ -1147,55 +1034,141 @@
             device_id_type=MESH,
         )
 
-    @pl.when(step == 0)
-    def _():
-        for load in loads:
-            load.start()
-        greet(plane_peers() + line_peers())
-        loads[0].wait()
-        loads[1].wait()
-        down.start(3, 4)
-
-    @pl.when(step == 1)
-    def _():
-        loads[2].wait()
-        loads[3].wait()
-        out.start(1, 2)
-        up.start(1, 2)
-
-    @pl.when(step == 2)
-    def _():
-        down.scatter3()
-
-    @pl.when(step == 5)
-    def _():
-        up.scatter2()
+    def early_copy(k):
+        if k == 0:
+            src, dst, peer = payload_ref, early_came, {"span": 1 - me}
+        else:
+            src, dst, peer = early_sum, early_all.at[s], {"seq": lax.rem(s + k, 16)}
+        return pltpu.make_async_remote_copy(
+            src_ref=src,
+            dst_ref=dst,
+            send_sem=send_early.at[k],
+            recv_sem=recv_early.at[k],
+            device_id=peer,
+            device_id_type=MESH,
+        )
+
+    def at(number):
+        return pl.when(step == number)
+
+    @at(0)
+    def _():
+        greet([{"span": 1 - me}] + [{"seq": lax.rem(s + k, 16)} for k in range(1, 16)])
+        early_copy(0).start()
+
+    @at(3)
+    def _():
+        early_copy(0).wait_recv()
+        early_sum[...] = (payload_ref[...] + early_came[...]).astype(BF16)
+        for k in range(1, 16):
+            early_copy(k).start()
+        early_all[s] = early_sum[...]
+
+    @at(2)
+    def _():
+        out.scatter1()
+
+    @at(4)
+    def _():
         out.scatter2()
 
-    @pl.when(step < PAIRS)
-    def _():
+    @at(6)
+    def _():
+        down.arrive(8, 9, 10, 11)
+        down.merge0()
+        down.start(1, 2)
+        out.scatter3()
+
+    @at(FIRST + 1)
+    def _():
+        up.scatter1()
+
+    @at(FIRST + 2)
+    def _():
+        down.drain(8, 9, 10, 11)
+        up.drain(0)
+        down.scatter2()
+
+    @at(FIRST + 5)
+    def _():
+        rounds[0].scatter1()
+
+    def between():
+        @at(FIRST + 4)
+        def _():
+            down.scatter3()
+
+        @at(FIRST + 5)
+        def _():
+            up.scatter2()
+
+    @at(0)
+    def _():
+        value = tn(att_ref[...], dattn_ref[...]).astype(BF16)
+        out_other[...] = value[:, : D // 2].reshape(out_own.shape)
+        out_own[...] = value[:, D // 2 :].reshape(out_own.shape)
+        out.scatter0()
+
+    @pl.when(jnp.logical_and(step >= 1, step < 5))
+    def _():
+        value = tn(act_ref[...], dlow_ref[...]).astype(BF16)
+        shape = down_own.shape[1:]
+        down_other[step - 1] = value[:, : D // 2].reshape(shape)
+        down_own[step - 1] = value[:, D // 2 :].reshape(shape)
+
+        for m in range(4):
+            @at(m + 1)
+            def _():
+                down.start(8 + m)
+
+    @pl.when(jnp.logical_and(step >= 5, step < FIRST))
+    def _():
+        value = tn(h_ref[...], dup_ref[...]).astype(BF16)
+        value = value.reshape(up_own.shape[:4] + (CHUNK,))
+        cols = pl.ds(pl.multiple_of(lax.rem(step - 5, 2) * CHUNK, CHUNK), CHUNK)
+
+        @pl.when(step < 7)
+        def _():
+            up_other[:, :, :, :, cols] = value
+
+        @pl.when(step >= 7)
+        def _():
+            up_own[:, :, :, :, cols] = value
+
+    @at(6)
+    def _():
+        up.scatter0()
+
+    @pl.when(jnp.logical_and(step >= FIRST, step < FIRST + PAIRS))
+    def _():
+        pair = step - FIRST
         stats = lse[0]
         dq, dk, dv = attend_back_slot(
-            ql[...], [ko[...], kx[...]], [vo[...], vx[...]], dol[...], [stats[0:1], stats[1:2]]
-        )
-        dq_ref[:rows, :] = turn_back(dq, cos, sin).astype(BF16)
-        keep_k[lax.rem(step, 2)] = dk[0]
-        keep_v[lax.rem(step, 2)] = dv[0]
-        leave[step, :rows, :PAIR] = dk[1].astype(BF16)
-        leave[step, :rows, PAIR:] = dv[1].astype(BF16)
+            ql[...], [ko[...], kx[...]], [vo[...], vx[...]], dol[...], al[...],
+            [stats[0:1], stats[1:2]], between,
+        )
+        dq = turn_back(dq, cos, sin).astype(BF16)
+        dq_ref[:rows, :] = dq
+        keep_q[lax.rem(pair, 2), :rows, :] = dq
+        keep_k[lax.rem(pair, 2)] = dk[0]
+        keep_v[lax.rem(pair, 2)] = dv[0]
+        leave[pair, :rows, :PAIR] = dk[1].astype(BF16)
+        leave[pair, :rows, PAIR:] = dv[1].astype(BF16)
         dq, dk, dv = attend_back_slot(
-            qs[...], [ks[...]], [vs[...]], dos[...], [stats[2:3], stats[3:4]]
-        )
-        dq_ref[rows:, :] = turn_back(dq, cos, sin).astype(BF16)
-        keep_sk[lax.rem(step, 2)] = dk[0]
-        keep_sv[lax.rem(step, 2)] = dv[0]
-        leave[step, rows:, :PAIR] = dk[0].astype(BF16)
-        leave[step, rows:, PAIR:] = dv[0].astype(BF16)
-        kv_copy(step).start()
-
-    @pl.when(step > 0)
-    def _():
-        pair = step - 1
+            qs[...], [ks[...]], [vs[...]], dos[...], as_[...], [stats[2:3], stats[3:4]]
+        )
+        dq = turn_back(dq, cos, sin).astype(BF16)
+        dq_ref[rows:, :] = dq
+        keep_q[lax.rem(pair, 2), rows:, :] = dq
+        keep_sk[lax.rem(pair, 2)] = dk[0]
+        keep_sv[lax.rem(pair, 2)] = dv[0]
+        leave[pair, rows:, :PAIR] = dk[0].astype(BF16)
+        leave[pair, rows:, PAIR:] = dv[0].astype(BF16)
+        kv_copy(pair).start()
+
+    @pl.when(step > FIRST)
+    def _():
+        pair = step - FIRST - 1
         kv_copy(pair).wait_recv()
         dk = keep_k[lax.rem(pair, 2)] + come[pair, :rows, :PAIR].astype(F32)
         dk_ref[:rows, :] = turn_back(dk, cos, sin).astype(BF16)
@@ -1204,147 +1177,176 @@
         zero = jnp.zeros((SHORT, PAIR), F32)
         sk = keep_sk[lax.rem(pair, 2)] + come[pair, rows:, :PAIR].astype(F32)
         sk = jnp.where(me == 0, turn_back(sk, cos[:SHORT], sin[:SHORT]), zero)
-        sv = jnp.where(me == 0, keep_sv[lax.rem(pair, 2)] + come[pair, rows:, PAIR:].astype(F32), zero)
+        sv = keep_sv[lax.rem(pair, 2)] + come[pair, rows:, PAIR:].astype(F32)
         dk_ref[rows : rows + SHORT, :] = sk.astype(BF16)
-        dv_ref[rows : rows + SHORT, :] = sv.astype(BF16)
+        dv_ref[rows : rows + SHORT, :] = jnp.where(me == 0, sv, zero).astype(BF16)
         rest = jnp.zeros((rows - SHORT, PAIR), BF16)
         dk_ref[rows + SHORT :, :] = rest
         dv_ref[rows + SHORT :, :] = rest
-
-    @pl.when(step == PAIRS)
-    def _():
+        later = lax.rem(pair, 2)
+        first, second = wide * (1 - me), wide * me
+        q_at = first + later * PAIR
+        k_at = (first + 2 * PAIR) * (1 - later) + second * later
+        v_at = second + PAIR + later * PAIR
+        d_round[:, pl.ds(pl.multiple_of(q_at, PAIR), PAIR)] = keep_q[later]
+        d_round[:, pl.ds(pl.multiple_of(k_at, PAIR), PAIR)] = dk_ref[...]
+        d_round[:, pl.ds(pl.multiple_of(v_at, PAIR), PAIR)] = dv_ref[...]
+
+    for k in range(ROUNDS):
+        @at(FIRST + 2 * k + 2)
+        def _():
+            value = tn(hid1_ref[...], d_round[...]).astype(BF16)
+            rounds[k].other[...] = value[:, :wide].reshape(half_shape(part, wide))
+            rounds[k].start(0)
+            rounds[k].own[...] = value[:, wide:].reshape(half_shape(part, wide))
+
+    @at(FIRST + PAIRS)
+    def _():
+        out_ref[...] = out.total()
+        for k in (1, 2):
+            rounds[k].arrive(0)
+            rounds[k].merge0()
+        rounds[0].add1(ra_ref, rb_ref)
         down_ref[...] = down.total()
         up.add2(up_ref)
-        out.add2(out_ref)
-        down.drain(3, 4, 5, 6, 7)
-        up.drain(1, 2, 3, 4)
-        out.drain(1, 2, 3, 4)
+        down.drain(*range(1, 8))
+        out.drain(*range(8))
+        up.drain(*range(1, 5))
+        rounds[0].drain(0, 1, 2)
+        rounds[1].drain(0)
+        rounds[2].drain(0)
         for pair in range(PAIRS):
             kv_copy(pair).wait_send()
-
-
-def back_call(q, kv, d_att, lse, cos, sin, handed, rows):
-    last = PAIRS - 1
-
-    def late(s):
-        return jnp.minimum(s, last)
-
-    def early(s):
-        return jnp.maximum(s - 1, 0)
-
-    def fixed(shape):
-        return pl.BlockSpec(shape, lambda s: (0,) * len(shape))
-
-    specs = [
-        pl.BlockSpec((rows, PAIR), lambda s: (0, late(s))),
-        pl.BlockSpec((rows, PAIR), lambda s: (1, late(s))),
-    ]
-    specs += [pl.BlockSpec((rows, PAIR), lambda s: (0, late(s)))] * 4
-    specs += [pl.BlockSpec((SHORT, PAIR), lambda s: (0, late(s)))] * 2
+        for k in range(16):
+            if k > 0:
+                early_copy(k).wait_recv()
+            early_copy(k).wait_send()
+        early_ref[...] = early_all[...]
+
+
+def middle_call(
+    act, d_low, att, d_attention, hidden, d_up, hidden1, payload, q, kv, d_att, lse, cos, sin, rows,
+):
     n = SLOTS * rows
+    half = FF // 2
     dr, dc = FF // 16, D // 2
-    ur, uc = D // 16, FF // 2
-    wr, wc = D // 16, D // 2
+    ur, wr = D // 16, D // 16
+
+    def clamp(s, low, high):
+        return jnp.minimum(jnp.maximum(s, low), high)
+
+    def order_of(k):
+        return k // 2 + lax.rem(k, 2) * ROUNDS
+
+    def now(s):
+        return order_of(clamp(s - FIRST, 0, PAIRS - 1))
+
+    def before(s):
+        return order_of(clamp(s - FIRST - 1, 0, PAIRS - 1))
+
+    def long():
+        return pl.BlockSpec((rows, PAIR), lambda s: (0, now(s)))
+
+    def second():
+        return pl.BlockSpec((rows, PAIR), lambda s: (1, now(s)))
+
+    def short():
+        return pl.BlockSpec((SHORT, PAIR), lambda s: (0, now(s)))
+
+    def low(shape):
+        return pltpu.VMEM(shape, BF16)
+
+    handed = ((4, ur, half), (2, 2, ur, WIDE), (2, 2, ur, WIDE), (2,) + half_shape(ur, WIDE))
+
     return pl.pallas_call(
-        back_kernel,
-        name="attend_back",
-        grid=(PAIRS + 1,),
+        middle_kernel,
+        name="middle",
+        grid=(FIRST + PAIRS + 1,),
         out_shape=(
             jax.ShapeDtypeStruct((n, D), BF16),
             jax.ShapeDtypeStruct((n, D), BF16),
             jax.ShapeDtypeStruct((n, D), BF16),
             jax.ShapeDtypeStruct((dr, dc), F32),
-            jax.ShapeDtypeStruct((4, ur, uc), BF16),
-            jax.ShapeDtypeStruct((4, wr, wc), BF16),
-        ),
-        in_specs=specs
-        + [
-            pl.BlockSpec((rows, PAIR), lambda s: (0, late(s))),
-            pl.BlockSpec((rows, PAIR), lambda s: (1, late(s))),
-            pl.BlockSpec((1, 4, rows), lambda s: (late(s), 0, 0)),
+            jax.ShapeDtypeStruct((wr, dc), F32),
+        )
+        + tuple(jax.ShapeDtypeStruct(o, BF16) for o in handed + ((16, 16, D),)),
+        in_specs=[
+            pl.BlockSpec((n, D), lambda s: (0, clamp(s - 1, 0, 3))),
+            whole((n, D)),
+            whole((n, D)),
+            whole((n, D)),
+            whole((n, D)),
+            pl.BlockSpec((n, CHUNK), lambda s: (0, clamp(s - 5, 0, 3))),
+            whole((n, D)),
+            whole((16, D)),
+            long(), second(), long(), long(), long(), long(), short(), short(), long(), second(),
+            long(), second(),
+            pl.BlockSpec((1, 4, rows), lambda s: (now(s), 0, 0)),
             whole((LEN, PAIR)),
             whole((LEN, PAIR)),
-        ]
-        + [ANY] * 4,
+        ],
         out_specs=(
-            pl.BlockSpec((n, PAIR), lambda s: (0, late(s))),
-            pl.BlockSpec((n, PAIR), lambda s: (0, early(s))),
-            pl.BlockSpec((n, PAIR), lambda s: (0, early(s))),
-            fixed((dr, dc)),
-            fixed((4, ur, uc)),
-            fixed((4, wr, wc)),
-        ),
-        scratch_shapes=[
-            pltpu.VMEM((2, 2, dr, dc), BF16),
-            pltpu.VMEM((2, 2, dr, dc), BF16),
-            pltpu.VMEM((4, dr, dc), BF16),
-            pltpu.VMEM((3, dr, dc), BF16),
-        ]
-        + [pltpu.VMEM(half_shape(ur, uc), BF16)]
-        + scatter_scratch(ur, uc, first=False, last=False)
-        + [pltpu.VMEM(half_shape(wr, wc), BF16)]
-        + scatter_scratch(wr, wc, first=False, last=False)
-        + [
-            pltpu.VMEM((PAIRS, rows + SHORT, 2 * PAIR), BF16),
-            pltpu.VMEM((PAIRS, rows + SHORT, 2 * PAIR), BF16),
-            pltpu.VMEM((2,) + (rows, PAIR), F32),
-            pltpu.VMEM((2,) + (rows, PAIR), F32),
-            pltpu.VMEM((2,) + (SHORT, PAIR), F32),
-            pltpu.VMEM((2,) + (SHORT, PAIR), F32),
-            DMA((18,)),
-            DMA((18,)),
-            DMA((PAIRS,)),
-            DMA((PAIRS,)),
-            DMA((4,)),
-        ],
+            pl.BlockSpec((n, PAIR), lambda s: (0, now(s))),
+            pl.BlockSpec((n, PAIR), lambda s: (0, before(s))),
+            pl.BlockSpec((n, PAIR), lambda s: (0, before(s))),
+            whole((dr, dc)),
+            whole((wr, dc)),
+        )
+        + tuple(whole(o) for o in handed + ((16, 16, D),)),
+        scratch_shapes=[low(half_shape(dr, dc))] * 3
+        + [low((2, 2, dr, dc))] * 2
+        + [low((4, dr, dc)), low((3, dr, dc))]
+        + [low(half_shape(wr, dc))] * 3
+        + [low((2, 2, wr, dc))] * 2
+        + [low((4, wr, dc)), low((3, wr, dc))]
+        + [low(half_shape(ur, half))] * 3
+        + [low((2, 2, ur, half))] * 2
+        + [low((4, ur, half))]
+        + [low((ROUNDS,) + half_shape(ur, WIDE))]
+        + [low((2, 2, ur, WIDE))] * 2
+        + [low((n, 2 * WIDE)), low((2, n, PAIR))]
+        + [low((PAIRS, rows + SHORT, 2 * PAIR))] * 2
+        + [pltpu.VMEM((2, rows, PAIR), F32)] * 2
+        + [pltpu.VMEM((2, SHORT, PAIR), F32)] * 2
+        + [pltpu.VMEM((16, D), F32), low((16, D)), low((16, 16, D))]
+        + [DMA((37,)), DMA((37,)), DMA((PAIRS,)), DMA((PAIRS,)), DMA((16,)), DMA((16,))],
         compiler_params=pltpu.CompilerParams(
-            collective_id=2, has_side_effects=True, vmem_limit_bytes=BIG
-        ),
-        cost_estimate=cost(40 * D * rows * (LEN + SHORT), 30e6, HEADS * rows * (LEN + SHORT)),
-    )(q, q, *kv, d_att, d_att, lse, cos, sin, *handed)
-
-
-BLOCKS = 3
+            collective_id=1, has_side_effects=True, vmem_limit_bytes=BIG
+        ),
+        cost_estimate=cost(2 * n * D * (2 * FF + D) + 40 * D * rows * (LEN + SHORT), 50e6),
+    )(
+        act, d_low, att, d_attention, hidden, d_up, hidden1, payload, q, q, *kv, d_att, d_att,
+        att, att, lse, cos, sin,
+    )
+
+
 TILES = 4
 
 
+def pack_rows(rows):
+    parts = [rows[r : r + 1, c : c + 128] for r in range(5) for c in range(0, D, 128)]
+    return jnp.concatenate(parts + [jnp.zeros((2, 128), F32)], axis=0).astype(BF16)
+
+
 def end_kernel(
-    tok_ref, dmid_ref, hidden_ref, mod_ref, gain_ref, weight_ref, lengths,
-    dq_any, dk_any, dv_any, up_any, out_any,
-    grad_ref, gqkv_ref, gup_ref, gout_ref, late_ref,
-    dqkv, hidden_t,
-    up2, up3, out2, out3,
-    other, own, came0, a1, b1, came2, came3,
-    sums, sums_came, sums_all, late_came,
-    send, recv, send_late, recv_late, local,
+    tok_ref, dmid_ref, dq_ref, dk_ref, dv_ref, mod_ref, gain_ref, weight_ref, lengths,
+    up_in, ra, rb, rown,
+    grad_ref, gqkv_ref, gup_ref, late_ref,
+    up2, up3, r2, r3, last_a, last_b, sums, sums_came, sums_all, late_came,
+    send, recv, send_late, recv_late,
 ):
     step = pl.program_id(0)
     s, me = lax.axis_index("seq"), lax.axis_index("span")
     up = Scatter(send, recv, 0, came2=up2, came3=up3)
-    out = Scatter(send, recv, 8, came2=out2, came3=out3)
-    blocks = [
+    rounds = [
         Scatter(
-            send, recv, 16 + 8 * b, other=other.at[b], own=own.at[b], came0=came0.at[b],
-            a1=a1.at[b], b1=b1.at[b], came2=came2.at[b], came3=came3.at[b],
-        )
-        for b in range(BLOCKS)
+            send, recv, 8 * (k + 1), own=rown.at[k - 1] if k else None,
+            a1=last_a.at[k - 1] if k else ra,
+            b1=last_b.at[k - 1] if k else rb,
+            came2=r2.at[k], came3=r3.at[k],
+        )
+        for k in range(ROUNDS)
     ]
-    loads = [
-        pltpu.make_async_copy(src, dst, local.at[i])
-        for i, (src, dst) in enumerate(
-            [(up_any, up2), (out_any, out2)]
-            + [
-                (a, dqkv.at[:, pl.ds(k * D, D)])
-                for k, a in enumerate([dq_any, dk_any, dv_any])
-            ]
-        )
-    ]
-    wide = 3 * D // 2 // BLOCKS
-
-    def product(core, b):
-        start = pl.multiple_of(core * (3 * D // 2) + b * wide, 128)
-        value = nn(hidden_t[...], dqkv[:, pl.ds(start, wide)]).astype(BF16)
-        return value.reshape(half_shape(D // 16, wide))
 
     def late_copy(k):
         if k == 0:
@@ -1360,95 +1362,72 @@
             device_id_type=MESH,
         )
 
-    @pl.when(step == 0)
-    def _():
-        for load in loads:
-            load.start()
-        hidden_t[...] = hidden_ref[...].T
+    def at(number):
+        return pl.when(step == number)
+
+    @at(0)
+    def _():
+        up2[...] = up_in[...]
+        sums[...] = jnp.zeros_like(sums)
         greet([{"span": 1 - me}] + [{"seq": lax.rem(s + k, 16)} for k in range(1, 16)])
-        loads[0].wait()
-        loads[1].wait()
         up.start(5, 6, 7)
-        out.start(5, 6, 7)
-        for load in loads[2:]:
-            load.wait()
-        sums[...] = jnp.zeros_like(sums)
-
-    for b in range(BLOCKS):
-        @pl.when(step == b)
-        def _():
-            other[b] = product(1 - me, b)
-            blocks[b].scatter0()
-            if b > 0:
-                blocks[b - 1].scatter1()
-            own[b] = product(me, b)
-
-    @pl.when(step == 3)
-    def _():
-        blocks[2].scatter1()
-        blocks[0].scatter2()
-
-    @pl.when(step == 4)
-    def _():
-        blocks[1].scatter2()
-
-    @pl.when(step == 5)
-    def _():
-        blocks[2].scatter2()
-        blocks[0].scatter3()
-
-    @pl.when(step == 6)
-    def _():
-        blocks[1].scatter3()
-
-    @pl.when(step >= BLOCKS)
-    def _():
-        t = step - BLOCKS
-        j = t // 2
-        size = tok_ref.shape[0]
-        swapped = jnp.full((1, D), jnp.where(lengths[1] > lengths[0], 1.0, 0.0))
-        mine = jnp.where(j == 0, swapped, 1.0 - swapped)
-        scale = jnp.where(mine == 0.0, mod_ref[0:1, D : 2 * D], mod_ref[1:2, D : 2 * D])
-        gain = wide_row(gain_ref)
-        start = pl.multiple_of(t * size, size)
-        d_hidden = nt(dqkv[pl.ds(start, size), :], weight_ref[...])
-        x = tok_ref[...].astype(F32)
-        center = x - row_mean(x)
-        r = lax.rsqrt(row_mean(center * center) + EPSILON)
-        xhat = center * r
-        hx = col_sum(d_hidden * xhat)
-        fx = d_hidden * (1.0 + scale) * gain
-        grad_ref[...] = dmid_ref[...] + r * (fx - row_mean(fx) - xhat * row_mean(fx * xhat))
-        shift = col_sum(d_hidden)
-        none = jnp.zeros((3, D), F32)
-        first, second = mine == 0.0, mine != 0.0
-        zero = jnp.zeros((1, D), F32)
-        sums[...] += jnp.concatenate(
-            [
-                jnp.where(first, shift, zero), jnp.where(first, hx * gain, zero),
-                jnp.where(second, shift, zero), jnp.where(second, hx * gain, zero),
-                hx * (1.0 + scale), none,
-            ],
-            axis=0,
-        )
-
-    @pl.when(step == BLOCKS + TILES - 1)
+        rounds[0].start(3, 4)
+        rounds[1].start(1, 2)
+        rounds[2].start(1, 2)
+
+    size = tok_ref.shape[0]
+    j = step // 2
+    swapped = jnp.full((1, D), jnp.where(lengths[1] > lengths[0], 1.0, 0.0))
+    mine = jnp.where(j == 0, swapped, 1.0 - swapped)
+    scale = jnp.where(mine == 0.0, mod_ref[0:1, D : 2 * D], mod_ref[1:2, D : 2 * D])
+    gain = wide_row(gain_ref)
+    d_hidden = (
+        nt(dq_ref[...], weight_ref[:, :D])
+        + nt(dk_ref[...], weight_ref[:, D : 2 * D])
+        + nt(dv_ref[...], weight_ref[:, 2 * D :])
+    )
+    x = tok_ref[...].astype(F32)
+    center = x - row_mean(x)
+    r = lax.rsqrt(row_mean(center * center) + EPSILON)
+    xhat = center * r
+    hx = col_sum(d_hidden * xhat)
+    fx = d_hidden * (1.0 + scale) * gain
+    grad_ref[...] = dmid_ref[...] + r * (fx - row_mean(fx) - xhat * row_mean(fx * xhat))
+    shift = col_sum(d_hidden)
+    first, second = mine == 0.0, mine != 0.0
+    zero = jnp.zeros((1, D), F32)
+    sums[...] += jnp.concatenate(
+        [
+            jnp.where(first, shift, zero), jnp.where(first, hx * gain, zero),
+            jnp.where(second, shift, zero), jnp.where(second, hx * gain, zero),
+            hx * (1.0 + scale), jnp.zeros((3, D), F32),
+        ],
+        axis=0,
+    )
+
+    @at(TILES - 1)
     def _():
         late_copy(0).start()
-        blocks[2].scatter3()
+        rounds[0].scatter3()
         late_copy(0).wait_recv()
-        sums_all[...] = sums[...] + sums_came[...]
+        sums_all[...] = pack_rows(sums[...] + sums_came[...])
         for k in range(1, 16):
             late_copy(k).start()
+        rounds[1].scatter2()
+        rounds[2].scatter2()
+        rounds[1].scatter3()
         late_came[s] = sums_all[...]
+        rounds[2].scatter3()
         gup_ref[...] = up.total()
-        gout_ref[...] = out.total()
-        for b in range(BLOCKS):
-            gqkv_ref[:, b * wide : (b + 1) * wide] = blocks[b].total()
+        for k in range(ROUNDS):
+            total = rounds[k].total()
+            for c in range(3):
+                cols = slice((c * ROUNDS + k) * PAIR, (c * ROUNDS + k + 1) * PAIR)
+                gqkv_ref[:, cols] = total[:, c * PAIR : (c + 1) * PAIR]
         up.drain(5, 6, 7)
-        out.drain(5, 6, 7)
-        for block in blocks:
-            block.drain(*range(8))
+        rounds[0].drain(*range(3, 8))
+        rounds[1].drain(*range(1, 8))
+        rounds[2].drain(*range(1, 8))
         for k in range(16):
             if k > 0:
                 late_copy(k).wait_recv()
@@ -1456,78 +1435,59 @@
         late_ref[...] = late_came[...]
 
 
-def end_call(tokens, d_mid, hidden, mod, gain, weight, lengths, dq, dk, dv, up2, out2, rows):
+def end_call(tokens, d_mid, dq, dk, dv, mod, gain, weight, lengths, handed, rows):
     n = SLOTS * rows
     size = n // TILES
     r = D // 16
-    wide = 3 * D // 2 // BLOCKS
-
-    def tile(s):
-        return (jnp.maximum(s - BLOCKS, 0), 0)
-
-    def fixed(shape):
-        return pl.BlockSpec(shape, lambda s: (0,) * len(shape))
-
-    def each(shape):
-        return pltpu.VMEM((BLOCKS,) + shape, BF16)
+
+    def tile():
+        return pl.BlockSpec((size, D), lambda s: (s, 0))
 
     return pl.pallas_call(
         end_kernel,
         name="end",
-        grid=(BLOCKS + TILES,),
+        grid=(TILES,),
         out_shape=(
             jax.ShapeDtypeStruct((n, D), F32),
             jax.ShapeDtypeStruct((r, 3 * D // 2), F32),
             jax.ShapeDtypeStruct((r, FF // 2), F32),
-            jax.ShapeDtypeStruct((r, D // 2), F32),
-            jax.ShapeDtypeStruct((16, 8, D), F32),
-        ),
-        in_specs=[
-            pl.BlockSpec((size, D), tile),
-            pl.BlockSpec((size, D), tile),
-            whole((n, D)),
+            jax.ShapeDtypeStruct((16, 32, 128), BF16),
+        ),
+        in_specs=[tile()] * 5
+        + [
             whole((8, 6 * D)),
             whole((D,)),
             whole((D, 3 * D)),
             pl.BlockSpec(memory_space=pltpu.SMEM),
         ]
-        + [ANY] * 5,
+        + [whole(a.shape) for a in handed],
         out_specs=(
-            pl.BlockSpec((size, D), tile),
-            fixed((r, 3 * D // 2)),
-            fixed((r, FF // 2)),
-            fixed((r, D // 2)),
-            fixed((16, 8, D)),
+            tile(),
+            whole((r, 3 * D // 2)),
+            whole((r, FF // 2)),
+            whole((16, 32, 128)),
         ),
         scratch_shapes=[
-            pltpu.VMEM((n, 3 * D), BF16),
-            pltpu.VMEM((D, n), BF16),
             pltpu.VMEM((4, r, FF // 2), BF16),
             pltpu.VMEM((3, r, FF // 2), BF16),
-            pltpu.VMEM((4, r, D // 2), BF16),
-            pltpu.VMEM((3, r, D // 2), BF16),
-            each(half_shape(r, wide)),
-            each(half_shape(r, wide)),
-            each(half_shape(r, wide)),
-            each((2, 2, r, wide)),
-            each((2, 2, r, wide)),
-            each((4, r, wide)),
-            each((3, r, wide)),
+            pltpu.VMEM((ROUNDS, 4, r, WIDE), BF16),
+            pltpu.VMEM((ROUNDS, 3, r, WIDE), BF16),
+            pltpu.VMEM((2, 2, 2, r, WIDE), BF16),
+            pltpu.VMEM((2, 2, 2, r, WIDE), BF16),
             pltpu.VMEM((8, D), F32),
             pltpu.VMEM((8, D), F32),
-            pltpu.VMEM((8, D), F32),
-            pltpu.VMEM((16, 8, D), F32),
-            DMA((16 + 8 * BLOCKS,)),
-            DMA((16 + 8 * BLOCKS,)),
+            pltpu.VMEM((32, 128), BF16),
+            pltpu.VMEM((16, 32, 128), BF16),
+            DMA((8 * (ROUNDS + 1),)),
+            DMA((8 * (ROUNDS + 1),)),
             DMA((16,)),
             DMA((16,)),
-            DMA((5,)),
         ],
         compiler_params=pltpu.CompilerParams(
             collective_id=3, has_side_effects=True, vmem_limit_bytes=BIG
         ),
-        cost_estimate=cost(4 * n * D * 3 * D, 30e6),
-    )(tokens, d_mid, hidden, mod, gain, weight, lengths, dq, dk, dv, up2, out2)
+        cost_estimate=cost(2 * n * D * 3 * D, 22e6),
+    )(tokens, d_mid, dq, dk, dv, mod, gain, weight, lengths, *handed)
 
 
 def exact(left, right, over):
@@ -1546,34 +1506,43 @@
     lengths, early_ref, late_ref, table_ref, silu_ref, weight_ref,
     qkv_in, out_in, up_in, down_in, sorted_any,
     ada_ref, bias_ref, gcond_ref, gain1_ref, gain2_ref, bd_ref, bu_ref,
-    qkv_ref, out_ref, up_ref, down_ref, natural_any, moved,
+    qkv_ref, out_ref, up_ref, down_ref, natural_any, stage, read, moved,
 ):
     seq = late_ref.shape[0]
     me, s = lax.axis_index("span"), lax.axis_index("seq")
     half = sorted_any.shape[0] // SLOTS
+    reads = [
+        pltpu.make_async_copy(sorted_any.at[pl.ds(j * half, half)], stage.at[j], read.at[j])
+        for j in range(SLOTS)
+    ]
     moves = [
         pltpu.make_async_copy(
-            sorted_any.at[pl.ds(j * half, half)],
+            stage.at[j],
             natural_any.at[pl.ds(pl.multiple_of(slot_of(lengths, j) * half, half), half)],
             moved.at[j],
         )
         for j in range(SLOTS)
     ]
-    for move in moves:
-        move.start()
+    for copy in reads:
+        copy.start()
     qkv_ref[...] = qkv_in[...]
     out_ref[...] = out_in[...]
     up_ref[...] = up_in[...]
     down_ref[...] = down_in[...]
-    early = early_ref[...].reshape(seq, 2, 16, D)
-    early = early[:, 0] + early[:, 1]
-    late = late_ref[...]
+    for j in range(SLOTS):
+        reads[j].wait()
+        moves[j].start()
+    early = early_ref[...].astype(F32)
+    packed = late_ref[...].astype(F32)
+    late = [
+        jnp.concatenate([packed[:, 6 * r + c] for c in range(6)], axis=1) for r in range(5)
+    ]
     mods = []
     for k in range(SLOTS):
         mods.append(
-            [late[:, 2 * k], late[:, 2 * k + 1]] + [early[:, 4 * k + b] for b in range(4)]
-        )
-    gain1_ref[...] = jnp.sum(late[:, 4], axis=0)
+            [late[2 * k], late[2 * k + 1]] + [early[:, 4 * k + b] for b in range(4)]
+        )
+    gain1_ref[...] = jnp.sum(late[4], axis=0)
     gain2_ref[...] = jnp.sum(early[:, 8], axis=0)
     bd_ref[...] = jnp.sum(early[:, 9], axis=0)
     for f in range(4):
@@ -1628,9 +1597,11 @@
             grid=(1,),
             in_specs=[whole(a.shape) for a in given] + [ANY],
             out_specs=[all_of(o) for o in outs] + [ANY],
-            scratch_shapes=[DMA((SLOTS,))],
-        ),
-        compiler_params=pltpu.CompilerParams(vmem_limit_bytes=32 << 20),
+            scratch_shapes=[
+                pltpu.VMEM((SLOTS, grad_in.shape[0] // SLOTS, D), F32), DMA((SLOTS,)), DMA((SLOTS,)),
+            ],
+        ),
+        compiler_params=pltpu.CompilerParams(vmem_limit_bytes=BIG),
         cost_estimate=cost(1e7, 12e6),
     )(lengths, *given, grad_in)
 
@@ -1684,14 +1655,12 @@
         up_weight, up_bias, down_weight, down_bias, rows,
     )
     if fast:
-        early = lax.all_gather(payload, ("seq", "span"), axis=0)
-        a1, b1, out0, up0 = weights_call(act, d_low, att, d_attention, hidden2, d_up)
-        dq, dk, dv, grad_down, up2, out2 = back_call(
-            q, kv, d_att, lse, cos, sin, (a1, b1, up0, out0), rows
-        )
-        grad_in, grad_qkv, grad_up, grad_out, late = end_call(
-            tokens_sorted, d_mid, hidden1_sorted, mod, gain1, qkv_weight, lengths, dq, dk, dv,
-            up2, out2, rows,
+        dq, dk, dv, grad_down, grad_out, *handed, early = middle_call(
+            act, d_low, att, d_attention, hidden2, d_up, hidden1_sorted, payload, q, kv, d_att,
+            lse, cos, sin, rows,
+        )
+        grad_in, grad_qkv, grad_up, late = end_call(
+            tokens_sorted, d_mid, dq, dk, dv, mod, gain1, qkv_weight, lengths, handed, rows
         )
         (
             grad_ada, ada_bias_sum, grad_cond, gain1_sum, gain2_sum, bd_sum, bu_sum,
@@ -1711,7 +1680,7 @@
     early = gather_all(payload[:14].reshape(-1))
 
     dq, dk, dv, dkx, dvx, dks, dvs = attend_back_call(
-        place, q, kv_long, kv_other, kv_short, d_att, lse, cos, sin, rows
+        place, q, kv_long, kv_other, kv_short, d_att, att, lse, cos, sin, rows
     )
     ek = ev = None
     for step in range(1, span):

time: 232 us -> 203 us (0.88)
  between operations: 14.2 us -> 0.87 us
  local copies, waits for them, and re-layouts: 11 us -> 0 us
  Pallas kernels: 206 us -> 202 us
    unnamed x28 -> x0, local copies, waits for them, and re-layouts: 11 us -> none
    pallas_call x3 -> x2, Pallas kernels: 119 us -> 114 us  [the longest x1 80 us: middle_call(): pl.pallas_call(middle_kernel, name='middle', grid=(FIRST + PAIRS + 1,), o...]
    pallas_call x1, Pallas kernels: 6.49 us -> 9.03 us  [condition_call(): pl.pallas_call(condition_kernel, name='condition', out_shape=tuple((jax.S...]
    pallas_call x1, Pallas kernels: 18.4 us -> 16 us  [attend_sorted_call(): pl.pallas_call(attend_sorted_kernel, name='attend', out_shape=(jax.ShapeD...]
  transfers between devices with their start and end apart: 1 -> 0, of which waited for: 0 -> 0; matrix products, arithmetic and copies ran while one was open for 0% -> 0% of each run, Pallas kernels for 52% -> 0%
where the time goes in v4:
time: 203 us
  Pallas kernels  202 us (100%)
    pallas_call x1, Pallas kernels, middle_call(): pl.pallas_call(middle_kernel, name='middle', grid=(FIRST + PAIRS + 1,), o...  80 us
    pallas_call x1, Pallas kernels, feed_call(): pl.pallas_call(partial(feed_kernel, halves), name='feed', out_shape=(jax....  37.6 us
    pallas_call x1, Pallas kernels, end_call(): pl.pallas_call(end_kernel, name='end', grid=(TILES,), out_shape=(jax.Shap...  33.9 us
    pallas_call x1, Pallas kernels, attend_sorted_call(): pl.pallas_call(attend_sorted_kernel, name='attend', out_shape=(jax.ShapeD...  16 us
    pallas_call x1, Pallas kernels, share_call(): pl.pallas_call(share_kernel, name='project', grid=(steps,), out_shape=(ja...  13.2 us
    pallas_call x1, Pallas kernels, modulation_call(): pl.pallas_call(partial(modulation_kernel, n), name='modulation', out_shap...  12.4 us
    pallas_call x1, Pallas kernels, condition_call(): pl.pallas_call(condition_kernel, name='condition', out_shape=tuple((jax.S...  9.03 us

profile of v4, /device:TPU:0, one launch (start us, length us, event | category | flops | bytes accessed | tf_op | source)
XLA Modules:
  0.0 203.0 jit_solution(8491384804742174430)
XLA Ops:
  0.6 12.4 %modulation.1 = (f32[8,4608]{1,0:T(8,128)}, f32[16,8,128]{2,1,0:T(8,128)}, f32[2,16,128]{2,1,0:T(8,128)}) custom-call(bf16[2,128]{1,0:T(2,128)(2,1)} %cond_ref.1, s32[2]{0:T(128)} %assign_ref.1, bf16[128,4608]{1,0:T(8,128)(2,1)} %weight_ref.7, bf16[4608]{0:T(1024)(128)(2,1)} %bias_ref.1), custom_call_target="tpu_custom_call" | custom-call | flops 10000000 | bytes 2000000 | tf_op jit(solution)/shard_map/modulation/pallas_call | solution.py:155
  13.1 13.2 %project.1 = (bf16[1024,768]{1,0:T(8,128)(2,1)}, bf16[1024,768]{1,0:T(8,128)(2,1)}, bf16[1024,1536]{1,0:T(8,128)(2,1)}, bf16[1024,1536]{1,0:T(8,128)(2,1)}) custom-call(bf16[1024,768]{1,0:T(8,128)(2,1)} %bitcast.5, f32[8,4608]{1,0:T(8,128)} %get-tuple-element.66.mod_ref, bf16[768]{0:T(1024)(128)(2,1)} %gain_ref.5, bf16[768,2304]{1,0:T(8,128)(2,1)} %weight_ref.6, ...), custom_call_target="tpu_custom_call" | custom-call | flops 3623878656 | bytes 14000000 | tf_op jit(solution)/shard_map/project/pallas_call | solution.py:750
  26.3 16.0 %attend.1 = (bf16[1024,768]{1,0:T(8,128)(2,1)}, f32[6,4,512]{2,1,0:T(4,128)}, bf16[1024,768]{1,0:T(8,128)(2,1)}, bf16[512,768]{1,0:T(8,128)(2,1)}, bf16[512,768]...) custom-call(s32[2]{0:T(128)} %lengths.5, ...), custom_call_target="tpu_custom_call" | custom-call | flops 7247757312 | bytes 16000000 | tf_op jit(solution)/shard_map/attend/pallas_call | solution.py:818
  42.3 37.6 %feed.1 = (bf16[1024,768]{1,0:T(8,128)(2,1)}, f32[1024,768]{1,0:T(8,128)}, bf16[1024,768]{1,0:T(8,128)(2,1)}, bf16[1024,3072]{1,0:T(8,128)(2,1)}, bf16[1024,768]...) custom-call(s32[2]{0:T(128)} %lengths.5, ...), custom_call_target="tpu_custom_call" | custom-call | flops 21743271936 | bytes 40000000 | tf_op jit(solution)/shard_map/feed/pallas_call | solution.py:515
  79.9 80.0 %middle.1 = (bf16[1024,768]{1,0:T(8,128)(2,1)}, bf16[1024,768]{1,0:T(8,128)(2,1)}, bf16[1024,768]{1,0:T(8,128)(2,1)}, f32[192,384]{1,0:T(8,128)}, f32[48,384]{1,...) custom-call(bf16[1024,3072]{1,0:T(8,128)(2,1)} %get-tuple-element.73, ...), custom_call_target="tpu_custom_call" | custom-call | flops 28991029248 | bytes 50000000 | tf_op jit(solution)/shard_map/middle/pallas_call | solution.py:1261
  159.9 33.9 %end.1 = (f32[1024,768]{1,0:T(8,128)}, f32[48,1152]{1,0:T(8,128)}, f32[48,1536]{1,0:T(8,128)}, bf16[16,32,128]{2,1,0:T(8,128)(2,1)}) custom-call(bf16[1024,768]{1,0:T(8,128)(2,1)} %get-tuple-element.90.tok_ref, f32[1024,768]{1,0:T(8,128)} %get-tuple-element.91.dmid_ref, bf16[1024,768]{1,0:T(8,128)(2,1)} %get-tuple-element.92.dq_ref, ...), custom_call_target="tpu_custom_call" | custom-call | flops 3623878656 | bytes 22000000 | tf_op jit(solution)/shard_map/end/pallas_call | solution.py:1446
  193.8 9.0 %condition.1 = (f32[8,2304]{1,0:T(8,128)}, f32[4608]{0:T(1024)}, f32[2,128]{1,0:T(2,128)}, f32[768]{0:T(1024)}, f32[768]{0:T(1024)}, /*index=5*/f32[768]{0:T(102...) custom-call(s32[2]{0:T(128)} %lengths.5, ...), custom_call_target="tpu_custom_call" | custom-call | flops 10000000 | bytes 12000000 | tf_op jit(solution)/shard_map/condition/pallas_call | solution.py:1591

commit v5 on v4

--- a/solution.py
+++ b/solution.py
@@ -100,7 +100,7 @@
 
 def modulation_kernel(
     n, cond_ref, assign_ref, weight_ref, bias_ref, mod_ref, table_ref, silu_ref,
-    own_ref, send, recv, local,
+    own_ref, send, recv, local, extra=(),
 ):
     me = lax.axis_index("seq")
     asked = [jnp.full((1, 128), assign_ref[k].astype(F32)) for k in range(SLOTS)]
@@ -112,9 +112,11 @@
         pl.semaphore_signal(
             barrier, inc=1, device_id={"seq": lax.rem(me + step, n)}, device_id_type=MESH
         )
+    for peer in extra:
+        pl.semaphore_signal(barrier, inc=1, device_id=peer, device_id_type=MESH)
     mine = pltpu.make_async_copy(own_ref, table_ref.at[me], local)
     mine.start()
-    pl.semaphore_wait(barrier, n - 1)
+    pl.semaphore_wait(barrier, n - 1 + len(extra))
     copies = []
     for step in range(1, n):
         copy = pltpu.make_async_remote_copy(
@@ -142,11 +144,12 @@
     silu = (cond / (1.0 + jnp.exp(-cond))).astype(BF16)
     mod_ref[...] = nn(silu, weight_ref[...]) + bias_ref[...].astype(F32).reshape(1, 6 * D)
     for slot in range(SLOTS):
-        wanted = table_ref[:, SLOTS + slot, :]
+        wanted = table_ref[:, SLOTS + slot, :][:, :n]
+        lane = lax.broadcasted_iota(jnp.int32, (n, n), 1).astype(F32) * SLOTS
         rows = jnp.zeros((n, 128), F32)
-        for k in range(SLOTS * n):
-            row = table_ref[k // SLOTS, k % SLOTS : k % SLOTS + 1, :]
-            rows += jnp.where(wanted == k, row, 0.0)
+        for k in range(SLOTS):
+            chosen = jnp.where(wanted == lane + k, 1.0, 0.0).astype(BF16)
+            rows += nn(chosen, table_ref[:, k, :].astype(BF16))
         silu_ref[slot] = (rows / (1.0 + jnp.exp(-rows))).astype(BF16).astype(F32)
 
 
@@ -690,8 +693,9 @@
 
 
 def share_kernel(
-    tok_ref, mod_ref, gain_ref, weight_ref, cos_ref, sin_ref,
-    q_ref, h_ref, kv_ref, kvx_any, stage, send, recv,
+    cond_ref, assign_ref, ada_ref, bias_ref, tok_ref, gain_ref, weight_ref, cos_ref, sin_ref,
+    q_ref, h_ref, kv_ref, mod_ref, table_out, silu_ref, kvx_any,
+    stage, table_ref, send, recv, own_ref, send_cond, recv_cond, local,
 ):
     step = pl.program_id(0)
     steps = stage.shape[0]
@@ -707,6 +711,14 @@
             device_id={"span": 1 - me},
             device_id_type=MESH,
         )
+
+    @pl.when(step == 0)
+    def _():
+        modulation_kernel(
+            table_ref.shape[0], cond_ref, assign_ref, ada_ref, bias_ref, mod_ref, table_ref,
+            silu_ref, own_ref, send_cond, recv_cond, local, ({"span": 1 - me},),
+        )
+        table_out[...] = table_ref[...]
 
     row = mod_ref[pl.ds(step // (steps // SLOTS), 1), :]
     shift, scale = row[:, :D], row[:, D : 2 * D]
@@ -717,21 +729,21 @@
     h_ref[...] = hidden
     start = (me * (steps // SLOTS) + lax.rem(step, steps // SLOTS)) * tile
     start = pl.multiple_of(start, tile)
-    cos = jnp.concatenate([cos_ref[pl.ds(start, tile), :]] * PAIRS, axis=1)
-    sin = jnp.concatenate([sin_ref[pl.ds(start, tile), :]] * PAIRS, axis=1)
-    k = turn(nn(hidden, weight_ref[:, D : 2 * D]), cos, sin).astype(BF16)
+    cos, sin = cos_ref[pl.ds(start, tile), :], sin_ref[pl.ds(start, tile), :]
+    k = nn(hidden, weight_ref[:, D : 2 * D])
+    k = [turn(k[:, p : p + PAIR], cos, sin).astype(BF16) for p in range(0, D, PAIR)]
+    k = jnp.concatenate(k, axis=1)
     v = nn(hidden, weight_ref[:, 2 * D :]).astype(BF16)
     kv_ref[:, :D] = k
     kv_ref[:, D:] = v
     stage[step, :, :D] = k
     stage[step, :, D:] = v
 
-    @pl.when(step == 0)
-    def _():
-        greet([{"span": 1 - me}])
+    q = nn(hidden, weight_ref[:, :D])
+    for p in range(0, D, PAIR):
+        q_ref[:, p : p + PAIR] = turn(q[:, p : p + PAIR], cos, sin).astype(BF16)
 
     copy(step).start()
-    q_ref[...] = turn(nn(hidden, weight_ref[:, :D]), cos, sin).astype(BF16)
 
     @pl.when(step == steps - 1)
     def _():
@@ -739,7 +751,7 @@
             copy(i).wait()
 
 
-def share_call(tokens, mod, gain, weight, cos, sin, rows):
+def share_call(cond, assignment, ada_weight, ada_bias, tokens, gain, weight, cos, sin, rows):
     tile = 256
     n = SLOTS * rows
     steps = n // tile
@@ -755,39 +767,56 @@
             jax.ShapeDtypeStruct((n, D), BF16),
             jax.ShapeDtypeStruct((n, D), BF16),
             jax.ShapeDtypeStruct((n, 2 * D), BF16),
+            jax.ShapeDtypeStruct((8, 6 * D), F32),
+            jax.ShapeDtypeStruct((16, 8, 128), F32),
+            jax.ShapeDtypeStruct((SLOTS, 16, 128), F32),
             jax.ShapeDtypeStruct((n, 2 * D), BF16),
         ),
         in_specs=[
+            whole((SLOTS, 128)),
+            pl.BlockSpec(memory_space=pltpu.SMEM),
+            whole((128, 6 * D)),
+            whole((6 * D,)),
             at(D),
-            whole((8, 6 * D)),
             whole((D,)),
             whole((D, 3 * D)),
             whole((LEN, PAIR)),
             whole((LEN, PAIR)),
         ],
-        out_specs=(at(D), at(D), at(2 * D), pl.BlockSpec(memory_space=pl.ANY)),
+        out_specs=(
+            at(D), at(D), at(2 * D), whole((8, 6 * D)), whole((16, 8, 128)),
+            whole((SLOTS, 16, 128)), pl.BlockSpec(memory_space=pl.ANY),
+        ),
         scratch_shapes=[
             pltpu.VMEM((steps, tile, 2 * D), BF16),
+            pltpu.VMEM((16, 8, 128), F32),
             pltpu.SemaphoreType.DMA((steps,)),
             pltpu.SemaphoreType.DMA((steps,)),
+            pltpu.VMEM((8, 128), F32),
+            pltpu.SemaphoreType.DMA((16,)),
+            pltpu.SemaphoreType.DMA((16,)),
+            pltpu.SemaphoreType.DMA,
         ],
         compiler_params=pltpu.CompilerParams(
             collective_id=4, has_side_effects=True, vmem_limit_bytes=BIG
         ),
         cost_estimate=cost(2 * n * D * 3 * D, 14e6),
-    )(tokens, mod, gain, weight, cos, sin)
+    )(cond, assignment, ada_weight, ada_bias, tokens, gain, weight, cos, sin)
 
 
 def attend_sorted_kernel(
     lengths, ql, qs, ko, vo, kx, vx, ks_own, vs_own, ks_other, vs_other,
+    tl, ts, cl, cs, hl, hs,
     out_ref, lse_ref, q_ref, ko_ref, vo_ref, kx_ref, vx_ref, ks_ref, vs_ref,
+    t_ref, c_ref, h_ref,
 ):
     rows = ql.shape[0]
     first = lax.axis_index("span") == 0
     ks = jnp.where(first, ks_own[...], ks_other[...])
     vs = jnp.where(first, vs_own[...], vs_other[...])
-    q_ref[:rows, :] = ql[...]
-    q_ref[rows:, :] = qs[...]
+    for ref, long, short in ((q_ref, ql, qs), (t_ref, tl, ts), (c_ref, cl, cs), (h_ref, hl, hs)):
+        ref[:rows, :] = long[...]
+        ref[rows:, :] = short[...]
     ks_ref[...] = ks
     vs_ref[...] = vs
     for ref, given in ((ko_ref, ko), (vo_ref, vo), (kx_ref, kx), (vx_ref, vx)):
@@ -802,12 +831,15 @@
     lse_ref[0, 3:4, :] = stats[1]
 
 
-def attend_sorted_call(lengths, q, kv, kvx, rows):
+def attend_sorted_call(lengths, q, kv, kvx, tokens, cot, hidden, rows):
     n = SLOTS * rows
     per = rows // SHORT
 
     def long(base):
         return pl.BlockSpec((rows, PAIR), lambda h, o: (slot_of(o, 0), base + h))
+
+    def second():
+        return pl.BlockSpec((rows, PAIR), lambda h, o: (slot_of(o, 1), h))
 
     def short(base):
         return pl.BlockSpec((SHORT, PAIR), lambda h, o: (slot_of(o, 1) * per, base + h))
@@ -824,23 +856,28 @@
             jax.ShapeDtypeStruct((n, D), BF16),
         )
         + (jax.ShapeDtypeStruct((rows, D), BF16),) * 4
-        + (jax.ShapeDtypeStruct((SHORT, D), BF16),) * 2,
+        + (jax.ShapeDtypeStruct((SHORT, D), BF16),) * 2
+        + (jax.ShapeDtypeStruct((n, D), BF16),) * 3,
         grid_spec=pltpu.PrefetchScalarGridSpec(
             num_scalar_prefetch=1,
             grid=(PAIRS,),
             in_specs=[
                 long(0),
-                pl.BlockSpec((rows, PAIR), lambda h, o: (slot_of(o, 1), h)),
+                second(),
                 long(0), long(PAIRS), long(0), long(PAIRS),
                 short(0), short(PAIRS), short(0), short(PAIRS),
-            ],
+            ]
+            + [long(0), second()] * 3,
             out_specs=[out(n), pl.BlockSpec((1, 4, rows), lambda h, o: (h, 0, 0)), out(n)]
             + [out(rows)] * 4
-            + [out(SHORT)] * 2,
+            + [out(SHORT)] * 2
+            + [out(n)] * 3,
         ),
         compiler_params=pltpu.CompilerParams(vmem_limit_bytes=BIG),
         cost_estimate=cost(16 * D * rows * (LEN + SHORT), 16e6, HEADS * rows * (LEN + SHORT)),
-    )(lengths, q, q, kv, kv, kvx, kvx, kv, kv, kvx, kvx)
+    )(
+        lengths, q, q, kv, kv, kvx, kvx, kv, kv, kvx, kvx, tokens, tokens, cot, cot, hidden, hidden
+    )
 
 
 def flip(index, bit):
@@ -979,45 +1016,253 @@
 DMA = pltpu.SemaphoreType.DMA
 
 
-FIRST = 9
+def both_kernel(
+    tok_ref, att_ref, cot_ref, mod_ref, gain_ref, wo_ref, wu_ref, bu_ref, wd_any, bd_ref, lengths,
+    out_ref, dmid_ref, datt_ref, h_ref, dup_ref, dattn_ref, payload_ref, a_ref, b_ref,
+    act_all, slope_all, dlow_all, mid_all, attention_all,
+    wd_ref, other, own, came0, a1, b1, send, recv, loaded,
+):
+    step = pl.program_id(0)
+    me = lax.axis_index("span")
+    down = Scatter(send, recv, 0, other=other, own=own, came0=came0, a1=a1, b1=b1)
+    load = pltpu.make_async_copy(wd_any, wd_ref, loaded)
+    tiles = act_all.shape[0] // tok_ref.shape[0]
+    tile = tok_ref.shape[0]
+    t = lax.rem(step, tiles)
+    at_rows = pl.ds(pl.multiple_of(t * tile, tile), tile)
+    halves = [h * me + (1 - h) * (1 - me) for h in range(2)]
+    swapped = jnp.full((1, D), jnp.where(lengths[1] > lengths[0], 1.0, 0.0))
+    mine = jnp.where(t // (tiles // SLOTS) == 0, swapped, 1.0 - swapped)
+
+    def modulation(b):
+        cols = slice(b * D, (b + 1) * D)
+        return jnp.where(mine == 0.0, mod_ref[0:1, cols], mod_ref[1:2, cols])
+
+    @pl.when(step == 0)
+    def _():
+        load.start()
+        greet(plane_peers())
+
+    @pl.when(step == 2 * tiles)
+    def _():
+        load.wait()
+        down.arrive(8, 9, 10, 11)
+        down.merge0()
+        down.start(1, 2)
+
+    @pl.when(step < tiles)
+    def _():
+        attention = nn(att_ref[...], wo_ref[...])
+        middle = tok_ref[...].astype(F32) + modulation(2) * attention
+        attention_all[at_rows, :] = attention
+        mid_all[at_rows, :] = middle
+        center = middle - row_mean(middle)
+        xhat = center * lax.rsqrt(row_mean(center * center) + EPSILON)
+        hidden = xhat * wide_row(gain_ref) * (1.0 + modulation(4)) + modulation(3)
+        hidden = hidden.astype(BF16)
+        h_ref[...] = hidden
+        d_low = (modulation(5) * cot_ref[...].astype(F32)).astype(BF16)
+        for h in range(2):
+            half = d_low[:, h * (D // 2) : (h + 1) * (D // 2)]
+            dlow_all[at_rows, part_of(halves[h], D // 2)] = half
+        up_bias = wide_row(bu_ref)
+        for f in range(0, FF, CHUNK):
+            cols = slice(f, f + CHUNK)
+            up = nn(hidden, wu_ref[:, cols]) + up_bias[:, cols]
+            square = up * up
+            bend = jnp.tanh(up * (GELU_C + (GELU_C * 0.044715) * square))
+            half = 0.5 * (1.0 + bend)
+            slope = half + (0.5 * up) * (1.0 - bend * bend) * (
+                GELU_C + (3 * GELU_C * 0.044715) * square
+            )
+            act_all[at_rows, cols] = (up * half).astype(BF16)
+            slope_all[at_rows, cols] = slope.astype(BF16)
+
+    @pl.when(jnp.logical_and(step >= tiles, step < 2 * tiles))
+    def _():
+        cols = pl.ds(pl.multiple_of(t * CHUNK, CHUNK), CHUNK)
+        value = tn(act_all[:, cols], dlow_all[...]).astype(BF16)
+        shape = own.shape[1:]
+        other[t] = value[:, : D // 2].reshape(shape)
+        own[t] = value[:, D // 2 :].reshape(shape)
+
+        for m in range(4):
+            @pl.when(t == m)
+            def _():
+                down.start(8 + m)
+
+    @pl.when(step >= 2 * tiles)
+    def _():
+        middle, attention = mid_all[at_rows, :], attention_all[at_rows, :]
+        gain = wide_row(gain_ref)
+        gate1, scale2, gate2 = modulation(2), modulation(4), modulation(5)
+        dy = cot_ref[...].astype(F32)
+        d_low = (gate2 * dy).astype(BF16)
+        lowered, d_hidden = None, None
+        sums = []
+        for f in range(0, FF, CHUNK):
+            cols = slice(f, f + CHUNK)
+            d_act = nt(d_low, wd_ref[cols, :])
+            d_up = (d_act * slope_all[at_rows, cols].astype(F32)).astype(BF16)
+            place = halves[f // (FF // 2)] * (FF // 2) + f % (FF // 2)
+            dup_ref[:, pl.ds(pl.multiple_of(place, CHUNK), CHUNK)] = d_up
+            sums.append(col_sum(d_up.astype(F32)))
+            low = nn(act_all[at_rows, cols], wd_ref[cols, :])
+            dh = nt(d_up, wu_ref[:, cols])
+            lowered = low if lowered is None else lowered + low
+            d_hidden = dh if d_hidden is None else d_hidden + dh
+        center = middle - row_mean(middle)
+        r = lax.rsqrt(row_mean(center * center) + EPSILON)
+        xhat = center * r
+        lowered = lowered + wide_row(bd_ref)
+        out_ref[...] = (middle + gate2 * lowered).astype(BF16)
+        hx = col_sum(d_hidden * xhat)
+        fx = d_hidden * (1.0 + scale2) * gain
+        d_mid = dy + r * (fx - row_mean(fx) - xhat * row_mean(fx * xhat))
+        dmid_ref[...] = d_mid
+        d_attention = (gate1 * d_mid).astype(BF16)
+        for h in range(2):
+            half = d_attention[:, h * (D // 2) : (h + 1) * (D // 2)]
+            dattn_ref[:, part_of(halves[h], D // 2)] = half
+        datt_ref[...] = nt(d_attention, wo_ref[...]).astype(BF16)
+        four = jnp.concatenate(
+            [
+                col_sum(d_mid * attention), col_sum(d_hidden), hx * gain,
+                col_sum(dy * lowered),
+            ],
+            axis=0,
+        )
+        is_second = jnp.concatenate([mine] * 4, axis=0) != 0.0
+        none = jnp.zeros((4, D), F32)
+        add_to(
+            payload_ref,
+            jnp.concatenate(
+                [
+                    jnp.where(is_second, none, four), jnp.where(is_second, four, none),
+                    hx * (1.0 + scale2), col_sum(d_low.astype(F32)), *sums,
+                    jnp.zeros((2, D), F32),
+                ],
+                axis=0,
+            ),
+            step == 2 * tiles,
+        )
+
+    @pl.when(step == 3 * tiles - 1)
+    def _():
+        down.add1(a_ref, b_ref)
+        down.drain(1, 2, 8, 9, 10, 11)
+
+
+def both_call(tokens, att, cot, mod, gain, wo, wu, bu, wd, bd, lengths, rows):
+    n = SLOTS * rows
+    tile = 256
+    tiles = n // tile
+    dr, dc = FF // 16, D // 2
+
+    def first():
+        return pl.BlockSpec((tile, D), lambda s: (jnp.minimum(s, tiles - 1), 0))
+
+    def last(width):
+        return pl.BlockSpec((tile, width), lambda s: (jnp.maximum(s - 2 * tiles, 0), 0))
+
+    def low(*shape):
+        return pltpu.VMEM(shape, BF16)
+
+    return pl.pallas_call(
+        both_kernel,
+        name="feed",
+        grid=(3 * tiles,),
+        out_shape=(
+            jax.ShapeDtypeStruct((n, D), BF16),
+            jax.ShapeDtypeStruct((n, D), F32),
+            jax.ShapeDtypeStruct((n, D), BF16),
+            jax.ShapeDtypeStruct((n, D), BF16),
+            jax.ShapeDtypeStruct((n, FF), BF16),
+            jax.ShapeDtypeStruct((n, D), BF16),
+            jax.ShapeDtypeStruct((16, D), F32),
+            jax.ShapeDtypeStruct((2, 2, dr, dc), BF16),
+            jax.ShapeDtypeStruct((2, 2, dr, dc), BF16),
+        ),
+        in_specs=[
+            first(),
+            first(),
+            pl.BlockSpec((tile, D), lambda s: (lax.rem(s, tiles), 0)),
+            whole((8, 6 * D)),
+            whole((D,)),
+            whole((D, D)),
+            whole((D, FF)),
+            whole((FF,)),
+            ANY,
+            whole((D,)),
+            pl.BlockSpec(memory_space=pltpu.SMEM),
+        ],
+        out_specs=(
+            last(D), last(D), last(D), first(), last(FF), last(D), whole((16, D)),
+            whole((2, 2, dr, dc)),
+            whole((2, 2, dr, dc)),
+        ),
+        scratch_shapes=[
+            low(n, FF), low(n, FF), low(n, D),
+            pltpu.VMEM((n, D), F32),
+            pltpu.VMEM((n, D), F32),
+        ]
+        + [low(FF, D)]
+        + [low(*half_shape(dr, dc))] * 3
+        + [low(2, 2, dr, dc)] * 2
+        + [DMA((12,)), DMA((12,)), DMA],
+        compiler_params=pltpu.CompilerParams(
+            collective_id=2, has_side_effects=True, vmem_limit_bytes=BIG
+        ),
+        cost_estimate=cost(2 * n * D * (5 * FF + 2 * D), 40e6, n * FF),
+    )(tokens, att, cot, mod, gain, wo, wu, bu, wd, bd, lengths)
+
+
+def pack_rows(rows, count):
+    parts = [rows[r : r + 1, c : c + 128] for r in range(count) for c in range(0, D, 128)]
+    rest = -len(parts) % 16
+    if rest:
+        parts.append(jnp.zeros((rest, 128), F32))
+    return jnp.concatenate(parts, axis=0).astype(BF16)
+
+
+FIRST = 5
 ROUNDS = PAIRS // 2
 WIDE = 3 * PAIR
 
 
 def middle_kernel(
-    act_ref, dlow_ref, att_ref, dattn_ref, h_ref, dup_ref, hid1_ref, payload_ref,
+    att_ref, dattn_ref, h_ref, dup_ref, hid1_ref, payload_ref, down_a, down_b,
     ql, qs, ko, vo, kx, vx, ks, vs, dol, dos, al, as_, lse, cos_ref, sin_ref,
-    dq_ref, dk_ref, dv_ref, down_ref, out_ref, up_ref, ra_ref, rb_ref, rown_ref, early_ref,
-    down_other, down_own, down_came, down_a, down_b, down2, down3,
+    dq_ref, dk_ref, dv_ref, down_ref, out_ref, up_ref, r_ref, ra_ref, rb_ref, rown_ref, early_ref,
+    down2, down3,
     out_other, out_own, out_came, out_a, out_b, out2, out3,
-    up_other, up_own, up_came, up_a, up_b, up2,
-    round_came, round_a, round_b, d_round, keep_q,
+    up_other, up_own, up_came, up_a, up_b, up2, up3,
+    round_other, round_came, round_a, round_b, round2, d_round, keep_q,
     leave, come, keep_k, keep_v, keep_sk, keep_sv, early_came, early_sum, early_all,
     send, recv, send_kv, recv_kv, send_early, recv_early,
 ):
     step = pl.program_id(0)
     s, me = lax.axis_index("seq"), lax.axis_index("span")
     rows = ql.shape[0]
-    down = Scatter(
-        send, recv, 0, other=down_other, own=down_own, came0=down_came, a1=down_a, b1=down_b,
-        came2=down2, came3=down3,
-    )
+    down = Scatter(send, recv, 0, a1=down_a, b1=down_b, came2=down2, came3=down3)
     out = Scatter(
         send, recv, 12, other=out_other, own=out_own, came0=out_came, a1=out_a, b1=out_b,
         came2=out2, came3=out3,
     )
     up = Scatter(
         send, recv, 20, other=up_other, own=up_own, came0=up_came, a1=up_a, b1=up_b, came2=up2,
+        came3=up3,
     )
     part, wide = hid1_ref.shape[1] // 16, WIDE
     rounds = [
         Scatter(
-            send, recv, 28 + 3 * k,
-            other=down_other.at[:, :, :, k * part : (k + 1) * part],
-            own=rown_ref.at[k - 1] if k else up_other.at[:, :, :, :, :wide],
+            send, recv, 28 + 5 * k,
+            other=round_other.at[k],
+            own=(up_other.at[:, :, :, :, :wide], up_other.at[:, :, :, :, wide : 2 * wide], rown_ref)[k],
             came0=round_came.at[k],
-            a1=round_a,
-            b1=round_b,
+            a1=round_a.at[k] if k < 2 else None,
+            b1=round_b.at[k] if k < 2 else None,
+            came2=round2,
         )
         for k in range(ROUNDS)
     ]
@@ -1035,10 +1280,14 @@
         )
 
     def early_copy(k):
+        half = pl.ds(pl.multiple_of(me * 48, 16), 48)
         if k == 0:
             src, dst, peer = payload_ref, early_came, {"span": 1 - me}
+        elif k == 16:
+            src, dst, peer = early_all.at[:, half], early_all.at[:, half], {"span": 1 - me}
         else:
-            src, dst, peer = early_sum, early_all.at[s], {"seq": lax.rem(s + k, 16)}
+            src, dst = early_sum.at[half], early_all.at[s, half]
+            peer = {"seq": lax.rem(s + k, 16)}
         return pltpu.make_async_remote_copy(
             src_ref=src,
             dst_ref=dst,
@@ -1054,15 +1303,23 @@
     @at(0)
     def _():
         greet([{"span": 1 - me}] + [{"seq": lax.rem(s + k, 16)} for k in range(1, 16)])
+        down.start(3, 4)
         early_copy(0).start()
 
     @at(3)
     def _():
         early_copy(0).wait_recv()
-        early_sum[...] = (payload_ref[...] + early_came[...]).astype(BF16)
+        early_sum[...] = pack_rows(payload_ref[...] + early_came[...], 16)
         for k in range(1, 16):
             early_copy(k).start()
-        early_all[s] = early_sum[...]
+        half = pl.ds(pl.multiple_of(me * 48, 16), 48)
+        early_all[s, half] = early_sum[half]
+
+    @at(FIRST + 3)
+    def _():
+        for k in range(1, 16):
+            early_copy(k).wait_recv()
+        early_copy(16).start()
 
     @at(2)
     def _():
@@ -1072,33 +1329,37 @@
     def _():
         out.scatter2()
 
-    @at(6)
-    def _():
-        down.arrive(8, 9, 10, 11)
-        down.merge0()
-        down.start(1, 2)
+    @at(FIRST)
+    def _():
+        up.scatter1()
+
+    @at(FIRST + 1)
+    def _():
         out.scatter3()
 
-    @at(FIRST + 1)
-    def _():
-        up.scatter1()
-
     @at(FIRST + 2)
     def _():
-        down.drain(8, 9, 10, 11)
         up.drain(0)
-        down.scatter2()
+
+    @at(3)
+    def _():
+        down.scatter3()
+
+    @at(FIRST + 4)
+    def _():
+        rounds[0].scatter1()
+
+    @at(FIRST + 4)
+    def _():
+        up.scatter3()
 
     @at(FIRST + 5)
     def _():
-        rounds[0].scatter1()
+        rounds[0].scatter2()
+        rounds[1].scatter1()
 
     def between():
-        @at(FIRST + 4)
-        def _():
-            down.scatter3()
-
-        @at(FIRST + 5)
+        @at(FIRST + 2)
         def _():
             up.scatter2()
 
@@ -1109,33 +1370,21 @@
         out_own[...] = value[:, D // 2 :].reshape(out_own.shape)
         out.scatter0()
 
-    @pl.when(jnp.logical_and(step >= 1, step < 5))
-    def _():
-        value = tn(act_ref[...], dlow_ref[...]).astype(BF16)
-        shape = down_own.shape[1:]
-        down_other[step - 1] = value[:, : D // 2].reshape(shape)
-        down_own[step - 1] = value[:, D // 2 :].reshape(shape)
-
-        for m in range(4):
-            @at(m + 1)
-            def _():
-                down.start(8 + m)
-
-    @pl.when(jnp.logical_and(step >= 5, step < FIRST))
+    @pl.when(jnp.logical_and(step >= 1, step < FIRST))
     def _():
         value = tn(h_ref[...], dup_ref[...]).astype(BF16)
         value = value.reshape(up_own.shape[:4] + (CHUNK,))
-        cols = pl.ds(pl.multiple_of(lax.rem(step - 5, 2) * CHUNK, CHUNK), CHUNK)
-
-        @pl.when(step < 7)
+        cols = pl.ds(pl.multiple_of(lax.rem(step - 1, 2) * CHUNK, CHUNK), CHUNK)
+
+        @pl.when(step < 3)
         def _():
             up_other[:, :, :, :, cols] = value
 
-        @pl.when(step >= 7)
+        @pl.when(step >= 3)
         def _():
             up_own[:, :, :, :, cols] = value
 
-    @at(6)
+    @at(2)
     def _():
         up.scatter0()
 
@@ -1203,29 +1452,28 @@
     @at(FIRST + PAIRS)
     def _():
         out_ref[...] = out.total()
-        for k in (1, 2):
-            rounds[k].arrive(0)
-            rounds[k].merge0()
-        rounds[0].add1(ra_ref, rb_ref)
+        rounds[0].add2(r_ref)
+        rounds[2].arrive(0)
+        rounds[2].merge0()
+        rounds[1].add1(ra_ref, rb_ref)
         down_ref[...] = down.total()
-        up.add2(up_ref)
-        down.drain(*range(1, 8))
+        up_ref[...] = up.total()
+        down.drain(*range(3, 8))
         out.drain(*range(8))
-        up.drain(*range(1, 5))
-        rounds[0].drain(0, 1, 2)
-        rounds[1].drain(0)
+        up.drain(*range(1, 8))
+        rounds[0].drain(*range(5))
+        rounds[1].drain(0, 1, 2)
         rounds[2].drain(0)
         for pair in range(PAIRS):
             kv_copy(pair).wait_send()
-        for k in range(16):
-            if k > 0:
-                early_copy(k).wait_recv()
+        early_copy(16).wait_recv()
+        for k in range(17):
             early_copy(k).wait_send()
         early_ref[...] = early_all[...]
 
 
 def middle_call(
-    act, d_low, att, d_attention, hidden, d_up, hidden1, payload, q, kv, d_att, lse, cos, sin, rows,
+    att, d_attention, hidden, d_up, hidden1, payload, down_a, down_b, q, kv, d_att, lse, cos, sin, rows,
 ):
     n = SLOTS * rows
     half = FF // 2
@@ -1256,7 +1504,7 @@
     def low(shape):
         return pltpu.VMEM(shape, BF16)
 
-    handed = ((4, ur, half), (2, 2, ur, WIDE), (2, 2, ur, WIDE), (2,) + half_shape(ur, WIDE))
+    handed = ((4, ur, WIDE), (2, 2, ur, WIDE), (2, 2, ur, WIDE), half_shape(ur, WIDE))
 
     return pl.pallas_call(
         middle_kernel,
@@ -1268,17 +1516,18 @@
             jax.ShapeDtypeStruct((n, D), BF16),
             jax.ShapeDtypeStruct((dr, dc), F32),
             jax.ShapeDtypeStruct((wr, dc), F32),
-        )
-        + tuple(jax.ShapeDtypeStruct(o, BF16) for o in handed + ((16, 16, D),)),
+            jax.ShapeDtypeStruct((ur, half), F32),
+        )
+        + tuple(jax.ShapeDtypeStruct(o, BF16) for o in handed + ((16, 96, 128),)),
         in_specs=[
-            pl.BlockSpec((n, D), lambda s: (0, clamp(s - 1, 0, 3))),
             whole((n, D)),
             whole((n, D)),
             whole((n, D)),
-            whole((n, D)),
-            pl.BlockSpec((n, CHUNK), lambda s: (0, clamp(s - 5, 0, 3))),
+            pl.BlockSpec((n, CHUNK), lambda s: (0, clamp(s - 1, 0, 3))),
             whole((n, D)),
             whole((16, D)),
+            whole((2, 2, dr, dc)),
+            whole((2, 2, dr, dc)),
             long(), second(), long(), long(), long(), long(), short(), short(), long(), second(),
             long(), second(),
             pl.BlockSpec((1, 4, rows), lambda s: (now(s), 0, 0)),
@@ -1291,58 +1540,52 @@
             pl.BlockSpec((n, PAIR), lambda s: (0, before(s))),
             whole((dr, dc)),
             whole((wr, dc)),
-        )
-        + tuple(whole(o) for o in handed + ((16, 16, D),)),
-        scratch_shapes=[low(half_shape(dr, dc))] * 3
-        + [low((2, 2, dr, dc))] * 2
-        + [low((4, dr, dc)), low((3, dr, dc))]
+            whole((ur, half)),
+        )
+        + tuple(whole(o) for o in handed + ((16, 96, 128),)),
+        scratch_shapes=[low((4, dr, dc)), low((3, dr, dc))]
         + [low(half_shape(wr, dc))] * 3
         + [low((2, 2, wr, dc))] * 2
         + [low((4, wr, dc)), low((3, wr, dc))]
         + [low(half_shape(ur, half))] * 3
         + [low((2, 2, ur, half))] * 2
-        + [low((4, ur, half))]
-        + [low((ROUNDS,) + half_shape(ur, WIDE))]
-        + [low((2, 2, ur, WIDE))] * 2
+        + [low((4, ur, half)), low((3, ur, half))]
+        + [low((ROUNDS,) + half_shape(ur, WIDE))] * 2
+        + [low((2, 2, 2, ur, WIDE))] * 2
+        + [low((4, ur, WIDE))]
         + [low((n, 2 * WIDE)), low((2, n, PAIR))]
         + [low((PAIRS, rows + SHORT, 2 * PAIR))] * 2
         + [pltpu.VMEM((2, rows, PAIR), F32)] * 2
         + [pltpu.VMEM((2, SHORT, PAIR), F32)] * 2
-        + [pltpu.VMEM((16, D), F32), low((16, D)), low((16, 16, D))]
-        + [DMA((37,)), DMA((37,)), DMA((PAIRS,)), DMA((PAIRS,)), DMA((16,)), DMA((16,))],
+        + [pltpu.VMEM((16, D), F32), low((96, 128)), low((16, 96, 128))]
+        + [DMA((43,)), DMA((43,)), DMA((PAIRS,)), DMA((PAIRS,)), DMA((17,)), DMA((17,))],
         compiler_params=pltpu.CompilerParams(
             collective_id=1, has_side_effects=True, vmem_limit_bytes=BIG
         ),
-        cost_estimate=cost(2 * n * D * (2 * FF + D) + 40 * D * rows * (LEN + SHORT), 50e6),
+        cost_estimate=cost(2 * n * D * (FF + 4 * D) + 40 * D * rows * (LEN + SHORT), 50e6),
     )(
-        act, d_low, att, d_attention, hidden, d_up, hidden1, payload, q, q, *kv, d_att, d_att,
+        att, d_attention, hidden, d_up, hidden1, payload, down_a, down_b, q, q, *kv, d_att, d_att,
         att, att, lse, cos, sin,
     )
 
 
 TILES = 4
-
-
-def pack_rows(rows):
-    parts = [rows[r : r + 1, c : c + 128] for r in range(5) for c in range(0, D, 128)]
-    return jnp.concatenate(parts + [jnp.zeros((2, 128), F32)], axis=0).astype(BF16)
 
 
 def end_kernel(
     tok_ref, dmid_ref, dq_ref, dk_ref, dv_ref, mod_ref, gain_ref, weight_ref, lengths,
-    up_in, ra, rb, rown,
-    grad_ref, gqkv_ref, gup_ref, late_ref,
-    up2, up3, r2, r3, last_a, last_b, sums, sums_came, sums_all, late_came,
+    r_in, ra, rb, rown,
+    grad_ref, gqkv_ref, late_ref,
+    r2, r3, last_a, last_b, sums, sums_came, sums_all, late_came,
     send, recv, send_late, recv_late,
 ):
     step = pl.program_id(0)
     s, me = lax.axis_index("seq"), lax.axis_index("span")
-    up = Scatter(send, recv, 0, came2=up2, came3=up3)
     rounds = [
         Scatter(
-            send, recv, 8 * (k + 1), own=rown.at[k - 1] if k else None,
-            a1=last_a.at[k - 1] if k else ra,
-            b1=last_b.at[k - 1] if k else rb,
+            send, recv, 8 * k, own=rown,
+            a1=last_a if k == 2 else ra,
+            b1=last_b if k == 2 else rb,
             came2=r2.at[k], came3=r3.at[k],
         )
         for k in range(ROUNDS)
@@ -1367,13 +1610,12 @@
 
     @at(0)
     def _():
-        up2[...] = up_in[...]
+        r2[0] = r_in[...]
         sums[...] = jnp.zeros_like(sums)
         greet([{"span": 1 - me}] + [{"seq": lax.rem(s + k, 16)} for k in range(1, 16)])
-        up.start(5, 6, 7)
-        rounds[0].start(3, 4)
-        rounds[1].start(1, 2)
         rounds[2].start(1, 2)
+        rounds[1].start(3, 4)
+        rounds[0].start(5, 6, 7)
 
     size = tok_ref.shape[0]
     j = step // 2
@@ -1408,25 +1650,21 @@
     @at(TILES - 1)
     def _():
         late_copy(0).start()
-        rounds[0].scatter3()
+        rounds[2].scatter2()
+        rounds[1].scatter3()
         late_copy(0).wait_recv()
-        sums_all[...] = pack_rows(sums[...] + sums_came[...])
+        sums_all[...] = pack_rows(sums[...] + sums_came[...], 5)
         for k in range(1, 16):
             late_copy(k).start()
-        rounds[1].scatter2()
-        rounds[2].scatter2()
-        rounds[1].scatter3()
         late_came[s] = sums_all[...]
         rounds[2].scatter3()
-        gup_ref[...] = up.total()
         for k in range(ROUNDS):
             total = rounds[k].total()
             for c in range(3):
                 cols = slice((c * ROUNDS + k) * PAIR, (c * ROUNDS + k + 1) * PAIR)
                 gqkv_ref[:, cols] = total[:, c * PAIR : (c + 1) * PAIR]
-        up.drain(5, 6, 7)
-        rounds[0].drain(*range(3, 8))
-        rounds[1].drain(*range(1, 8))
+        rounds[0].drain(*range(5, 8))
+        rounds[1].drain(*range(3, 8))
         rounds[2].drain(*range(1, 8))
         for k in range(16):
             if k > 0:
@@ -1450,7 +1688,6 @@
         out_shape=(
             jax.ShapeDtypeStruct((n, D), F32),
             jax.ShapeDtypeStruct((r, 3 * D // 2), F32),
-            jax.ShapeDtypeStruct((r, FF // 2), F32),
             jax.ShapeDtypeStruct((16, 32, 128), BF16),
         ),
         in_specs=[tile()] * 5
@@ -1464,22 +1701,19 @@
         out_specs=(
             tile(),
             whole((r, 3 * D // 2)),
-            whole((r, FF // 2)),
             whole((16, 32, 128)),
         ),
         scratch_shapes=[
-            pltpu.VMEM((4, r, FF // 2), BF16),
-            pltpu.VMEM((3, r, FF // 2), BF16),
             pltpu.VMEM((ROUNDS, 4, r, WIDE), BF16),
             pltpu.VMEM((ROUNDS, 3, r, WIDE), BF16),
-            pltpu.VMEM((2, 2, 2, r, WIDE), BF16),
-            pltpu.VMEM((2, 2, 2, r, WIDE), BF16),
+            pltpu.VMEM((2, 2, r, WIDE), BF16),
+            pltpu.VMEM((2, 2, r, WIDE), BF16),
             pltpu.VMEM((8, D), F32),
             pltpu.VMEM((8, D), F32),
             pltpu.VMEM((32, 128), BF16),
             pltpu.VMEM((16, 32, 128), BF16),
-            DMA((8 * (ROUNDS + 1),)),
-            DMA((8 * (ROUNDS + 1),)),
+            DMA((8 * ROUNDS,)),
+            DMA((8 * ROUNDS,)),
             DMA((16,)),
             DMA((16,)),
         ],
@@ -1490,49 +1724,45 @@
     )(tokens, d_mid, dq, dk, dv, mod, gain, weight, lengths, *handed)
 
 
-def exact(left, right, over):
-    return lax.dot_general(
-        left, right, (over, ((), ())), precision=HIGHEST, preferred_element_type=F32
-    )
-
-
-def exact(left, right, over):
-    return lax.dot_general(
-        left, right, (over, ((), ())), precision=HIGHEST, preferred_element_type=F32
-    )
+def thirds(value):
+    high = value.astype(BF16)
+    rest = value - high.astype(F32)
+    middle = rest.astype(BF16)
+    return [high, middle, (rest - middle.astype(F32)).astype(BF16)]
 
 
 def condition_kernel(
     lengths, early_ref, late_ref, table_ref, silu_ref, weight_ref,
-    qkv_in, out_in, up_in, down_in, sorted_any,
+    qkv_in, out_in, up_in, down_in, sorted_any, result_any,
     ada_ref, bias_ref, gcond_ref, gain1_ref, gain2_ref, bd_ref, bu_ref,
-    qkv_ref, out_ref, up_ref, down_ref, natural_any, stage, read, moved,
+    qkv_ref, out_ref, up_ref, down_ref, natural_any, final_any, stage, stage_out, read, moved,
 ):
     seq = late_ref.shape[0]
     me, s = lax.axis_index("span"), lax.axis_index("seq")
     half = sorted_any.shape[0] // SLOTS
-    reads = [
-        pltpu.make_async_copy(sorted_any.at[pl.ds(j * half, half)], stage.at[j], read.at[j])
-        for j in range(SLOTS)
-    ]
-    moves = [
-        pltpu.make_async_copy(
-            stage.at[j],
-            natural_any.at[pl.ds(pl.multiple_of(slot_of(lengths, j) * half, half), half)],
-            moved.at[j],
-        )
-        for j in range(SLOTS)
-    ]
+    reads, moves = [], []
+    given = ((sorted_any, stage, natural_any), (result_any, stage_out, final_any))
+    for i, (src, held, dst) in enumerate(given):
+        for j in range(SLOTS):
+            to = pl.ds(pl.multiple_of(slot_of(lengths, j) * half, half), half)
+            at = i * SLOTS + j
+            reads.append(
+                pltpu.make_async_copy(src.at[pl.ds(j * half, half)], held.at[j], read.at[at])
+            )
+            moves.append(pltpu.make_async_copy(held.at[j], dst.at[to], moved.at[at]))
     for copy in reads:
         copy.start()
     qkv_ref[...] = qkv_in[...]
     out_ref[...] = out_in[...]
     up_ref[...] = up_in[...]
     down_ref[...] = down_in[...]
-    for j in range(SLOTS):
-        reads[j].wait()
-        moves[j].start()
-    early = early_ref[...].astype(F32)
+    for come, go in zip(reads, moves):
+        come.wait()
+        go.start()
+    packed = early_ref[...].astype(F32)
+    early = [
+        jnp.concatenate([packed[:, 6 * r + c] for c in range(6)], axis=1) for r in range(14)
+    ]
     packed = late_ref[...].astype(F32)
     late = [
         jnp.concatenate([packed[:, 6 * r + c] for c in range(6)], axis=1) for r in range(5)
@@ -1540,26 +1770,29 @@
     mods = []
     for k in range(SLOTS):
         mods.append(
-            [late[2 * k], late[2 * k + 1]] + [early[:, 4 * k + b] for b in range(4)]
+            [late[2 * k], late[2 * k + 1]] + [early[4 * k + b] for b in range(4)]
         )
     gain1_ref[...] = jnp.sum(late[4], axis=0)
-    gain2_ref[...] = jnp.sum(early[:, 8], axis=0)
-    bd_ref[...] = jnp.sum(early[:, 9], axis=0)
+    gain2_ref[...] = jnp.sum(early[8], axis=0)
+    bd_ref[...] = jnp.sum(early[9], axis=0)
     for f in range(4):
-        bu_ref[f * D : (f + 1) * D] = jnp.sum(early[:, 10 + f], axis=0)
-    own = [jnp.zeros((8, D), F32)] * 6
-    row = lax.broadcasted_iota(jnp.int32, (8, seq), 0)
-    wanted = (s * SLOTS + row).astype(F32)
-    for k in range(SLOTS):
-        asked = table_ref[:, SLOTS + k, :].T[:8]
-        chosen = jnp.where(jnp.logical_and(asked == wanted, row < SLOTS), 1.0, 0.0)
-        for b in range(6):
-            own[b] = own[b] + exact(chosen, mods[k][b], ((1,), (0,)))
-    d_silu = jnp.zeros((8, 128), F32)
+        bu_ref[f * D : (f + 1) * D] = jnp.sum(early[10 + f], axis=0)
+    own = []
+    asked = [
+        jnp.concatenate([table_ref[:, SLOTS + k, :]] * 6, axis=1) for k in range(SLOTS)
+    ]
     for b in range(6):
         cols = slice(b * D, (b + 1) * D)
         bias_ref[cols] = jnp.sum(mods[0][b] + mods[1][b], axis=0)
-        d_silu += exact(own[b], weight_ref[:, cols].astype(F32), ((1,), (1,)))
+        rows = []
+        for r in range(SLOTS):
+            wanted = (s * SLOTS + r).astype(F32)
+            picked = [jnp.where(asked[k] == wanted, mods[k][b], 0.0) for k in range(SLOTS)]
+            rows.append(col_sum(picked[0] + picked[1]))
+        own.append(jnp.concatenate(rows + [jnp.zeros((8 - SLOTS, D), F32)], axis=0))
+    own = jnp.concatenate(own, axis=1)
+    d_silu = nt(jnp.concatenate(thirds(own), axis=0), weight_ref[...])
+    d_silu = d_silu[:8] + d_silu[8:16] + d_silu[16:24]
     v = table_ref[s]
     sig = 1.0 / (1.0 + jnp.exp(-v))
     gcond_ref[...] = (d_silu * (sig * (1.0 + v * (1.0 - sig))))[:SLOTS]
@@ -1568,18 +1801,18 @@
         s * rows + lax.broadcasted_iota(jnp.int32, (rows, 128), 0)
     )
     pick = jnp.where(pick, 1.0, 0.0)
-    silu = [exact(pick, silu_ref[k], ((1,), (1,))) for k in range(SLOTS)]
+    silu = [nt(pick.astype(BF16), silu_ref[k].astype(BF16)).astype(BF16) for k in range(SLOTS)]
+    silu = jnp.concatenate(silu * 3, axis=1)
     for b in range(3):
-        total = jnp.zeros((rows, D), F32)
-        for k in range(SLOTS):
-            block = jnp.where(me == 0, mods[k][b], mods[k][3 + b])
-            total += exact(silu[k], block, ((1,), (0,)))
-        ada_ref[:, b * D : (b + 1) * D] = total
+        blocks = [jnp.where(me == 0, mods[k][b], mods[k][3 + b]) for k in range(SLOTS)]
+        split = [part for part in zip(*(thirds(block) for block in blocks))]
+        right = jnp.concatenate([block for part in split for block in part], axis=0)
+        ada_ref[:, b * D : (b + 1) * D] = nn(silu, right)
     for move in moves:
         move.wait()
 
 
-def condition_call(lengths, early, late, table, silu, ada_weight, tiles, grad_in):
+def condition_call(lengths, early, late, table, silu, ada_weight, tiles, grad_in, result):
     seq = late.shape[0]
 
     def all_of(shape):
@@ -1591,19 +1824,23 @@
     return pl.pallas_call(
         condition_kernel,
         name="condition",
-        out_shape=tuple(jax.ShapeDtypeStruct(o, F32) for o in outs + (grad_in.shape,)),
+        out_shape=tuple(jax.ShapeDtypeStruct(o, F32) for o in outs + (grad_in.shape,))
+        + (jax.ShapeDtypeStruct(result.shape, BF16),),
         grid_spec=pltpu.PrefetchScalarGridSpec(
             num_scalar_prefetch=1,
             grid=(1,),
-            in_specs=[whole(a.shape) for a in given] + [ANY],
-            out_specs=[all_of(o) for o in outs] + [ANY],
+            in_specs=[whole(a.shape) for a in given] + [ANY] * 2,
+            out_specs=[all_of(o) for o in outs] + [ANY] * 2,
             scratch_shapes=[
-                pltpu.VMEM((SLOTS, grad_in.shape[0] // SLOTS, D), F32), DMA((SLOTS,)), DMA((SLOTS,)),
+                pltpu.VMEM((SLOTS, grad_in.shape[0] // SLOTS, D), F32),
+                pltpu.VMEM((SLOTS, grad_in.shape[0] // SLOTS, D), BF16),
+                DMA((2 * SLOTS,)),
+                DMA((2 * SLOTS,)),
             ],
         ),
         compiler_params=pltpu.CompilerParams(vmem_limit_bytes=BIG),
         cost_estimate=cost(1e7, 12e6),
-    )(lengths, *given, grad_in)
+    )(lengths, *given, grad_in, result)
 
 
 def from_peers(array, span):
@@ -1631,14 +1868,18 @@
     )
     fast = seq == 16 and span == 2
     cos, sin = (jnp.asarray(table) for table in rotary(LEN))
-    mod, table, silu_all = modulation_call(conditions, assignment, ada_weight, ada_bias, seq)
-
     tokens2 = tokens.reshape(flat, D)
     gain1, gain2 = norm1_gain, norm2_gain
     if fast:
-        q, hidden1, kv, kvx = share_call(tokens2, mod, gain1, qkv_weight, cos, sin, rows)
-        att, lse, q, *kv = attend_sorted_call(lengths, q, kv, kvx, rows)
+        q, hidden1, kv, mod, table, silu_all, kvx = share_call(
+            conditions, assignment, ada_weight, ada_bias, tokens2, gain1, qkv_weight, cos, sin,
+            rows,
+        )
+        att, lse, q, *kv, tokens2, cot, hidden1 = attend_sorted_call(
+            lengths, q, kv, kvx, tokens2, cotangent.reshape(flat, D), hidden1, rows
+        )
     else:
+        mod, table, _ = modulation_call(conditions, assignment, ada_weight, ada_bias, seq)
         q, hidden1, kv_long, kv_tail = project_call(
             place, tokens2, mod, gain1, qkv_weight, cos, sin, rows
         )
@@ -1647,6 +1888,30 @@
         sent = [lax.ppermute(kv_short, "span", [(0, i)]) for i in range(1, span)]
         kv_short = jnp.where(span_at == 0, kv_short, sum(sent[1:], sent[0]))
         att, lse = attend_call(q, kv_long, kv_other, kv_short, rows)
+    if fast:
+        out, d_mid, d_att, hidden2, d_up, d_attention, payload, *handed = both_call(
+            tokens2, att, cot, mod, gain2, out_weight, up_weight, up_bias, down_weight,
+            down_bias, lengths, rows,
+        )
+        dq, dk, dv, grad_down, grad_out, grad_up, *handed, early = middle_call(
+            att, d_attention, hidden2, d_up, hidden1, payload, *handed, q, kv, d_att, lse,
+            cos, sin, rows,
+        )
+        grad_in, grad_qkv, late = end_call(
+            tokens2, d_mid, dq, dk, dv, mod, gain1, qkv_weight, lengths, handed, rows
+        )
+        (
+            grad_ada, ada_bias_sum, grad_cond, gain1_sum, gain2_sum, bd_sum, bu_sum,
+            grad_qkv, grad_out, grad_up, grad_down, grad_in, out,
+        ) = condition_call(
+            lengths, early, late, table, silu_all, ada_weight,
+            (grad_qkv, grad_out, grad_up, grad_down), grad_in, out,
+        )
+        return (
+            out.reshape(tokens.shape), grad_in.reshape(tokens.shape), grad_cond, gain1_sum,
+            grad_ada, ada_bias_sum, grad_qkv, grad_out, gain2_sum, grad_up, bu_sum, grad_down,
+            bd_sum,
+        )
     (
         out, d_mid, d_att, act, d_low, hidden2, d_up, d_attention, payload, tokens_sorted,
         hidden1_sorted,
@@ -1654,26 +1919,6 @@
         fast, lengths, tokens2, att, cotangent.reshape(flat, D), hidden1, mod, gain2, out_weight,
         up_weight, up_bias, down_weight, down_bias, rows,
     )
-    if fast:
-        dq, dk, dv, grad_down, grad_out, *handed, early = middle_call(
-            act, d_low, att, d_attention, hidden2, d_up, hidden1_sorted, payload, q, kv, d_att,
-            lse, cos, sin, rows,
-        )
-        grad_in, grad_qkv, grad_up, late = end_call(
-            tokens_sorted, d_mid, dq, dk, dv, mod, gain1, qkv_weight, lengths, handed, rows
-        )
-        (
-            grad_ada, ada_bias_sum, grad_cond, gain1_sum, gain2_sum, bd_sum, bu_sum,
-            grad_qkv, grad_out, grad_up, grad_down, grad_in,
-        ) = condition_call(
-            lengths, early, late, table, silu_all, ada_weight,
-            (grad_qkv, grad_out, grad_up, grad_down), grad_in,
-        )
-        return (
-            out.reshape(tokens.shape), grad_in.reshape(tokens.shape), grad_cond, gain1_sum,
-            grad_ada, ada_bias_sum, grad_qkv, grad_out, gain2_sum, grad_up, bu_sum, grad_down,
-            bd_sum,
-        )
     grad_down = weight_gradient(act, d_low)
     grad_up = weight_gradient(hidden2, d_up)
     grad_out = weight_gradient(att, d_attention)

time: 203 us -> 195 us (0.961)
  Pallas kernels: 202 us -> 194 us
    pallas_call x1, Pallas kernels: 80 us -> 67.6 us  [middle_call(): pl.pallas_call(middle_kernel, name='middle', grid=(FIRST + PAIRS + 1,), o...]
    pallas_call x1, Pallas kernels: 13.2 us -> 22.9 us  [share_call(): pl.pallas_call(share_kernel, name='project', grid=(steps,), out_shape=(ja...]
    pallas_call x1, Pallas kernels: 33.9 us -> 26.7 us  [end_call(): pl.pallas_call(end_kernel, name='end', grid=(TILES,), out_shape=(jax.Shap...]
    pallas_call x2 -> x1, Pallas kernels: 50.1 us -> 52.7 us  [both_call(): pl.pallas_call(both_kernel, name='feed', grid=(3 * tiles,), out_shape=(ja...]
where the time goes in v5:
time: 195 us
  Pallas kernels  194 us (99%)
    pallas_call x1, Pallas kernels, middle_call(): pl.pallas_call(middle_kernel, name='middle', grid=(FIRST + PAIRS + 1,), o...  67.6 us
    pallas_call x1, Pallas kernels, both_call(): pl.pallas_call(both_kernel, name='feed', grid=(3 * tiles,), out_shape=(ja...  52.7 us
    pallas_call x1, Pallas kernels, end_call(): pl.pallas_call(end_kernel, name='end', grid=(TILES,), out_shape=(jax.Shap...  26.7 us
    pallas_call x1, Pallas kernels, share_call(): pl.pallas_call(share_kernel, name='project', grid=(steps,), out_shape=(ja...  22.9 us
    pallas_call x1, Pallas kernels, attend_sorted_call(): pl.pallas_call(attend_sorted_kernel, name='attend', out_shape=(jax.ShapeD...  17.2 us
    pallas_call x1, Pallas kernels, condition_call(): pl.pallas_call(condition_kernel, name='condition', out_shape=tuple((jax.S...  7.05 us

profile of v5, /device:TPU:0, one launch (start us, length us, event | category | flops | bytes accessed | tf_op | source)
XLA Modules:
  0.0 195.0 jit_solution(13162458424975178623)
XLA Ops:
  0.6 22.9 %project.1 = (bf16[1024,768]{1,0:T(8,128)(2,1)}, bf16[1024,768]{1,0:T(8,128)(2,1)}, bf16[1024,1536]{1,0:T(8,128)(2,1)}, f32[8,4608]{1,0:T(8,128)}, f32[16,8,128]...) custom-call(bf16[2,128]{1,0:T(2,128)(2,1)} %cond_ref.1, s32[2]{0:T(128)} %assign_ref.1, ...), custom_call_target="tpu_custom_call" | custom-call | flops 3623878656 | bytes 14000000 | tf_op jit(solution)/shard_map/project/pallas_call | solution.py:762
  23.6 17.2 %attend.1 = (bf16[1024,768]{1,0:T(8,128)(2,1)}, f32[6,4,512]{2,1,0:T(4,128)}, bf16[1024,768]{1,0:T(8,128)(2,1)}, bf16[512,768]{1,0:T(8,128)(2,1)}, bf16[512,768]...) custom-call(s32[2]{0:T(128)} %lengths.7, ...), custom_call_target="tpu_custom_call" | custom-call | flops 7247757312 | bytes 16000000 | tf_op jit(solution)/shard_map/attend/pallas_call | solution.py:850
  40.8 52.7 %feed.1 = (bf16[1024,768]{1,0:T(8,128)(2,1)}, f32[1024,768]{1,0:T(8,128)}, bf16[1024,768]{1,0:T(8,128)(2,1)}, bf16[1024,768]{1,0:T(8,128)(2,1)}, bf16[1024,3072]...) custom-call(bf16[1024,768]{1,0:T(8,128)(2,1)} %get-tuple-element.73., ...), custom_call_target="tpu_custom_call" | custom-call | flops 26575110144 | bytes 40000000 | tf_op jit(solution)/shard_map/feed/pallas_call | solution.py:1171
  93.5 67.6 %middle.1 = (bf16[1024,768]{1,0:T(8,128)(2,1)}, bf16[1024,768]{1,0:T(8,128)(2,1)}, bf16[1024,768]{1,0:T(8,128)(2,1)}, f32[192,384]{1,0:T(8,128)}, f32[48,384]{1,...) custom-call(bf16[1024,768]{1,0:T(8,128)(2,1)} %get-tuple-element.72., ...), custom_call_target="tpu_custom_call" | custom-call | flops 27783069696 | bytes 50000000 | tf_op jit(solution)/shard_map/middle/pallas_call | solution.py:1509
  161.1 26.7 %end.1 = (f32[1024,768]{1,0:T(8,128)}, f32[48,1152]{1,0:T(8,128)}, bf16[16,32,128]{2,1,0:T(8,128)(2,1)}) custom-call(bf16[1024,768]{1,0:T(8,128)(2,1)} %get-tuple-element.73.tok_ref, f32[1024,768]{1,0:T(8,128)} %get-tuple-element.93.dmid_ref, bf16[1024,768]{1,0:T(8,128)(2,1)} %get-tuple-element.94.dq_ref, bf16[1024,768]{1,0:T(8,128)(2,1)} %get-tuple-element.95.dk_ref, ...), custom_call_target="tpu_custom_call" | custom-call | flops 3623878656 | bytes 22000000 | tf_op jit(solution)/shard_map/end/pallas_call | solution.py:1684
  187.8 7.0 %condition.1 = (f32[8,2304]{1,0:T(8,128)}, f32[4608]{0:T(1024)}, f32[2,128]{1,0:T(2,128)}, f32[768]{0:T(1024)}, f32[768]{0:T(1024)}, /*index=5*/f32[768]{0:T(102...) custom-call(s32[2]{0:T(128)} %lengths.7, ...), custom_call_target="tpu_custom_call" | custom-call | flops 10000000 | bytes 12000000 | tf_op jit(solution)/shard_map/condition/pallas_call | solution.py:1824

commit v6 on v5

--- a/solution.py
+++ b/solution.py
@@ -100,7 +100,7 @@
 
 def modulation_kernel(
     n, cond_ref, assign_ref, weight_ref, bias_ref, mod_ref, table_ref, silu_ref,
-    own_ref, send, recv, local, extra=(),
+    own_ref, send, recv, local, extra=(), ready=None,
 ):
     me = lax.axis_index("seq")
     asked = [jnp.full((1, 128), assign_ref[k].astype(F32)) for k in range(SLOTS)]
@@ -132,6 +132,8 @@
     mine.wait()
     for copy in copies:
         copy.wait()
+    if ready is not None:
+        ready()
     source = lax.broadcasted_iota(jnp.int32, (n, 128), 0).astype(F32) * SLOTS
     rows = []
     for slot in range(SLOTS):
@@ -693,9 +695,9 @@
 
 
 def share_kernel(
-    cond_ref, assign_ref, ada_ref, bias_ref, tok_ref, gain_ref, weight_ref, cos_ref, sin_ref,
+    cond_ref, assign_ref, ada_any, bias_ref, tok_ref, gain_ref, weight_any, cos_ref, sin_ref,
     q_ref, h_ref, kv_ref, mod_ref, table_out, silu_ref, kvx_any,
-    stage, table_ref, send, recv, own_ref, send_cond, recv_cond, local,
+    stage, table_ref, ada_ref, weight_ref, send, recv, own_ref, send_cond, recv_cond, local, loaded,
 ):
     step = pl.program_id(0)
     steps = stage.shape[0]
@@ -714,10 +716,17 @@
 
     @pl.when(step == 0)
     def _():
+        loads = [
+            pltpu.make_async_copy(ada_any, ada_ref, loaded.at[0]),
+            pltpu.make_async_copy(weight_any, weight_ref, loaded.at[1]),
+        ]
+        for load in loads:
+            load.start()
         modulation_kernel(
             table_ref.shape[0], cond_ref, assign_ref, ada_ref, bias_ref, mod_ref, table_ref,
-            silu_ref, own_ref, send_cond, recv_cond, local, ({"span": 1 - me},),
-        )
+            silu_ref, own_ref, send_cond, recv_cond, local, ({"span": 1 - me},), loads[0].wait,
+        )
+        loads[1].wait()
         table_out[...] = table_ref[...]
 
     row = mod_ref[pl.ds(step // (steps // SLOTS), 1), :]
@@ -775,11 +784,11 @@
         in_specs=[
             whole((SLOTS, 128)),
             pl.BlockSpec(memory_space=pltpu.SMEM),
-            whole((128, 6 * D)),
+            pl.BlockSpec(memory_space=pl.ANY),
             whole((6 * D,)),
             at(D),
             whole((D,)),
-            whole((D, 3 * D)),
+            pl.BlockSpec(memory_space=pl.ANY),
             whole((LEN, PAIR)),
             whole((LEN, PAIR)),
         ],
@@ -790,12 +799,15 @@
         scratch_shapes=[
             pltpu.VMEM((steps, tile, 2 * D), BF16),
             pltpu.VMEM((16, 8, 128), F32),
+            pltpu.VMEM((128, 6 * D), BF16),
+            pltpu.VMEM((D, 3 * D), BF16),
             pltpu.SemaphoreType.DMA((steps,)),
             pltpu.SemaphoreType.DMA((steps,)),
             pltpu.VMEM((8, 128), F32),
             pltpu.SemaphoreType.DMA((16,)),
             pltpu.SemaphoreType.DMA((16,)),
             pltpu.SemaphoreType.DMA,
+            pltpu.SemaphoreType.DMA((2,)),
         ],
         compiler_params=pltpu.CompilerParams(
             collective_id=4, has_side_effects=True, vmem_limit_bytes=BIG
@@ -1017,15 +1029,18 @@
 
 
 def both_kernel(
-    tok_ref, att_ref, cot_ref, mod_ref, gain_ref, wo_ref, wu_ref, bu_ref, wd_any, bd_ref, lengths,
+    tok_ref, att_ref, cot_ref, mod_ref, gain_ref, wo_any, wu_any, bu_ref, wd_any, bd_ref, lengths,
     out_ref, dmid_ref, datt_ref, h_ref, dup_ref, dattn_ref, payload_ref, a_ref, b_ref,
     act_all, slope_all, dlow_all, mid_all, attention_all,
-    wd_ref, other, own, came0, a1, b1, send, recv, loaded,
+    wo_ref, wu_ref, wd_ref, other, own, came0, a1, b1, send, recv, loaded,
 ):
     step = pl.program_id(0)
     me = lax.axis_index("span")
     down = Scatter(send, recv, 0, other=other, own=own, came0=came0, a1=a1, b1=b1)
-    load = pltpu.make_async_copy(wd_any, wd_ref, loaded)
+    loads = [
+        pltpu.make_async_copy(src, dst, loaded.at[k])
+        for k, (src, dst) in enumerate([(wo_any, wo_ref), (wu_any, wu_ref), (wd_any, wd_ref)])
+    ]
     tiles = act_all.shape[0] // tok_ref.shape[0]
     tile = tok_ref.shape[0]
     t = lax.rem(step, tiles)
@@ -1040,12 +1055,16 @@
 
     @pl.when(step == 0)
     def _():
-        load.start()
+        loads[0].start()
+        loads[1].start()
         greet(plane_peers())
+        loads[0].wait()
+        loads[1].wait()
+        loads[2].start()
 
     @pl.when(step == 2 * tiles)
     def _():
-        load.wait()
+        loads[2].wait()
         down.arrive(8, 9, 10, 11)
         down.merge0()
         down.start(1, 2)
@@ -1189,8 +1208,8 @@
             pl.BlockSpec((tile, D), lambda s: (lax.rem(s, tiles), 0)),
             whole((8, 6 * D)),
             whole((D,)),
-            whole((D, D)),
-            whole((D, FF)),
+            ANY,
+            ANY,
             whole((FF,)),
             ANY,
             whole((D,)),
@@ -1206,10 +1225,10 @@
             pltpu.VMEM((n, D), F32),
             pltpu.VMEM((n, D), F32),
         ]
-        + [low(FF, D)]
+        + [low(D, D), low(D, FF), low(FF, D)]
         + [low(*half_shape(dr, dc))] * 3
         + [low(2, 2, dr, dc)] * 2
-        + [DMA((12,)), DMA((12,)), DMA],
+        + [DMA((12,)), DMA((12,)), DMA((3,))],
         compiler_params=pltpu.CompilerParams(
             collective_id=2, has_side_effects=True, vmem_limit_bytes=BIG
         ),
@@ -1231,15 +1250,15 @@
 
 
 def middle_kernel(
-    att_ref, dattn_ref, h_ref, dup_ref, hid1_ref, payload_ref, down_a, down_b,
+    att_ref, dattn_ref, h_any, dup_ref, hid1_any, payload_ref, down_a, down_b,
     ql, qs, ko, vo, kx, vx, ks, vs, dol, dos, al, as_, lse, cos_ref, sin_ref,
     dq_ref, dk_ref, dv_ref, down_ref, out_ref, up_ref, r_ref, ra_ref, rb_ref, rown_ref, early_ref,
-    down2, down3,
+    h_ref, hid1_ref, down2, down3,
     out_other, out_own, out_came, out_a, out_b, out2, out3,
     up_other, up_own, up_came, up_a, up_b, up2, up3,
     round_other, round_came, round_a, round_b, round2, d_round, keep_q,
     leave, come, keep_k, keep_v, keep_sk, keep_sv, early_came, early_sum, early_all,
-    send, recv, send_kv, recv_kv, send_early, recv_early,
+    send, recv, send_kv, recv_kv, send_early, recv_early, loaded,
 ):
     step = pl.program_id(0)
     s, me = lax.axis_index("seq"), lax.axis_index("span")
@@ -1278,6 +1297,11 @@
             device_id={"span": 1 - me},
             device_id_type=MESH,
         )
+
+    loads = [
+        pltpu.make_async_copy(h_any, h_ref, loaded.at[0]),
+        pltpu.make_async_copy(hid1_any, hid1_ref, loaded.at[1]),
+    ]
 
     def early_copy(k):
         half = pl.ds(pl.multiple_of(me * 48, 16), 48)
@@ -1302,6 +1326,8 @@
 
     @at(0)
     def _():
+        for load in loads:
+            load.start()
         greet([{"span": 1 - me}] + [{"seq": lax.rem(s + k, 16)} for k in range(1, 16)])
         down.start(3, 4)
         early_copy(0).start()
@@ -1321,6 +1347,11 @@
             early_copy(k).wait_recv()
         early_copy(16).start()
 
+    @at(1)
+    def _():
+        for load in loads:
+            load.wait()
+
     @at(2)
     def _():
         out.scatter1()
@@ -1353,12 +1384,12 @@
     def _():
         up.scatter3()
 
-    @at(FIRST + 5)
-    def _():
-        rounds[0].scatter2()
-        rounds[1].scatter1()
-
     def between():
+        @at(FIRST + 5)
+        def _():
+            rounds[0].scatter2()
+            rounds[1].scatter1()
+
         @at(FIRST + 2)
         def _():
             up.scatter2()
@@ -1522,9 +1553,9 @@
         in_specs=[
             whole((n, D)),
             whole((n, D)),
-            whole((n, D)),
+            ANY,
             pl.BlockSpec((n, CHUNK), lambda s: (0, clamp(s - 1, 0, 3))),
-            whole((n, D)),
+            ANY,
             whole((16, D)),
             whole((2, 2, dr, dc)),
             whole((2, 2, dr, dc)),
@@ -1543,7 +1574,7 @@
             whole((ur, half)),
         )
         + tuple(whole(o) for o in handed + ((16, 96, 128),)),
-        scratch_shapes=[low((4, dr, dc)), low((3, dr, dc))]
+        scratch_shapes=[low((n, D)), low((n, D)), low((4, dr, dc)), low((3, dr, dc))]
         + [low(half_shape(wr, dc))] * 3
         + [low((2, 2, wr, dc))] * 2
         + [low((4, wr, dc)), low((3, wr, dc))]
@@ -1558,7 +1589,7 @@
         + [pltpu.VMEM((2, rows, PAIR), F32)] * 2
         + [pltpu.VMEM((2, SHORT, PAIR), F32)] * 2
         + [pltpu.VMEM((16, D), F32), low((96, 128)), low((16, 96, 128))]
-        + [DMA((43,)), DMA((43,)), DMA((PAIRS,)), DMA((PAIRS,)), DMA((17,)), DMA((17,))],
+        + [DMA((43,)), DMA((43,)), DMA((PAIRS,)), DMA((PAIRS,)), DMA((17,)), DMA((17,)), DMA((2,))],
         compiler_params=pltpu.CompilerParams(
             collective_id=1, has_side_effects=True, vmem_limit_bytes=BIG
         ),
@@ -1573,11 +1604,11 @@
 
 
 def end_kernel(
-    tok_ref, dmid_ref, dq_ref, dk_ref, dv_ref, mod_ref, gain_ref, weight_ref, lengths,
+    tok_ref, dmid_ref, dq_ref, dk_ref, dv_ref, mod_ref, gain_ref, weight_any, lengths,
     r_in, ra, rb, rown,
     grad_ref, gqkv_ref, late_ref,
-    r2, r3, last_a, last_b, sums, sums_came, sums_all, late_came,
-    send, recv, send_late, recv_late,
+    weight_ref, r2, r3, last_a, last_b, sums, sums_came, sums_all, late_came,
+    send, recv, send_late, recv_late, loaded,
 ):
     step = pl.program_id(0)
     s, me = lax.axis_index("seq"), lax.axis_index("span")
@@ -1610,12 +1641,15 @@
 
     @at(0)
     def _():
+        load = pltpu.make_async_copy(weight_any, weight_ref, loaded)
+        load.start()
         r2[0] = r_in[...]
         sums[...] = jnp.zeros_like(sums)
         greet([{"span": 1 - me}] + [{"seq": lax.rem(s + k, 16)} for k in range(1, 16)])
         rounds[2].start(1, 2)
         rounds[1].start(3, 4)
         rounds[0].start(5, 6, 7)
+        load.wait()
 
     size = tok_ref.shape[0]
     j = step // 2
@@ -1694,7 +1728,7 @@
         + [
             whole((8, 6 * D)),
             whole((D,)),
-            whole((D, 3 * D)),
+            ANY,
             pl.BlockSpec(memory_space=pltpu.SMEM),
         ]
         + [whole(a.shape) for a in handed],
@@ -1704,6 +1738,7 @@
             whole((16, 32, 128)),
         ),
         scratch_shapes=[
+            pltpu.VMEM((D, 3 * D), BF16),
             pltpu.VMEM((ROUNDS, 4, r, WIDE), BF16),
             pltpu.VMEM((ROUNDS, 3, r, WIDE), BF16),
             pltpu.VMEM((2, 2, r, WIDE), BF16),
@@ -1716,6 +1751,7 @@
             DMA((8 * ROUNDS,)),
             DMA((16,)),
             DMA((16,)),
+            DMA,
         ],
         compiler_params=pltpu.CompilerParams(
             collective_id=3, has_side_effects=True, vmem_limit_bytes=BIG

time: 195 us -> 190 us (0.974)
  Pallas kernels: 194 us -> 189 us
    pallas_call x1, Pallas kernels: 26.7 us -> 24.5 us  [end_call(): pl.pallas_call(end_kernel, name='end', grid=(TILES,), out_shape=(jax.Shap...]
where the time goes in v6:
time: 190 us
  Pallas kernels  189 us (99%)
    pallas_call x1, Pallas kernels, middle_call(): pl.pallas_call(middle_kernel, name='middle', grid=(FIRST + PAIRS + 1,), o...  66.3 us
    pallas_call x1, Pallas kernels, both_call(): pl.pallas_call(both_kernel, name='feed', grid=(3 * tiles,), out_shape=(ja...  52.2 us
    pallas_call x1, Pallas kernels, end_call(): pl.pallas_call(end_kernel, name='end', grid=(TILES,), out_shape=(jax.Shap...  24.5 us
    pallas_call x1, Pallas kernels, share_call(): pl.pallas_call(share_kernel, name='project', grid=(steps,), out_shape=(ja...  21.5 us
    pallas_call x1, Pallas kernels, attend_sorted_call(): pl.pallas_call(attend_sorted_kernel, name='attend', out_shape=(jax.ShapeD...  17.2 us
    pallas_call x1, Pallas kernels, condition_call(): pl.pallas_call(condition_kernel, name='condition', out_shape=tuple((jax.S...  7.05 us

profile of v6, /device:TPU:0, one launch (start us, length us, event | category | flops | bytes accessed | tf_op | source)
XLA Modules:
  0.0 189.8 jit_solution(2567537166934858244)
XLA Ops:
  0.6 21.5 %project.1 = (bf16[1024,768]{1,0:T(8,128)(2,1)}, bf16[1024,768]{1,0:T(8,128)(2,1)}, bf16[1024,1536]{1,0:T(8,128)(2,1)}, f32[8,4608]{1,0:T(8,128)}, f32[16,8,128]...) custom-call(bf16[2,128]{1,0:T(2,128)(2,1)} %cond_ref.1, s32[2]{0:T(128)} %assign_ref.1, ...), custom_call_target="tpu_custom_call" | custom-call | flops 3623878656 | bytes 14000000 | tf_op jit(solution)/shard_map/project/pallas_call | solution.py:771
  22.2 17.2 %attend.1 = (bf16[1024,768]{1,0:T(8,128)(2,1)}, f32[6,4,512]{2,1,0:T(4,128)}, bf16[1024,768]{1,0:T(8,128)(2,1)}, bf16[512,768]{1,0:T(8,128)(2,1)}, bf16[512,768]...) custom-call(s32[2]{0:T(128)} %lengths.7, ...), custom_call_target="tpu_custom_call" | custom-call | flops 7247757312 | bytes 16000000 | tf_op jit(solution)/shard_map/attend/pallas_call | solution.py:862
  39.4 52.2 %feed.1 = (bf16[1024,768]{1,0:T(8,128)(2,1)}, f32[1024,768]{1,0:T(8,128)}, bf16[1024,768]{1,0:T(8,128)(2,1)}, bf16[1024,768]{1,0:T(8,128)(2,1)}, bf16[1024,3072]...) custom-call(bf16[1024,768]{1,0:T(8,128)(2,1)} %get-tuple-element.73., ...), custom_call_target="tpu_custom_call" | custom-call | flops 26575110144 | bytes 40000000 | tf_op jit(solution)/shard_map/feed/pallas_call | solution.py:1190
  91.6 66.3 %middle.1 = (bf16[1024,768]{1,0:T(8,128)(2,1)}, bf16[1024,768]{1,0:T(8,128)(2,1)}, bf16[1024,768]{1,0:T(8,128)(2,1)}, f32[192,384]{1,0:T(8,128)}, f32[48,384]{1,...) custom-call(bf16[1024,768]{1,0:T(8,128)(2,1)} %get-tuple-element.72., ...), custom_call_target="tpu_custom_call" | custom-call | flops 27783069696 | bytes 50000000 | tf_op jit(solution)/shard_map/middle/pallas_call | solution.py:1540
  158.0 24.5 %end.1 = (f32[1024,768]{1,0:T(8,128)}, f32[48,1152]{1,0:T(8,128)}, bf16[16,32,128]{2,1,0:T(8,128)(2,1)}) custom-call(bf16[1024,768]{1,0:T(8,128)(2,1)} %get-tuple-element.73.tok_ref, f32[1024,768]{1,0:T(8,128)} %get-tuple-element.93.dmid_ref, bf16[1024,768]{1,0:T(8,128)(2,1)} %get-tuple-element.94.dq_ref, bf16[1024,768]{1,0:T(8,128)(2,1)} %get-tuple-element.95.dk_ref, ...), custom_call_target="tpu_custom_call" | custom-call | flops 3623878656 | bytes 22000000 | tf_op jit(solution)/shard_map/end/pallas_call | solution.py:1718
  182.5 7.0 %condition.1 = (f32[8,2304]{1,0:T(8,128)}, f32[4608]{0:T(1024)}, f32[2,128]{1,0:T(2,128)}, f32[768]{0:T(1024)}, f32[768]{0:T(1024)}, /*index=5*/f32[768]{0:T(102...) custom-call(s32[2]{0:T(128)} %lengths.7, ...), custom_call_target="tpu_custom_call" | custom-call | flops 10000000 | bytes 12000000 | tf_op jit(solution)/shard_map/condition/pallas_call | solution.py:1860

commit v7 on v6

--- a/solution.py
+++ b/solution.py
@@ -18,6 +18,7 @@
 SHORT = 128
 SLOTS = 2
 CHUNK = 768
+STRIP = 1536
 EPSILON = 1e-5
 LOG2E = 1.4426950408889634
 GELU_C = 0.7978845608028654
@@ -833,14 +834,14 @@
     vs_ref[...] = vs
     for ref, given in ((ko_ref, ko), (vo_ref, vo), (kx_ref, kx), (vx_ref, vx)):
         ref[...] = given[...]
+    out, stats = attend_slot(qs[...], [ks], [vs])
+    out_ref[rows:, :] = out
+    lse_ref[0, 2:3, :] = stats[0]
+    lse_ref[0, 3:4, :] = stats[1]
     out, stats = attend_slot(ql[...], [ko[...], kx[...]], [vo[...], vx[...]])
     out_ref[:rows, :] = out
     lse_ref[0, 0:1, :] = stats[0]
     lse_ref[0, 1:2, :] = stats[1]
-    out, stats = attend_slot(qs[...], [ks], [vs])
-    out_ref[rows:, :] = out
-    lse_ref[0, 2:3, :] = stats[0]
-    lse_ref[0, 3:4, :] = stats[1]
 
 
 def attend_sorted_call(lengths, q, kv, kvx, tokens, cot, hidden, rows):
@@ -1085,8 +1086,8 @@
             half = d_low[:, h * (D // 2) : (h + 1) * (D // 2)]
             dlow_all[at_rows, part_of(halves[h], D // 2)] = half
         up_bias = wide_row(bu_ref)
-        for f in range(0, FF, CHUNK):
-            cols = slice(f, f + CHUNK)
+        for f in range(0, FF, STRIP):
+            cols = slice(f, f + STRIP)
             up = nn(hidden, wu_ref[:, cols]) + up_bias[:, cols]
             square = up * up
             bend = jnp.tanh(up * (GELU_C + (GELU_C * 0.044715) * square))
@@ -1119,12 +1120,12 @@
         d_low = (gate2 * dy).astype(BF16)
         lowered, d_hidden = None, None
         sums = []
-        for f in range(0, FF, CHUNK):
-            cols = slice(f, f + CHUNK)
+        for f in range(0, FF, STRIP):
+            cols = slice(f, f + STRIP)
             d_act = nt(d_low, wd_ref[cols, :])
             d_up = (d_act * slope_all[at_rows, cols].astype(F32)).astype(BF16)
             place = halves[f // (FF // 2)] * (FF // 2) + f % (FF // 2)
-            dup_ref[:, pl.ds(pl.multiple_of(place, CHUNK), CHUNK)] = d_up
+            dup_ref[:, pl.ds(pl.multiple_of(place, STRIP), STRIP)] = d_up
             sums.append(col_sum(d_up.astype(F32)))
             low = nn(act_all[at_rows, cols], wd_ref[cols, :])
             dh = nt(d_up, wu_ref[:, cols])
@@ -1144,6 +1145,8 @@
             half = d_attention[:, h * (D // 2) : (h + 1) * (D // 2)]
             dattn_ref[:, part_of(halves[h], D // 2)] = half
         datt_ref[...] = nt(d_attention, wo_ref[...]).astype(BF16)
+        total = jnp.concatenate(sums, axis=1)
+        sums = [total[:, f : f + D] for f in range(0, FF, D)]
         four = jnp.concatenate(
             [
                 col_sum(d_mid * attention), col_sum(d_hidden), hx * gain,
@@ -1792,9 +1795,6 @@
     out_ref[...] = out_in[...]
     up_ref[...] = up_in[...]
     down_ref[...] = down_in[...]
-    for come, go in zip(reads, moves):
-        come.wait()
-        go.start()
     packed = early_ref[...].astype(F32)
     early = [
         jnp.concatenate([packed[:, 6 * r + c] for c in range(6)], axis=1) for r in range(14)
@@ -1829,6 +1829,9 @@
     own = jnp.concatenate(own, axis=1)
     d_silu = nt(jnp.concatenate(thirds(own), axis=0), weight_ref[...])
     d_silu = d_silu[:8] + d_silu[8:16] + d_silu[16:24]
+    for come, go in zip(reads, moves):
+        come.wait()
+        go.start()
     v = table_ref[s]
     sig = 1.0 / (1.0 + jnp.exp(-v))
     gcond_ref[...] = (d_silu * (sig * (1.0 + v * (1.0 - sig))))[:SLOTS]

time: 190 us -> 189 us (level)
  no operation moved by 1% of the time
where the time goes in v7:
time: 189 us
  Pallas kernels  188 us (99%)
    pallas_call x1, Pallas kernels, middle_call(): pl.pallas_call(middle_kernel, name='middle', grid=(FIRST + PAIRS + 1,), o...  66.3 us
    pallas_call x1, Pallas kernels, both_call(): pl.pallas_call(both_kernel, name='feed', grid=(3 * tiles,), out_shape=(ja...  51.5 us
    pallas_call x1, Pallas kernels, end_call(): pl.pallas_call(end_kernel, name='end', grid=(TILES,), out_shape=(jax.Shap...  24.6 us
    pallas_call x1, Pallas kernels, share_call(): pl.pallas_call(share_kernel, name='project', grid=(steps,), out_shape=(ja...  21.5 us
    pallas_call x1, Pallas kernels, attend_sorted_call(): pl.pallas_call(attend_sorted_kernel, name='attend', out_shape=(jax.ShapeD...  17 us
    pallas_call x1, Pallas kernels, condition_call(): pl.pallas_call(condition_kernel, name='condition', out_shape=tuple((jax.S...  7.06 us

profile of v7, /device:TPU:0, one launch (start us, length us, event | category | flops | bytes accessed | tf_op | source)
XLA Modules:
  0.0 188.9 jit_solution(16566075089021135621)
XLA Ops:
  0.6 21.5 %project.1 = (bf16[1024,768]{1,0:T(8,128)(2,1)}, bf16[1024,768]{1,0:T(8,128)(2,1)}, bf16[1024,1536]{1,0:T(8,128)(2,1)}, f32[8,4608]{1,0:T(8,128)}, f32[16,8,128]...) custom-call(bf16[2,128]{1,0:T(2,128)(2,1)} %cond_ref.1, s32[2]{0:T(128)} %assign_ref.1, ...), custom_call_target="tpu_custom_call" | custom-call | flops 3623878656 | bytes 14000000 | tf_op jit(solution)/shard_map/project/pallas_call | solution.py:772
  22.2 17.0 %attend.1 = (bf16[1024,768]{1,0:T(8,128)(2,1)}, f32[6,4,512]{2,1,0:T(4,128)}, bf16[1024,768]{1,0:T(8,128)(2,1)}, bf16[512,768]{1,0:T(8,128)(2,1)}, bf16[512,768]...) custom-call(s32[2]{0:T(128)} %lengths.7, ...), custom_call_target="tpu_custom_call" | custom-call | flops 7247757312 | bytes 16000000 | tf_op jit(solution)/shard_map/attend/pallas_call | solution.py:863
  39.2 51.5 %feed.1 = (bf16[1024,768]{1,0:T(8,128)(2,1)}, f32[1024,768]{1,0:T(8,128)}, bf16[1024,768]{1,0:T(8,128)(2,1)}, bf16[1024,768]{1,0:T(8,128)(2,1)}, bf16[1024,3072]...) custom-call(bf16[1024,768]{1,0:T(8,128)(2,1)} %get-tuple-element.73., ...), custom_call_target="tpu_custom_call" | custom-call | flops 26575110144 | bytes 40000000 | tf_op jit(solution)/shard_map/feed/pallas_call | solution.py:1193
  90.7 66.3 %middle.1 = (bf16[1024,768]{1,0:T(8,128)(2,1)}, bf16[1024,768]{1,0:T(8,128)(2,1)}, bf16[1024,768]{1,0:T(8,128)(2,1)}, f32[192,384]{1,0:T(8,128)}, f32[48,384]{1,...) custom-call(bf16[1024,768]{1,0:T(8,128)(2,1)} %get-tuple-element.72., ...), custom_call_target="tpu_custom_call" | custom-call | flops 27783069696 | bytes 50000000 | tf_op jit(solution)/shard_map/middle/pallas_call | solution.py:1543
  157.1 24.6 %end.1 = (f32[1024,768]{1,0:T(8,128)}, f32[48,1152]{1,0:T(8,128)}, bf16[16,32,128]{2,1,0:T(8,128)(2,1)}) custom-call(bf16[1024,768]{1,0:T(8,128)(2,1)} %get-tuple-element.73.tok_ref, f32[1024,768]{1,0:T(8,128)} %get-tuple-element.93.dmid_ref, bf16[1024,768]{1,0:T(8,128)(2,1)} %get-tuple-element.94.dq_ref, bf16[1024,768]{1,0:T(8,128)(2,1)} %get-tuple-element.95.dk_ref, ...), custom_call_target="tpu_custom_call" | custom-call | flops 3623878656 | bytes 22000000 | tf_op jit(solution)/shard_map/end/pallas_call | solution.py:1721
  181.6 7.1 %condition.1 = (f32[8,2304]{1,0:T(8,128)}, f32[4608]{0:T(1024)}, f32[2,128]{1,0:T(2,128)}, f32[768]{0:T(1024)}, f32[768]{0:T(1024)}, /*index=5*/f32[768]{0:T(102...) custom-call(s32[2]{0:T(128)} %lengths.7, ...), custom_call_target="tpu_custom_call" | custom-call | flops 10000000 | bytes 12000000 | tf_op jit(solution)/shard_map/condition/pallas_call | solution.py:1863
